TPU v7x, 256 devices: a whole 4x4x8 slice. The times are simulated.
256 devices in a mesh: role: 2 (over x_hi), dp: 8 (over x_lo, y), seq: 16 (over z, core).
Axes of the slice: x: 4 (x_hi: 2, x_lo: 2; x = x_hi * 2 + x_lo), y: 4, z: 8, core: 2. Of those that a mesh axis runs over, the one named last changes fastest.
Arguments:
- latents: bfloat16 [2, 8, 2048, 64], P('role', 'dp', 'seq'), may hold values from -6 to 6
- next_latents: bfloat16 [8, 2048, 64], P('dp', 'seq'), may hold values from -6 to 6
- noise: bfloat16 [8, 2048, 64], P('dp', 'seq'), may hold values from -6 to 6
- advantage: float32 [8], P('dp'), may hold values from -3 to 3
- old_logp: float32 [8], P('dp'), may hold values from -2.6 to -1.2
- timesteps: int32 [2, 8], P('role', 'dp'), may hold values from 0 to 9
- embed_weight: bfloat16 [64, 3072], replicated, may hold values from -0.75 to 0.75
- modulation: float32 [10, 2, 3072], replicated, may hold values from -24 to 24
- qkv_weight: bfloat16 [2, 3, 3072, 4096], P('role', None, 'dp', 'seq'), may hold values from -7.2 to 7.2
- head_weight: bfloat16 [2, 4096, 64], P('role', 'seq'), may hold values from -3 to 3
Outputs:
- fresh_latents: bfloat16 [2, 8, 2048, 64], P('role', 'dp', 'seq')
- head_next: bfloat16 [2, 4096, 64], P('role', 'seq')
All inputs are finite; a program needn't handle non-finite values.
Results may differ from a plain program's by a relative error of at most 0.012.
The roundings to bfloat16 on the way count: a program that leaves them out, or rounds other values in their place, can miss the bound.
Values may be sent and summed in bfloat16 or wider, within the bound.
No kernel may reach another device: no remote copies, remote signals or barrier semaphores. Data moves between devices by JAX's collectives and lax.ppermute only.
A program may use at most 128 MiB of HBM per device.

v0:
```python
import jax
import jax.numpy as jnp
from jax import lax
from jax.sharding import PartitionSpec as P

HD = 128


noise_level = 0.8
step_size = 0.5
norm_eps = 1e-06
update_eps = 1e-06


def from_behind(value, axis, by):
    devices = lax.axis_size(axis)
    pairs = [(i, i + by) for i in range(devices) if 0 <= i + by < devices]
    return lax.ppermute(value, axis, pairs)


def normalize(embedded, shift_scale):
    values = embedded.astype(jnp.float32)
    center = jnp.mean(values, axis=-1, keepdims=True)
    spread = jnp.mean((values - center) * (values - center), axis=-1, keepdims=True)
    normed = (values - center) * lax.rsqrt(spread + norm_eps)
    return (normed * (1.0 + shift_scale[1]) + shift_scale[0]).astype(jnp.bfloat16)


def on_device(
    latents,
    next_latents,
    noise,
    advantage,
    old_logp,
    timesteps,
    embed_weight,
    modulation,
    qkv_weight,
    head_weight,
):
    role_id = lax.axis_index("role")
    own_latent = latents[0, 0]
    step_index = timesteps[0, 0]
    steps_count = modulation.shape[0]
    width = modulation.shape[2]
    step_onehot = (jnp.arange(steps_count) == step_index).astype(jnp.float32)
    shift_scale = jnp.dot(
        step_onehot, modulation.reshape(steps_count, 2 * width), precision=lax.Precision.HIGHEST
    ).reshape(2, width)
    projections = lax.all_gather(qkv_weight[0], "dp", axis=1, tiled=True)
    columns = projections.shape[2]
    factor = 1.0 / width**0.5
    own_embedded = jnp.dot(own_latent, embed_weight, preferred_element_type=jnp.float32).astype(
        jnp.bfloat16
    )
    modulated = normalize(lax.all_gather(own_embedded, "seq", axis=0, tiled=True), shift_scale)
    parts = [
        (
            jnp.dot(modulated, projections[index], preferred_element_type=jnp.float32) * factor
        ).astype(jnp.bfloat16)
        for index in range(3)
    ]
    projected = jnp.concatenate(parts, axis=1)
    length = projected.shape[0]
    heads_here = columns // HD
    queries = projected[:, :columns].reshape(length, heads_here, HD)
    keys_all = projected[:, columns : 2 * columns].reshape(length, heads_here, HD)
    values_all = projected[:, 2 * columns :].reshape(length, heads_here, HD)
    block_rows = min(512, length)
    query_blocks = queries.reshape(length // block_rows, block_rows, heads_here, HD)

    def attend(query_part):
        scores = jnp.einsum(
            "qhd,khd->hqk", query_part, keys_all, preferred_element_type=jnp.float32
        ) * (1.0 / HD**0.5)
        row_max = jnp.max(scores, axis=-1, keepdims=True)
        exp_scores = jnp.exp(scores - row_max)
        soft_weights = (exp_scores / jnp.sum(exp_scores, axis=-1, keepdims=True)).astype(
            jnp.bfloat16
        )
        outputs = jnp.einsum(
            "hqk,khd->qhd", soft_weights, values_all, preferred_element_type=jnp.float32
        ).astype(jnp.bfloat16)
        return outputs.reshape(block_rows, columns)

    attended = lax.map(attend, query_blocks).reshape(length, columns)
    tok_rows = own_latent.shape[0]
    channels = own_latent.shape[1]
    head_copy = head_weight[0]
    rows = attended
    velocity = lax.psum_scatter(
        jnp.dot(rows, head_copy, preferred_element_type=jnp.float32),
        "seq",
        scatter_dimension=0,
        tiled=True,
    )
    mean_next = own_latent.astype(jnp.float32) - velocity * (1.0 / steps_count)
    fresh_own = (mean_next + noise_level * noise[0].astype(jnp.float32)).astype(jnp.bfloat16)
    residual = next_latents[0].astype(jnp.float32) - mean_next
    squared = lax.psum(jnp.sum(residual * residual), "seq")
    logp = -squared / (2.0 * noise_level * noise_level * tok_rows * lax.axis_size("seq") * channels)
    ratio = jnp.exp(logp - old_logp[0])
    weighted = (advantage[0] * ratio * residual).astype(jnp.bfloat16)
    rows = attended
    partial_grad = lax.dot_general(
        rows,
        lax.all_gather(weighted, "seq", axis=0, tiled=True),
        (((0,), (0,)), ((), ())),
        preferred_element_type=jnp.float32,
    )
    gradient = lax.psum(partial_grad, "dp")
    square_sum = lax.psum(jnp.sum(gradient * gradient), "seq")
    mean_square = square_sum / (columns * lax.axis_size("seq") * channels)
    updated = (
        head_copy.astype(jnp.float32) - step_size * gradient * lax.rsqrt(mean_square + update_eps)
    ).astype(jnp.bfloat16)
    fresh_received = from_behind(fresh_own, "role", 1)
    weight_received = from_behind(updated, "role", -1)
    fresh_out = jnp.where(role_id == 0, fresh_own, fresh_received)
    weight_out = jnp.where(role_id == 1, updated, weight_received)
    return (fresh_out[None, None], weight_out[None])


def solution(mesh):
    in_specs = (
        P("role", "dp", "seq", None),
        P("dp", "seq", None),
        P("dp", "seq", None),
        P("dp"),
        P("dp"),
        P("role", "dp"),
        P(),
        P(),
        P("role", None, "dp", "seq"),
        P("role", "seq", None),
    )
    out_specs = (P("role", "dp", "seq", None), P("role", "seq", None))
    return jax.shard_map(
        on_device, mesh=mesh, in_specs=in_specs, out_specs=out_specs, check_vma=False
    )
```

profile of v0, /device:TPU:1, one launch (start us, length us, event | category | flops | bytes accessed | tf_op | source)
XLA Modules:
  0.0 455.4 jit_solution(15562075552844462150)
XLA Ops:
  7.2 0.0 copy-start
  7.2 0.0 all-gather.4.cloned.1.call-start
  7.2 0.9 copy-done
  8.2 2.0 convolution_convert_fusion
  10.2 0.0 all-gather.4.cloned.1.call-update
  10.2 0.0 all-gather.6.cloned.1.call-start
  10.2 0.7 all-gather.6.cloned.1.call-update
  10.9 0.0 reduce-scatter.2.cloned.1.call-start
  11.0 1.1 pad
  12.1 0.1 copy.30
  12.8 0.2 fusion.25
  13.1 77.1 %all-gather.4.cloned.1.call-done = bf16[2048,3072]{1,0:T(8,128)(2,1)} async-done(((bf16[128,3072]{1,0:T(8,128)(2,1)}), bf16[2048,3072]{1,0:T(8,128)(2,1)}) %all-gather.4.cloned.1.call-update) | async-done | bytes 12582928 | tf_op jit(solution)/shard_map/all_gather | solution.py:56
  90.2 6.3 %convert_reduce_fusion = f32[2048]{0:T(1024)S(1)} fusion(bf16[2048,3072]{1,0:T(8,128)(2,1)} %all-gather.4.cloned.1.call-done), kind=kLoop, calls=%fused_computation.15 | loop fusion | flops 12580864 | bytes 12591104 | tf_op jit(solution)/shard_map/reduce_sum | solution.py:23
  96.5 8.0 %fusion.13 = f32[2048]{0:T(1024)S(1)} fusion(bf16[2048,3072]{1,0:T(8,128)(2,1)} %all-gather.4.cloned.1.call-done, f32[2048]{0:T(1024)S(1)} %broadcast_multiply_fusion), kind=kLoop, calls=%fused_computation.18 | loop fusion | flops 25163776 | bytes 12599296 | tf_op jit(solution)/shard_map/reduce_sum | solution.py:24
  104.5 13.7 %fusion.16 = bf16[2048,3072]{1,0:T(8,128)(2,1)} fusion(bf16[2048,3072]{1,0:T(8,128)(2,1)} %all-gather.4.cloned.1.call-done, f32[3072]{0:T(1024)S(1)} %get-tuple-element.55, f32[3072]{0:T(1024)S(1)} %get-tuple-element.54, f32[2048]{0:T(1024)S(1)} %add_rsqrt_fusion, f32[2048]{0:T(1024)S(1)} %broadcast_multiply_fusion), kind=kLoop, calls=%fused_computation.21 | loop fusion | flops 37748736 | bytes 25206784 | tf_op jit(solution)/shard_map/convert_element_type | solution.py:26
  118.2 32.1 %all-gather.6.cloned.1.call-done = bf16[1,3,3072,256]{3,2,1,0:T(8,128)(2,1)} async-done(((bf16[1,3,384,256]{3,2,1,0:T(8,128)(2,1)}), bf16[1,3,3072,256]{3,2,1,0:T(8,128)(2,1)}) %all-gather.6.cloned.1.call-update) | async-done | bytes 4718608 | tf_op jit(solution)/shard_map/all_gather | solution.py:50
  150.2 8.5 %fusion.17 = bf16[2048,256]{1,0:T(8,128)(2,1)S(1)} fusion(bf16[2048,3072]{1,0:T(8,128)(2,1)} %fusion.16, bf16[1,3,3072,256]{3,2,1,0:T(8,128)(2,1)} %all-gather.6.cloned.1.call-done), kind=kOutput, calls=%fused_computation.24 | convolution fusion | flops 3222274048 | bytes 15204352 | tf_op jit(solution)/shard_map/dot_general | solution.py:59
  158.7 1.4 copy.25
  160.2 8.5 %fusion.20 = bf16[256,2,8,128]{3,2,1,0:T(8,128)(2,1)S(1)} fusion(bf16[2048,3072]{1,0:T(8,128)(2,1)} %fusion.16, bf16[1,3,3072,256]{3,2,1,0:T(8,128)(2,1)} %all-gather.6.cloned.1.call-done), kind=kOutput, calls=%fused_computation.32 | convolution fusion | flops 3222274048 | bytes 15204352 | tf_op jit(solution)/shard_map/dot_general | solution.py:59
  168.7 1.1 copy.43
  169.8 8.5 %fusion.19 = bf16[2048,256]{1,0:T(8,128)(2,1)S(1)} fusion(bf16[2048,3072]{1,0:T(8,128)(2,1)} %fusion.16, bf16[1,3,3072,256]{3,2,1,0:T(8,128)(2,1)} %all-gather.6.cloned.1.call-done), kind=kOutput, calls=%fused_computation.28 | convolution fusion | flops 3222274048 | bytes 15204352 | tf_op jit(solution)/shard_map/dot_general | solution.py:59
  178.4 0.3 reshape_reshape.3
  178.7 0.0 copy-start.2
  178.7 0.0 copy-start.1
  178.7 0.0 copy-start.3
  178.7 0.0 copy-start.4
  178.7 51.0 %while.10 = (s32[]{:T(128)}, bf16[4,512,256]{2,1,0:T(8,128)(2,1)S(1)}, bf16[4,512,2,128]{3,2,1,0:T(2,128)(2,1)S(1)}, bf16[2048,2,128]{2,0,1:T(8,128)(2,1)}, bf16[2048,2,128]{0,2,1:T(8,128)(2,1)}, /*index=5*/s32[]{:T(128)}) while((s32[]{:T(128)}, bf16[4,512,256]{2,1,0:T(8,128)(2,1)S(1)}, bf16[4,512,2,128]{3,2,1,0:T(2,128)(2,1)S(1)}, ...), condition=%wide.region_5.6_spmd, body=%wide.region_2.5_spmd.sunk | while | flops 1084360704 | bytes 20979788 | solution.py:86
  178.9 0.2 constant_dynamic-slice_fusion.2
  179.1 7.1 %fusion.49 = (f32[2,512]{1,0:T(2,128)S(1)}, f32[2,512,2048]{2,1,0:T(8,128)}) fusion(bf16[2048,2,128]{2,0,1:T(8,128)(2,1)} %get-tuple-element.106, bf16[1,512,2,128]{3,2,1,0:T(2,128)(2,1)S(1)} %constant_dynamic-slice_fusion.2), kind=kOutput, calls=%fused_computation.55.clone.1 | convolution fusion | flops 543164416 | bytes 9703424 | tf_op jit(solution)/shard_map/while/body/eval_jaxpr/sub | solution.py:77
  186.2 5.2 %fusion.50 = bf16[2,512,128]{1,2,0:T(8,128)(2,1)S(1)} fusion(bf16[2048,2,128]{0,2,1:T(8,128)(2,1)} %get-tuple-element.107, f32[2,512,2048]{2,1,0:T(8,128)} %get-tuple-element.89, f32[2,512]{1,0:T(2,128)S(1)} %get-tuple-element.90), kind=kOutput, calls=%fused_computation.7.clone.1 | convolution fusion | flops 541196288 | bytes 9703424 | tf_op jit(solution)/shard_map/while/body/eval_jaxpr/hqk,khd->qhd/dot_general | solution.py:81
  191.5 0.1 copy.47
  191.6 0.2 constant_dynamic-slice_fusion.2
  191.8 7.1 %fusion.49 = (f32[2,512]{1,0:T(2,128)S(1)}, f32[2,512,2048]{2,1,0:T(8,128)}) fusion(bf16[2048,2,128]{2,0,1:T(8,128)(2,1)} %get-tuple-element.106, bf16[1,512,2,128]{3,2,1,0:T(2,128)(2,1)S(1)} %constant_dynamic-slice_fusion.2), kind=kOutput, calls=%fused_computation.55.clone.1 | convolution fusion | flops 543164416 | bytes 9703424 | tf_op jit(solution)/shard_map/while/body/eval_jaxpr/sub | solution.py:77
  198.9 5.2 %fusion.50 = bf16[2,512,128]{1,2,0:T(8,128)(2,1)S(1)} fusion(bf16[2048,2,128]{0,2,1:T(8,128)(2,1)} %get-tuple-element.107, f32[2,512,2048]{2,1,0:T(8,128)} %get-tuple-element.89, f32[2,512]{1,0:T(2,128)S(1)} %get-tuple-element.90), kind=kOutput, calls=%fused_computation.7.clone.1 | convolution fusion | flops 541196288 | bytes 9703424 | tf_op jit(solution)/shard_map/while/body/eval_jaxpr/hqk,khd->qhd/dot_general | solution.py:81
  204.2 0.1 copy.47
  204.3 0.2 constant_dynamic-slice_fusion.2
  204.5 7.1 %fusion.49 = (f32[2,512]{1,0:T(2,128)S(1)}, f32[2,512,2048]{2,1,0:T(8,128)}) fusion(bf16[2048,2,128]{2,0,1:T(8,128)(2,1)} %get-tuple-element.106, bf16[1,512,2,128]{3,2,1,0:T(2,128)(2,1)S(1)} %constant_dynamic-slice_fusion.2), kind=kOutput, calls=%fused_computation.55.clone.1 | convolution fusion | flops 543164416 | bytes 9703424 | tf_op jit(solution)/shard_map/while/body/eval_jaxpr/sub | solution.py:77
  211.6 5.2 %fusion.50 = bf16[2,512,128]{1,2,0:T(8,128)(2,1)S(1)} fusion(bf16[2048,2,128]{0,2,1:T(8,128)(2,1)} %get-tuple-element.107, f32[2,512,2048]{2,1,0:T(8,128)} %get-tuple-element.89, f32[2,512]{1,0:T(2,128)S(1)} %get-tuple-element.90), kind=kOutput, calls=%fused_computation.7.clone.1 | convolution fusion | flops 541196288 | bytes 9703424 | tf_op jit(solution)/shard_map/while/body/eval_jaxpr/hqk,khd->qhd/dot_general | solution.py:81
  216.9 0.1 copy.47
  217.0 0.2 constant_dynamic-slice_fusion.2
  217.2 7.1 %fusion.49 = (f32[2,512]{1,0:T(2,128)S(1)}, f32[2,512,2048]{2,1,0:T(8,128)}) fusion(bf16[2048,2,128]{2,0,1:T(8,128)(2,1)} %get-tuple-element.106, bf16[1,512,2,128]{3,2,1,0:T(2,128)(2,1)S(1)} %constant_dynamic-slice_fusion.2), kind=kOutput, calls=%fused_computation.55.clone.1 | convolution fusion | flops 543164416 | bytes 9703424 | tf_op jit(solution)/shard_map/while/body/eval_jaxpr/sub | solution.py:77
  224.3 5.2 %fusion.50 = bf16[2,512,128]{1,2,0:T(8,128)(2,1)S(1)} fusion(bf16[2048,2,128]{0,2,1:T(8,128)(2,1)} %get-tuple-element.107, f32[2,512,2048]{2,1,0:T(8,128)} %get-tuple-element.89, f32[2,512]{1,0:T(2,128)S(1)} %get-tuple-element.90), kind=kOutput, calls=%fused_computation.7.clone.1 | convolution fusion | flops 541196288 | bytes 9703424 | tf_op jit(solution)/shard_map/while/body/eval_jaxpr/hqk,khd->qhd/dot_general | solution.py:81
  229.6 0.1 copy.47
  229.7 0.0 copy-done.2
  229.7 1.2 fusion.22
  231.0 0.0 reduce-scatter.2.cloned.1.call-update
  231.0 0.0 all-reduce.2.cloned.1.call-start
  231.7 51.8 %reduce-scatter.2.cloned.1.call-done = f32[128,64]{0,1:T(8,128)} async-done(((f32[2048,64]{0,1:T(8,128)}), f32[128,64]{0,1:T(8,128)}) %reduce-scatter.2.cloned.1.call-update) | async-done | bytes 32784 | tf_op jit(solution)/shard_map/reduce_scatter | solution.py:91
  283.5 1.4 multiply_reduce_fusion.2
  285.5 27.0 %psum.21 = f32[]{:T(128)} all-reduce(f32[]{:T(128)} %multiply_reduce_fusion.2), channel_id=1, replica_groups=mesh['role'=2,'dp'=8,'seq'=16] {'seq'}, use_global_device_ids=true, to_apply=%region_8.9 | all-reduce | flops 1 | bytes 8 | tf_op jit(solution)/shard_map/psum | solution.py:100
  313.2 0.8 multiply_convert_fusion
  314.0 16.3 %all_gather.11 = bf16[2048,64]{0,1:T(8,128)(2,1)S(1)} all-gather(bf16[128,64]{0,1:T(8,128)(2,1)S(1)} %get-tuple-element.52), channel_id=1, replica_groups=mesh['role'=2,'dp'=8,'seq'=16] {'seq'}, dimensions={0}, use_global_device_ids=true | all-gather | bytes 278528 | tf_op jit(solution)/shard_map/all_gather | solution.py:107
  330.3 0.9 fusion.31
  331.2 0.0 all-reduce.2.cloned.1.call-update
  331.3 73.7 %all-reduce.2.cloned.1.call-done = f32[256,64]{0,1:T(8,128)} async-done(((f32[256,64]{0,1:T(8,128)}), f32[256,64]{0,1:T(8,128)}) %all-reduce.2.cloned.1.call-update) | async-done | bytes 65552 | tf_op jit(solution)/shard_map/psum | solution.py:111
  404.9 1.5 multiply_reduce_fusion.1
  406.4 4.3 collective-permute-start
  410.7 29.8 %psum.23 = f32[]{:T(128)} all-reduce(f32[]{:T(128)} %multiply_reduce_fusion.1), channel_id=1, replica_groups=mesh['role'=2,'dp'=8,'seq'=16] {'seq'}, use_global_device_ids=true, to_apply=%region_11.12 | all-reduce | flops 1 | bytes 8 | tf_op jit(solution)/shard_map/psum | solution.py:112
  441.2 0.9 subtract_convert_fusion
  442.1 1.3 collective-permute-start.1
  443.4 0.0 collective-permute-done
  443.4 0.6 select_bitcast_fusion.1
  444.0 4.2 collective-permute-done.1
  448.2 0.6 select_bitcast_fusion
  (11 shorter events, 0.1 us)
Async XLA Ops:
  7.2 1.0 copy-start
  7.2 83.0 %all-gather.4.cloned.1.call-start = ((), (), s32[]{:S(2)}) async-start(), calls=%async_computation.1 | async-start | bytes 13369344 | tf_op jit(solution)/shard_map/all_gather | solution.py:56
  10.2 140.0 %all-gather.6.cloned.1.call-start = ((), (), s32[]{:S(2)}) async-start(), calls=%async_computation.4 | async-start | bytes 5308416 | tf_op jit(solution)/shard_map/all_gather | solution.py:50
  10.9 272.5 %reduce-scatter.2.cloned.1.call-start = ((), (), s32[]{:S(2)}) async-start(), calls=%async_computation.2 | async-start | bytes 557056 | tf_op jit(solution)/shard_map/reduce_scatter | solution.py:91
  178.7 51.1 %copy-start.2 = (bf16[1,256,64]{1,2,0:T(8,128)(2,1)S(1)}, bf16[1,256,64]{1,2,0:T(8,128)(2,1)}, u32[]{:S(2)}) copy-start(bf16[1,256,64]{1,2,0:T(8,128)(2,1)} %param.21) | copy-start | bytes 98308
  178.7 104.8 %copy-start.1 = (bf16[1,1,128,64]{2,3,1,0:T(8,128)(2,1)S(1)}, bf16[1,1,128,64]{2,3,1,0:T(8,128)(2,1)}, u32[]{:S(2)}) copy-start(bf16[1,1,128,64]{2,3,1,0:T(8,128)(2,1)} %param.12) | copy-start | bytes 49156
  178.7 104.8 %copy-start.3 = (bf16[1,128,64]{1,2,0:T(8,128)(2,1)S(1)}, bf16[1,128,64]{1,2,0:T(8,128)(2,1)}, u32[]{:S(2)}) copy-start(bf16[1,128,64]{1,2,0:T(8,128)(2,1)} %param.13) | copy-start | bytes 49156
  178.7 134.5 %copy-start.4 = (bf16[1,128,64]{1,2,0:T(8,128)(2,1)S(1)}, bf16[1,128,64]{1,2,0:T(8,128)(2,1)}, u32[]{:S(2)}) copy-start(bf16[1,128,64]{1,2,0:T(8,128)(2,1)} %param.14) | copy-start | bytes 49156
  231.0 173.9 %all-reduce.2.cloned.1.call-start = ((), (), s32[]{:S(2)}) async-start(), calls=%async_computation.3 | async-start | bytes 131072 | tf_op jit(solution)/shard_map/psum | solution.py:111
  406.4 37.0 %collective-permute-start = (bf16[128,64]{0,1:T(8,128)(2,1)S(1)}, bf16[128,64]{0,1:T(8,128)(2,1)S(1)}, u32[]{:S(2)}, u32[]{:S(2)}) collective-permute-start(bf16[128,64]{0,1:T(8,128)(2,1)S(1)} %get-tuple-element.53), channel_id=1, source_target_pairs={{0,128},{1,129},{2,130},{3,131},{4,132},{5,133},{6,134},{7,135},{8... | collective-permute-start | bytes 49160 | tf_op jit(solution)/shard_map/ppermute | solution.py:18
  442.1 6.2 %collective-permute-start.1 = (bf16[256,64]{0,1:T(8,128)(2,1)S(1)}, bf16[256,64]{0,1:T(8,128)(2,1)S(1)}, u32[]{:S(2)}, u32[]{:S(2)}) collective-permute-start(bf16[256,64]{0,1:T(8,128)(2,1)S(1)} %subtract_convert_fusion), channel_id=1, source_target_pairs={{128,0},{129,1},{130,2},{131,3},{132,4},{133,5},{134,6},{135,7},{1... | collective-permute-start | bytes 98312 | tf_op jit(solution)/shard_map/ppermute | solution.py:18
Sparse Core Ops, SparseCore 0:
  10.3 79.8 all-gather.3
  92.0 58.1 all-gather.5
  231.1 52.2 reduce-scatter.1
  331.4 73.5 all-reduce.1
where the time goes:
time: 456 us; the launch traced here: 455 us
  waiting for transfers between devices  240 us (53%)
  matrix products  79.2 us (17%)
  blocking collectives  73.1 us (16%)
  other arithmetic  33.6 us (7%)
  between operations  17.3 us (4%)
  local copies, waits for them, and re-layouts  6.37 us (1%)
  starting transfers between devices  5.75 us (1%)
    all_gather x1, waiting for transfers between devices, on_device(): lax.all_gather(own_embedded, 'seq', axis=0, tiled=True)  77.1 us
    psum x1, waiting for transfers between devices, on_device(): gradient = lax.psum(partial_grad, 'dp')  73.7 us
    reduce_scatter x1, waiting for transfers between devices, on_device(): lax.psum_scatter(jnp.dot(rows, head_copy, preferred_element_type=jnp.floa...  51.8 us
    all_gather x1, waiting for transfers between devices, on_device(): projections = lax.all_gather(qkv_weight[0], 'dp', axis=1, tiled=True)  32.1 us
    psum x1, blocking collectives, on_device(): square_sum = lax.psum(jnp.sum(gradient * gradient), 'seq')  29.8 us
    sub x4, matrix products, attend(): exp_scores = jnp.exp(scores - row_max)  28.4 us
    psum x1, blocking collectives, on_device(): squared = lax.psum(jnp.sum(residual * residual), 'seq')  27 us
    dot_general x3, matrix products, on_device(): jnp.dot(modulated, projections[index], preferred_element_type=jnp.float32)  25.6 us
  transfers between devices with their start and end apart: 6, of which 5 were waited for; matrix products, arithmetic and copies ran while one was open for 7% of the time, Pallas kernels for 0%

commit v1 on v0

v1 whole, which is shorter than its diff:
```python
import functools
import math

import jax
import jax.numpy as jnp
from jax import lax
from jax.experimental import pallas as pl
from jax.experimental.pallas import tpu as pltpu
from jax.sharding import PartitionSpec as P

HD = 128
LANES = 128

noise_level = 0.8
step_size = 0.5
norm_eps = 1e-06
update_eps = 1e-06

bf16 = jnp.bfloat16
f32 = jnp.float32

VMEM = pl.BlockSpec(memory_space=pltpu.VMEM)
SMEM = pl.BlockSpec(memory_space=pltpu.SMEM)
PARAMS = pltpu.CompilerParams(vmem_limit_bytes=48 * 1024 * 1024)


def dot(a, b, precision=None):
    return lax.dot_general(
        a, b, (((1,), (0,)), ((), ())), precision=precision, preferred_element_type=f32
    )


def dot_nt(a, b, precision=None):
    return lax.dot_general(
        a, b, (((1,), (1,)), ((), ())), precision=precision, preferred_element_type=f32
    )


HIGHEST = lax.Precision.HIGHEST


def partial_kernel(
    steps_ref, place_ref, latent_ref, embed_ref, modulation_ref, weight_ref, sums_ref, scaled_ref, left_ref
):
    latent = latent_ref[...].astype(f32).T
    embedded = dot(latent.astype(bf16), embed_ref[...]).astype(bf16).astype(f32)
    width = embedded.shape[1]
    center = jnp.sum(embedded, axis=1, keepdims=True) * (1.0 / width)
    spread = jnp.sum((embedded - center) * (embedded - center), axis=1, keepdims=True) * (1.0 / width)
    scaled_ref[...] = (latent * lax.rsqrt(spread + norm_eps)).T

    channels, rows = embed_ref.shape[0], weight_ref.shape[1]
    rollouts = sums_ref.shape[0]
    block = channels + 16
    start = pl.multiple_of(place_ref[0] * rows, LANES)
    mean = jnp.sum(embed_ref[...].astype(f32), axis=1, keepdims=True) * (1.0 / width)
    centered = embed_ref[:, pl.ds(start, rows)].astype(f32) - mean
    row = lax.broadcasted_iota(jnp.int32, (16, rows), 0)
    for i in range(rollouts):
        step = steps_ref[i]
        shift = modulation_ref[step, 0:1, pl.ds(start, rows)]
        scale = modulation_ref[step, 1:2, pl.ds(start, rows)]
        high = shift.astype(bf16).astype(f32)
        tail = jnp.where(row == 0, high, jnp.where(row == 1, shift - high, 0.0))
        left_ref[i * block : i * block + channels, :] = (centered * (1.0 + scale)).astype(bf16)
        left_ref[i * block + channels : (i + 1) * block, :] = tail.astype(bf16)
    slot = lax.broadcasted_iota(jnp.int32, (16, LANES), 0)
    tails = [jnp.zeros((16, LANES), f32) for _ in range(rollouts)]
    for j in range(3):
        product = dot(left_ref[...], weight_ref[j])
        for i in range(rollouts):
            for h in range(2):
                c = 2 * j + h
                part = product[i * block : (i + 1) * block, h * HD : (h + 1) * HD]
                sums_ref[i, c * channels : (c + 1) * channels, :] = part[:channels].astype(bf16)
                offset = part[channels : channels + 1] + part[channels + 1 : channels + 2]
                high = offset.astype(bf16).astype(f32)
                tails[i] = jnp.where(slot == c, high, jnp.where(slot == c + 8, offset - high, tails[i]))
    for i in range(rollouts):
        sums_ref[i, 6 * channels : 6 * channels + 16, :] = tails[i].astype(bf16)


def absorb_kernel(sums_ref, head_ref, scaled_ref, pack_ref, values_ref, offsets_ref, *, factor, logit):
    channels = head_ref.shape[0]
    total = sums_ref[0].astype(f32)
    for i in range(1, sums_ref.shape[0]):
        total += sums_ref[i].astype(f32)
    total = total * factor
    blocks = [total[c * channels : (c + 1) * channels] for c in range(6)]
    offsets = total[6 * channels : 6 * channels + 8] + total[6 * channels + 8 : 6 * channels + 16]
    queries, keys, values = blocks[0:2], blocks[2:4], blocks[4:6]
    none = jnp.zeros((channels, LANES), f32)

    def beside(parts):
        return jnp.concatenate([parts[0], none], axis=0), jnp.concatenate([none, parts[1]], axis=0)

    heads = [head_ref[:, h * HD : (h + 1) * HD].astype(f32) for h in range(2)]
    query_pads, key_pads, value_pads = beside(queries), beside(keys), beside(values)
    bilinear = sum(dot_nt(keys[h], query_pads[h], HIGHEST) for h in range(2)) * logit
    outward = sum(dot_nt(heads[h], value_pads[h], HIGHEST) for h in range(2))
    pack_ref[0:channels, :] = scaled_ref[...].astype(bf16)
    pack_ref[channels : 2 * channels, :] = bilinear.astype(bf16)
    pack_ref[2 * channels : 3 * channels, :] = outward.astype(bf16)

    slot = lax.broadcasted_iota(jnp.int32, (8, LANES), 0)
    lane = lax.broadcasted_iota(jnp.int32, (8, LANES), 1)

    def pick(array, c):
        return jnp.sum(jnp.where(slot == c, array, 0.0), axis=0, keepdims=True)

    by_keys = [dot_nt(offsets, key_pads[h], HIGHEST) * logit for h in range(2)]
    by_queries = [dot_nt(offsets, query_pads[h], HIGHEST) * logit for h in range(2)]
    by_heads = [dot_nt(offsets, jnp.concatenate([heads[h], none], axis=0), HIGHEST) for h in range(2)]
    query_constant = pick(by_keys[0], 0) + pick(by_keys[1], 1)
    key_constant = pick(by_queries[0], 2) + pick(by_queries[1], 3)
    both = [
        jnp.sum(pick(offsets, h) * pick(offsets, 2 + h), axis=1, keepdims=True) * logit for h in range(2)
    ]
    outward_constant = pick(by_heads[0], 4) + pick(by_heads[1], 5)
    tail = jnp.where(slot == 0, query_constant, 0.0)
    tail = jnp.where(slot == 1, key_constant, tail)
    tail = jnp.where(slot == 2, jnp.where(lane < channels, both[0], both[1]), tail)
    tail = jnp.where(slot == 3, outward_constant, tail)
    pack_ref[3 * channels : 3 * channels + 16, :] = jnp.concatenate([tail, jnp.zeros_like(tail)], axis=0).astype(bf16)
    values_ref[0:channels, :] = values[0]
    values_ref[channels : 2 * channels, :] = values[1]
    offsets_ref[...] = offsets


def attend_kernel(
    pack_ref,
    scaled_ref,
    latent_ref,
    next_ref,
    noise_ref,
    fresh_ref,
    pieces_ref,
    keys_ref,
    values_ref,
    attended_ref,
    own_ref,
    velocity_ref,
    *,
    steps_count,
):
    blocks = pack_ref.shape[0]
    channels, tokens = latent_ref.shape
    length = blocks * tokens
    unit = (lax.broadcasted_iota(jnp.int32, (64, tokens), 0) == 0).astype(f32)
    constants = jnp.zeros((16, LANES), f32)
    for s in range(blocks):
        block = pack_ref[s, 0:channels, :]
        here = slice(s * tokens, (s + 1) * tokens)
        values_ref[0:channels, here] = block
        keys_ref[here, :] = jnp.concatenate([block.astype(f32), unit], axis=0).T.astype(bf16)
        constants += pack_ref[s, 3 * channels : 3 * channels + 16, :].astype(f32)
    values_ref[channels : channels + 16, :] = (
        lax.broadcasted_iota(jnp.int32, (16, length), 0) == 0
    ).astype(bf16)
    own = scaled_ref[...]
    none = jnp.zeros_like(own)
    own_ref[...] = jnp.concatenate(
        [jnp.concatenate([own, none], axis=1), jnp.concatenate([none, own], axis=1)], axis=0
    ).astype(bf16)
    velocity_ref[...] = jnp.zeros_like(velocity_ref)
    first = lax.broadcasted_iota(jnp.int32, (16, 2 * tokens), 0) == 0
    side = lax.broadcasted_iota(jnp.int32, (1, 2 * tokens), 1) < tokens
    rest = jnp.zeros((LANES - channels - 16, 2 * tokens), f32)

    def scores_of(s):
        own_pair = own_ref[...]
        queries = dot(pack_ref[s, channels : 2 * channels, :], own_pair)
        tail = pack_ref[s, 3 * channels : 3 * channels + 16, :]
        level = dot(tail, own_pair)[1:2, :]
        tail = tail.astype(f32)
        level += jnp.where(side, tail[2:3, 0:1], tail[2:3, channels : channels + 1])
        columns = jnp.concatenate([tail, jnp.zeros((LANES - 16, LANES), f32)], axis=0).T
        queries += jnp.concatenate(
            [
                jnp.broadcast_to(columns[0:channels, 0:1], (channels, tokens)),
                jnp.broadcast_to(columns[channels : 2 * channels, 0:1], (channels, tokens)),
            ],
            axis=1,
        )
        queries = jnp.concatenate([queries, jnp.where(first, level, 0.0), rest], axis=0).astype(bf16)
        return dot(keys_ref[...], queries)

    def finish(s, scores):
        top = jnp.max(scores, axis=0, keepdims=True)
        probs = jnp.exp2(scores - top).astype(bf16)
        sums = dot(values_ref[...], probs)
        normed = sums[0:channels] * (1.0 / sums[channels : channels + 1])
        stacked = jnp.concatenate([normed[:, :tokens], normed[:, tokens:]], axis=0).astype(bf16)
        attended_ref[s] = stacked
        velocity_ref[...] += dot(pack_ref[s, 2 * channels : 3 * channels, :], stacked)

    def body(s, carry):
        finish(s, scores_of(s))
        return carry

    lax.fori_loop(0, blocks, body, 0)

    velocity = velocity_ref[...] + jnp.concatenate(
        [constants, jnp.zeros((LANES - 16, LANES), f32)], axis=0
    ).T[0:channels, 3:4]
    mean_next = latent_ref[...].astype(f32) - velocity * (1.0 / steps_count)
    fresh_ref[...] = (mean_next + noise_level * noise_ref[...].astype(f32)).astype(bf16)
    residual = next_ref[...].astype(f32) - mean_next
    squared = jnp.sum(jnp.sum(residual * residual, axis=1, keepdims=True), axis=0, keepdims=True)
    residual = residual.astype(bf16)
    wide = jnp.concatenate([residual, jnp.zeros((LANES - channels, tokens), bf16)], axis=0)
    column_sums = dot_nt(jnp.ones((16, tokens), bf16), wide)
    slot = lax.broadcasted_iota(jnp.int32, (16, LANES), 0)
    high = squared.astype(bf16).astype(f32)
    tail = jnp.where(slot == 0, column_sums, jnp.where(slot == 1, high, jnp.where(slot == 2, squared - high, 0.0)))
    tail = tail.astype(bf16)
    for s in range(blocks):
        pieces_ref[s, 0:channels, :] = dot_nt(residual, attended_ref[s]).astype(bf16)
        pieces_ref[s, channels : channels + 16, :] = tail


def gradient_kernel(pieces_ref, values_ref, offsets_ref, gain_ref, old_ref, out_ref, *, entries):
    total = pieces_ref[0].astype(f32)
    for s in range(1, pieces_ref.shape[0]):
        total += pieces_ref[s].astype(f32)
    channels = out_ref.shape[1]
    tail = total[channels : channels + 16]
    squared = tail[1:2, 0:1] + tail[2:3, 0:1]
    logp = -squared / (2.0 * noise_level * noise_level * entries)
    scale = gain_ref[0] * jnp.exp(logp - old_ref[0])
    column = jnp.concatenate([tail, jnp.zeros((LANES - 16, LANES), f32)], axis=0).T[0:channels, 0:1]
    product = total[0:channels]
    none = jnp.zeros((channels, LANES), f32)
    parts = []
    for h in range(2):
        values = values_ref[h * channels : (h + 1) * channels, :]
        padded = jnp.concatenate([values, none] if h == 0 else [none, values], axis=0)
        parts.append(dot(product, padded, HIGHEST) + column * offsets_ref[4 + h : 5 + h, :])
    gradient = jnp.concatenate(parts, axis=1) * scale
    for i in range(out_ref.shape[0]):
        out_ref[i] = gradient


def total_kernel(parts_ref, gradient_ref, squares_ref):
    gradient = parts_ref[0]
    for i in range(1, parts_ref.shape[0]):
        gradient += parts_ref[i]
    gradient_ref[...] = gradient
    squares = jnp.sum(gradient * gradient, axis=0, keepdims=True)
    squares = squares[:, 0:LANES] + squares[:, LANES:]
    for s in range(squares_ref.shape[0]):
        squares_ref[s] = squares


def update_kernel(gradient_ref, squares_ref, head_ref, out_ref, *, entries):
    squares = squares_ref[0]
    for s in range(1, squares_ref.shape[0]):
        squares += squares_ref[s]
    mean_square = jnp.sum(squares, axis=1, keepdims=True) * (1.0 / entries)
    change = step_size * gradient_ref[...] * lax.rsqrt(mean_square + update_eps)
    out_ref[...] = (head_ref[...].astype(f32) - change).astype(bf16)


def call(kernel, outs, specs, scratch=()):
    single = not isinstance(outs, (list, tuple))
    return pl.pallas_call(
        kernel,
        out_shape=outs,
        in_specs=specs,
        out_specs=VMEM if single else [VMEM] * len(outs),
        scratch_shapes=list(scratch),
        compiler_params=PARAMS,
    )


def shape(*dims, dtype=f32):
    return jax.ShapeDtypeStruct(dims, dtype)


def on_device(
    latents,
    next_latents,
    noise,
    advantage,
    old_logp,
    timesteps,
    embed_weight,
    modulation,
    qkv_weight,
    head_weight,
):
    role_id = lax.axis_index("role")
    rollouts, blocks = lax.axis_size("dp"), lax.axis_size("seq")
    latent = latents[0, 0].T
    channels, tokens = latent.shape
    width = modulation.shape[2]
    steps_count = modulation.shape[0]
    rows = qkv_weight.shape[2]
    columns = qkv_weight.shape[3]
    head = head_weight[0].T

    steps = lax.all_to_all(
        jnp.broadcast_to(timesteps.reshape(1, 1, 1), (rollouts, 1, LANES)), "dp", 0, 0
    )[:, 0, 0]
    place = lax.axis_index("dp").reshape(1)
    sums, scaled = call(
        partial_kernel,
        [shape(rollouts, 6 * channels + 16, LANES, dtype=bf16), shape(channels, tokens)],
        [SMEM, SMEM] + [VMEM] * 4,
        [pltpu.VMEM((rollouts * (channels + 16), rows), bf16)],
    )(steps, place, latent, embed_weight, modulation, qkv_weight[0])
    sums = lax.all_to_all(sums, "dp", 0, 0)
    pack, values, offsets = call(
        functools.partial(absorb_kernel, factor=width**-0.5, logit=math.log2(math.e) / HD**0.5),
        [shape(3 * channels + 16, LANES, dtype=bf16), shape(2 * channels, HD), shape(8, HD)],
        [VMEM] * 3,
    )(sums, head, scaled)
    packs = lax.all_gather(pack, "seq", axis=0, tiled=False)
    fresh, pieces = call(
        functools.partial(attend_kernel, steps_count=steps_count),
        [shape(channels, tokens, dtype=bf16), shape(blocks, channels + 16, LANES, dtype=bf16)],
        [VMEM] * 5,
        [
            pltpu.VMEM((blocks * tokens, LANES), bf16),
            pltpu.VMEM((channels + 16, blocks * tokens), bf16),
            pltpu.VMEM((blocks, 2 * channels, tokens), bf16),
            pltpu.VMEM((2 * channels, 2 * tokens), bf16),
            pltpu.VMEM((channels, tokens), f32),
        ],
    )(packs, scaled, latent, next_latents[0].T, noise[0].T)
    fresh_received = lax.ppermute(fresh, "role", [(0, 1)])
    pieces = lax.all_to_all(pieces, "seq", 0, 0)
    parts = call(
        functools.partial(gradient_kernel, entries=tokens * blocks * channels),
        shape(rollouts, channels, columns),
        [VMEM, VMEM, VMEM, SMEM, SMEM],
    )(pieces, values, offsets, advantage, old_logp)
    parts = lax.all_to_all(parts, "dp", 0, 0)
    gradient, squares = call(
        total_kernel,
        [shape(channels, columns), shape(blocks, 1, LANES)],
        [VMEM],
    )(parts)
    squares = lax.all_to_all(squares, "seq", 0, 0)
    updated = call(
        functools.partial(update_kernel, entries=columns * blocks * channels),
        shape(channels, columns, dtype=bf16),
        [VMEM] * 3,
    )(gradient, squares, head)
    weight_received = lax.ppermute(updated, "role", [(1, 0)])
    fresh_out = jnp.where(role_id == 0, fresh, fresh_received).T
    weight_out = jnp.where(role_id == 1, updated, weight_received).T
    return (fresh_out[None, None], weight_out[None])


def solution(mesh):
    in_specs = (
        P("role", "dp", "seq", None),
        P("dp", "seq", None),
        P("dp", "seq", None),
        P("dp"),
        P("dp"),
        P("role", "dp"),
        P(),
        P(),
        P("role", None, "dp", "seq"),
        P("role", "seq", None),
    )
    out_specs = (P("role", "dp", "seq", None), P("role", "seq", None))
    return jax.shard_map(
        on_device, mesh=mesh, in_specs=in_specs, out_specs=out_specs, check_vma=False
    )
```

time: 456 us -> 133 us (0.29)
  waiting for transfers between devices: 240 us -> 32.9 us
  matrix products: 79.2 us -> 0 us
  blocking collectives: 73.1 us -> 39 us
  other arithmetic: 33.6 us -> 1.23 us
  Pallas kernels: 0 us -> 30.1 us
  starting transfers between devices: 5.75 us -> 22.7 us
  between operations: 17.3 us -> 2.68 us
    all_gather x2 -> x0, waiting for transfers between devices: 109 us -> none  [the longest x1 77.1 us: on_device(): lax.all_gather(own_embedded, 'seq', axis=0, tiled=True)]
    psum x1 -> x0, waiting for transfers between devices: 73.7 us -> none  [on_device(): gradient = lax.psum(partial_grad, 'dp')]
    psum x2 -> x0, blocking collectives: 56.8 us -> none  [the longest x1 29.8 us: on_device(): square_sum = lax.psum(jnp.sum(gradient * gradient), 'seq')]
    reduce_scatter x1 -> x0, waiting for transfers between devices: 51.8 us -> none  [on_device(): lax.psum_scatter(jnp.dot(rows, head_copy, preferred_element_type=jnp.floa...]
    dot_general x11 -> x0, matrix products: 50.8 us -> none  [the longest x3 25.6 us: on_device(): jnp.dot(modulated, projections[index], preferred_element_type=jnp.float32)]
    pallas_call x0 -> x6, Pallas kernels: none -> 30.1 us  [the longest x1 25.6 us: on_device(): call(functools.partial(attend_kernel, steps_count=steps_count), [shape(ch...]
    all_to_all x0 -> x4, waiting for transfers between devices: none -> 28.6 us  [the longest x1 11.8 us: on_device(): pieces = lax.all_to_all(pieces, 'seq', 0, 0)]
    sub x4 -> x0, matrix products: 28.4 us -> none  [attend(): exp_scores = jnp.exp(scores - row_max)]
  transfers between devices with their start and end apart: 6 -> 6, of which waited for: 5 -> 5; matrix products, arithmetic and copies ran while one was open for 7% -> 0% of each run, Pallas kernels for 0% -> 1%
where the time goes in v1:
time: 133 us; the launch traced here: 132 us
  blocking collectives  39 us (29%)
  waiting for transfers between devices  32.9 us (25%)
  Pallas kernels  30.1 us (23%)
  starting transfers between devices  22.7 us (17%)
  local copies, waits for them, and re-layouts  3.85 us (3%)
  between operations  2.68 us (2%)
    pallas_call x1, Pallas kernels, on_device(): call(functools.partial(attend_kernel, steps_count=steps_count), [shape(ch...  25.6 us
    all_gather x1, blocking collectives, on_device(): packs = lax.all_gather(pack, 'seq', axis=0, tiled=False)  25.5 us
    all_to_all x1, blocking collectives, on_device(): sums = lax.all_to_all(sums, 'dp', 0, 0)  13.5 us
    all_to_all x1, waiting for transfers between devices, on_device(): pieces = lax.all_to_all(pieces, 'seq', 0, 0)  11.8 us
    all_to_all x1, waiting for transfers between devices, on_device(): squares = lax.all_to_all(squares, 'seq', 0, 0)  6.98 us
    all_to_all x1, starting transfers between devices, on_device(): lax.all_to_all(jnp.broadcast_to(timesteps.reshape(1, 1, 1), (rollouts, 1,...  5.95 us
    all_to_all x1, waiting for transfers between devices, on_device(): parts = lax.all_to_all(parts, 'dp', 0, 0)  4.94 us
    all_to_all x1, waiting for transfers between devices, on_device(): lax.all_to_all(jnp.broadcast_to(timesteps.reshape(1, 1, 1), (rollouts, 1,...  4.93 us
  transfers between devices with their start and end apart: 6, of which 5 were waited for; matrix products, arithmetic and copies ran while one was open for 0% of the time, Pallas kernels for 1%

profile of v1, /device:TPU:1, one launch (start us, length us, event | category | flops | bytes accessed | tf_op | source)
XLA Modules:
  0.0 132.4 jit_solution(10519458978973193833)
XLA Ops:
  1.3 0.0 copy-start.4
  1.3 0.6 broadcast_in_dim.14
  1.9 5.9 %all-to-all-start = ((s32[8,1,128]{2,1,0:T(1,128)}), s32[8,1,128]{2,1,0:T(1,128)S(1)}, u32[]{:S(2)}, u32[]{:S(2)}) async-start(s32[8,1,128]{2,1,0:T(1,128)} %broadcast_in_dim.14), calls=%async_computation | async-start | bytes 8192 | tf_op jit(solution)/shard_map/all_to_all | solution.py:302
  7.8 4.9 %all-to-all-done = s32[8,1,128]{2,1,0:T(1,128)S(1)} async-done(((s32[8,1,128]{2,1,0:T(1,128)}), s32[8,1,128]{2,1,0:T(1,128)S(1)}, u32[]{:S(2)}, u32[]{:S(2)}) %all-to-all-start) | async-done | bytes 4128 | tf_op jit(solution)/shard_map/all_to_all | solution.py:302
  12.8 0.2 slice_reduce_fusion.steps_ref
  13.0 0.0 copy-done.4
  13.0 0.0 copy-start
  13.0 1.1 copy-done
  14.1 0.0 copy-start.1
  14.1 1.0 copy-done.1
  15.1 0.0 copy-start.2
  15.1 0.9 copy-done.2
  16.0 1.8 %shard_map.113 = (bf16[8,400,128]{2,1,0:T(8,128)(2,1)S(1)}, f32[64,128]{1,0:T(8,128)S(1)}) custom-call(s32[8]{0:T(128)S(1)} %slice_reduce_fusion.steps_ref, s32[1]{0:T(128)} %bitcast.1.place_ref, bf16[64,128]{1,0:T(8,128)(2,1)S(1)} %bitcast.29, bf16[64,3072]{1,0:T(8,128)(2,1)S(1)} %copy-done.1, f32[10,2,3072]{2,1,0:T(2,128)S(1)} %copy-done.2, ...), custom_call_target="tpu_custom_call" | custom-call | tf_op jit(solution)/shard_map/pallas_call | solution.py:306
  17.8 0.0 copy-start.3
  17.8 13.5 %all_to_all.25.sums_ref = bf16[8,400,128]{2,1,0:T(8,128)(2,1)S(1)} all-to-all(bf16[8,400,128]{2,1,0:T(8,128)(2,1)S(1)} %get-tuple-element.11), channel_id=1, replica_groups=mesh['role'=2,'dp'=8,'seq'=16] {'dp'}, dimensions={0} | all-to-all | bytes 1638400 | tf_op jit(solution)/shard_map/all_to_all | solution.py:312
  31.3 0.0 copy-done.3
  31.3 0.9 shard_map.114
  32.2 0.0 copy-start.5
  32.2 0.0 copy-start.6
  32.2 25.5 %all-gather = bf16[3328,128]{1,0:T(8,128)(2,1)S(1)} all-gather(bf16[208,128]{1,0:T(8,128)(2,1)S(1)} %get-tuple-element.13), channel_id=2, replica_groups=mesh['role'=2,'dp'=8,'seq'=16] {'seq'}, dimensions={0}, use_global_device_ids=true | all-gather | bytes 905216 | tf_op jit(solution)/shard_map/all_gather | solution.py:318
  57.7 0.0 copy-done.5
  57.7 0.0 copy-done.6
  57.7 25.6 %shard_map.115 = (bf16[64,128]{1,0:T(8,128)(2,1)S(1)}, bf16[16,80,128]{2,1,0:T(8,128)(2,1)}) custom-call(bf16[16,208,128]{2,1,0:T(8,128)(2,1)S(1)} %bitcast.25, f32[64,128]{1,0:T(8,128)S(1)} %get-tuple-element.12.scaled_ref, bf16[64,128]{1,0:T(8,128)(2,1)S(1)} %bitcast.30, bf16[64,128]{1,0:T(8,128)(2,1)S(1)} %bitcast.31, bf16[64,128]{1,0:T(8,128)(2,1)S(1)} %bitcast.32), custom_call_target="tpu_custom_call" | custom-call | tf_op jit(solution)/shard_map/pallas_call | solution.py:319
  83.4 3.8 %all-to-all-start.2 = ((bf16[16,80,128]{2,1,0:T(8,128)(2,1)}), bf16[16,80,128]{2,1,0:T(8,128)(2,1)S(1)}, u32[]{:S(2)}, u32[]{:S(2)}) async-start(bf16[16,80,128]{2,1,0:T(8,128)(2,1)} %get-tuple-element.15), calls=%async_computation.2 | async-start | bytes 655360 | tf_op jit(solution)/shard_map/all_to_all | solution.py:332
  88.5 11.8 %all-to-all-done.2.pieces_ref = bf16[16,80,128]{2,1,0:T(8,128)(2,1)S(1)} async-done(((bf16[16,80,128]{2,1,0:T(8,128)(2,1)}), bf16[16,80,128]{2,1,0:T(8,128)(2,1)S(1)}, u32[]{:S(2)}, u32[]{:S(2)}) %all-to-all-start.2) | async-done | bytes 327712 | tf_op jit(solution)/shard_map/all_to_all | solution.py:332
  100.2 1.1 shard_map.116
  101.3 3.5 %all-to-all-start.3 = ((f32[8,64,256]{2,1,0:T(8,128)}), f32[8,64,256]{2,1,0:T(8,128)S(1)}, u32[]{:S(2)}, u32[]{:S(2)}) async-start(f32[8,64,256]{2,1,0:T(8,128)} %shard_map.116), calls=%async_computation.3 | async-start | bytes 1048576 | tf_op jit(solution)/shard_map/all_to_all | solution.py:338
  104.8 4.4 %collective-permute-start = (bf16[64,128]{1,0:T(8,128)(2,1)S(1)}, bf16[64,128]{1,0:T(8,128)(2,1)S(1)}, u32[]{:S(2)}, u32[]{:S(2)}) collective-permute-start(bf16[64,128]{1,0:T(8,128)(2,1)S(1)} %get-tuple-element.14), channel_id=1, source_target_pairs={{0,128},{1,129},{2,130},{3,131},{4,132},{5,133},{6,134},{7,135},{8... | collective-permute-start | bytes 49160 | tf_op jit(solution)/shard_map/ppermute | solution.py:331
  109.2 4.9 %all-to-all-done.3.parts_ref = f32[8,64,256]{2,1,0:T(8,128)S(1)} async-done(((f32[8,64,256]{2,1,0:T(8,128)}), f32[8,64,256]{2,1,0:T(8,128)S(1)}, u32[]{:S(2)}, u32[]{:S(2)}) %all-to-all-start.3) | async-done | bytes 524320 | tf_op jit(solution)/shard_map/all_to_all | solution.py:338
  114.1 0.6 shard_map.117
  114.8 3.8 %all-to-all-start.4 = ((f32[16,1,128]{2,1,0:T(1,128)}), f32[16,1,128]{2,1,0:T(1,128)S(1)}, u32[]{:S(2)}, u32[]{:S(2)}) async-start(f32[16,1,128]{2,1,0:T(1,128)} %get-tuple-element.19), calls=%async_computation.4 | async-start | bytes 16384 | tf_op jit(solution)/shard_map/all_to_all | solution.py:344
  118.5 7.0 %all-to-all-done.4.squares_ref = f32[16,1,128]{2,1,0:T(1,128)S(1)} async-done(((f32[16,1,128]{2,1,0:T(1,128)}), f32[16,1,128]{2,1,0:T(1,128)S(1)}, u32[]{:S(2)}, u32[]{:S(2)}) %all-to-all-start.4) | async-done | bytes 8224 | tf_op jit(solution)/shard_map/all_to_all | solution.py:344
  125.5 0.1 shard_map.118
  125.6 1.3 collective-permute-start.1
  126.9 0.0 collective-permute-done
  126.9 0.6 select_bitcast_fusion.1
  127.5 4.2 %collective-permute-done.1 = bf16[64,256]{1,0:T(8,128)(2,1)S(1)} collective-permute-done((bf16[64,256]{1,0:T(8,128)(2,1)S(1)}, bf16[64,256]{1,0:T(8,128)(2,1)S(1)}, u32[]{:S(2)}, u32[]{:S(2)}) %collective-permute-start.1) | collective-permute-done | bytes 32800 | tf_op jit(solution)/shard_map/ppermute | solution.py:350
  131.8 0.6 select_bitcast_fusion
Async XLA Ops:
  1.3 11.7 %copy-start.4 = (bf16[1,1,128,64]{2,3,1,0:T(8,128)(2,1)S(1)}, bf16[1,1,128,64]{2,3,1,0:T(8,128)(2,1)}, u32[]{:S(2)}) copy-start(bf16[1,1,128,64]{2,3,1,0:T(8,128)(2,1)} %param.10) | copy-start | bytes 49156
  1.9 10.9 %all-to-all-start = ((s32[8,1,128]{2,1,0:T(1,128)}), s32[8,1,128]{2,1,0:T(1,128)S(1)}, u32[]{:S(2)}, u32[]{:S(2)}) async-start(s32[8,1,128]{2,1,0:T(1,128)} %broadcast_in_dim.14), calls=%async_computation | async-start | bytes 8192 | tf_op jit(solution)/shard_map/all_to_all | solution.py:302
  13.0 1.1 copy-start
  14.1 1.0 copy-start.1
  15.1 0.9 copy-start.2
  17.8 13.5 %copy-start.3 = (bf16[1,256,64]{1,2,0:T(8,128)(2,1)S(1)}, bf16[1,256,64]{1,2,0:T(8,128)(2,1)}, u32[]{:S(2)}) copy-start(bf16[1,256,64]{1,2,0:T(8,128)(2,1)} %param.19) | copy-start | bytes 98308
  32.2 25.5 %copy-start.5 = (bf16[1,128,64]{1,2,0:T(8,128)(2,1)S(1)}, bf16[1,128,64]{1,2,0:T(8,128)(2,1)}, u32[]{:S(2)}) copy-start(bf16[1,128,64]{1,2,0:T(8,128)(2,1)} %param.11) | copy-start | bytes 49156
  32.2 25.5 %copy-start.6 = (bf16[1,128,64]{1,2,0:T(8,128)(2,1)S(1)}, bf16[1,128,64]{1,2,0:T(8,128)(2,1)}, u32[]{:S(2)}) copy-start(bf16[1,128,64]{1,2,0:T(8,128)(2,1)} %param.12) | copy-start | bytes 49156
  83.4 16.9 %all-to-all-start.2 = ((bf16[16,80,128]{2,1,0:T(8,128)(2,1)}), bf16[16,80,128]{2,1,0:T(8,128)(2,1)S(1)}, u32[]{:S(2)}, u32[]{:S(2)}) async-start(bf16[16,80,128]{2,1,0:T(8,128)(2,1)} %get-tuple-element.15), calls=%async_computation.2 | async-start | bytes 655360 | tf_op jit(solution)/shard_map/all_to_all | solution.py:332
  101.3 12.8 %all-to-all-start.3 = ((f32[8,64,256]{2,1,0:T(8,128)}), f32[8,64,256]{2,1,0:T(8,128)S(1)}, u32[]{:S(2)}, u32[]{:S(2)}) async-start(f32[8,64,256]{2,1,0:T(8,128)} %shard_map.116), calls=%async_computation.3 | async-start | bytes 1048576 | tf_op jit(solution)/shard_map/all_to_all | solution.py:338
  104.8 22.1 %collective-permute-start = (bf16[64,128]{1,0:T(8,128)(2,1)S(1)}, bf16[64,128]{1,0:T(8,128)(2,1)S(1)}, u32[]{:S(2)}, u32[]{:S(2)}) collective-permute-start(bf16[64,128]{1,0:T(8,128)(2,1)S(1)} %get-tuple-element.14), channel_id=1, source_target_pairs={{0,128},{1,129},{2,130},{3,131},{4,132},{5,133},{6,134},{7,135},{8... | collective-permute-start | bytes 49160 | tf_op jit(solution)/shard_map/ppermute | solution.py:331
  114.8 10.8 %all-to-all-start.4 = ((f32[16,1,128]{2,1,0:T(1,128)}), f32[16,1,128]{2,1,0:T(1,128)S(1)}, u32[]{:S(2)}, u32[]{:S(2)}) async-start(f32[16,1,128]{2,1,0:T(1,128)} %get-tuple-element.19), calls=%async_computation.4 | async-start | bytes 16384 | tf_op jit(solution)/shard_map/all_to_all | solution.py:344
  125.6 6.2 %collective-permute-start.1 = (bf16[64,256]{1,0:T(8,128)(2,1)S(1)}, bf16[64,256]{1,0:T(8,128)(2,1)S(1)}, u32[]{:S(2)}, u32[]{:S(2)}) collective-permute-start(bf16[64,256]{1,0:T(8,128)(2,1)S(1)} %shard_map.118), channel_id=1, source_target_pairs={{128,0},{129,1},{130,2},{131,3},{132,4},{133,5},{134,6},{135,7},{1... | collective-permute-start | bytes 98312 | tf_op jit(solution)/shard_map/ppermute | solution.py:350

commit v2 on v1

v2 whole, which is shorter than its diff:
```python
import functools
import math

import jax
import jax.numpy as jnp
from jax import lax
from jax.experimental import pallas as pl
from jax.experimental.pallas import tpu as pltpu
from jax.sharding import PartitionSpec as P

HD = 128
LANES = 128
CORES = 2

noise_level = 0.8
step_size = 0.5
norm_eps = 1e-06
update_eps = 1e-06

bf16 = jnp.bfloat16
f32 = jnp.float32

VMEM = pl.BlockSpec(memory_space=pltpu.VMEM)
SMEM = pl.BlockSpec(memory_space=pltpu.SMEM)
HBM = pl.BlockSpec(memory_space=pltpu.HBM)


def dot(a, b, precision=None):
    return lax.dot_general(
        a, b, (((1,), (0,)), ((), ())), precision=precision, preferred_element_type=f32
    )


def dot_nt(a, b, precision=None):
    return lax.dot_general(
        a, b, (((1,), (1,)), ((), ())), precision=precision, preferred_element_type=f32
    )


HIGHEST = lax.Precision.HIGHEST


def token_kernel(place_ref, latent_ref, next_ref, noise_ref, embed_ref, tokens_ref, centered_ref, ahead_ref, drawn_ref):
    latent = latent_ref[...].astype(f32)
    ahead_ref[...] = next_ref[...].astype(f32) - latent
    drawn_ref[...] = latent + noise_level * noise_ref[...].astype(f32)
    embed = embed_ref[...]
    embedded = dot(latent.T.astype(bf16), embed).astype(bf16).astype(f32)
    width = embedded.shape[1]
    center = jnp.sum(embedded, axis=1, keepdims=True) * (1.0 / width)
    spread = jnp.sum((embedded - center) * (embedded - center), axis=1, keepdims=True) * (1.0 / width)
    tokens_ref[...] = (latent.T * lax.rsqrt(spread + norm_eps)).T.astype(bf16)
    mean = jnp.sum(embed.astype(f32), axis=1, keepdims=True) * (1.0 / width)
    rows = centered_ref.shape[1]
    start = pl.multiple_of(place_ref[0] * rows, LANES)
    centered_ref[...] = embed_ref[:, pl.ds(start, rows)].astype(f32) - mean


def partial_kernel(place_ref, centered_ref, modulation_ref, weight_ref, sums_ref, left_ref):
    channels, rows = centered_ref.shape
    steps = sums_ref.shape[0]
    block = channels + 16
    start = pl.multiple_of(place_ref[0] * rows, LANES)
    centered = centered_ref[...]
    row = lax.broadcasted_iota(jnp.int32, (16, rows), 0)
    for i in range(steps):
        shift = modulation_ref[i, 0:1, pl.ds(start, rows)]
        scale = modulation_ref[i, 1:2, pl.ds(start, rows)]
        high = shift.astype(bf16).astype(f32)
        tail = jnp.where(row == 0, high, jnp.where(row == 1, shift - high, 0.0))
        left_ref[i * block : i * block + channels, :] = (centered * (1.0 + scale)).astype(bf16)
        left_ref[i * block + channels : (i + 1) * block, :] = tail.astype(bf16)
    slot = lax.broadcasted_iota(jnp.int32, (16, LANES), 0)
    tails = [jnp.zeros((16, LANES), f32) for _ in range(steps)]
    for j in range(3):
        product = dot(left_ref[...], weight_ref[j])
        for i in range(steps):
            for h in range(2):
                c = 2 * j + h
                part = product[i * block : (i + 1) * block, h * HD : (h + 1) * HD]
                sums_ref[i, c * channels : (c + 1) * channels, :] = part[:channels].astype(bf16)
                offset = part[channels : channels + 1] + part[channels + 1 : channels + 2]
                high = offset.astype(bf16).astype(f32)
                tails[i] = jnp.where(slot == c, high, jnp.where(slot == c + 8, offset - high, tails[i]))
    for i in range(steps):
        sums_ref[i, 6 * channels : 6 * channels + 16, :] = tails[i].astype(bf16)


def step_kernel(step_ref, out_ref):
    out_ref[...] = jnp.broadcast_to(step_ref[0, 0], out_ref.shape)


def choose_kernel(steps_ref, sums_ref, out_ref):
    for i in range(out_ref.shape[0]):
        out_ref[i] = sums_ref[steps_ref[i]]


def absorb_kernel(sums_ref, head_ref, pack_ref, values_ref, offsets_ref, *, factor, logit):
    channels = head_ref.shape[0]
    total = sums_ref[0].astype(f32)
    for i in range(1, sums_ref.shape[0]):
        total += sums_ref[i].astype(f32)
    total = total * factor
    blocks = [total[c * channels : (c + 1) * channels] for c in range(6)]
    offsets = total[6 * channels : 6 * channels + 8] + total[6 * channels + 8 : 6 * channels + 16]
    queries, keys, values = blocks[0:2], blocks[2:4], blocks[4:6]
    none = jnp.zeros((channels, LANES), f32)

    def beside(parts):
        return jnp.concatenate([parts[0], none], axis=0), jnp.concatenate([none, parts[1]], axis=0)

    heads = [head_ref[:, h * HD : (h + 1) * HD].astype(f32) for h in range(2)]
    query_pads, key_pads, value_pads = beside(queries), beside(keys), beside(values)
    bilinear = sum(dot_nt(keys[h], query_pads[h], HIGHEST) for h in range(2)) * logit
    outward = sum(dot_nt(heads[h], value_pads[h], HIGHEST) for h in range(2))

    slot = lax.broadcasted_iota(jnp.int32, (8, LANES), 0)
    lane = lax.broadcasted_iota(jnp.int32, (8, LANES), 1)

    def pick(array, c):
        return jnp.sum(jnp.where(slot == c, array, 0.0), axis=0, keepdims=True)

    by_keys = [dot_nt(offsets, key_pads[h], HIGHEST) * logit for h in range(2)]
    by_queries = [dot_nt(offsets, query_pads[h], HIGHEST) * logit for h in range(2)]
    by_heads = [dot_nt(offsets, jnp.concatenate([heads[h], none], axis=0), HIGHEST) for h in range(2)]
    query_constant = pick(by_keys[0], 0) + pick(by_keys[1], 1)
    key_constant = pick(by_queries[0], 2) + pick(by_queries[1], 3)
    both = [
        jnp.sum(pick(offsets, h) * pick(offsets, 2 + h), axis=1, keepdims=True) * logit for h in range(2)
    ]
    outward_constant = pick(by_heads[0], 4) + pick(by_heads[1], 5)
    tail = jnp.where(slot == 0, query_constant, 0.0)
    tail = jnp.where(slot == 1, key_constant, tail)
    tail = jnp.where(slot == 2, jnp.where(lane < channels, both[0], both[1]), tail)
    tail = jnp.where(slot == 3, outward_constant, tail)
    pack = jnp.concatenate([bilinear, outward, tail, jnp.zeros_like(tail)], axis=0).astype(bf16)
    for z in range(pack_ref.shape[0]):
        pack_ref[z] = pack
    values_ref[0:channels, :] = values[0]
    values_ref[channels : 2 * channels, :] = values[1]
    offsets_ref[...] = offsets


def tokens_kernel(core_ref, near_ref, far_ref, keys_ref, values_ref, own_ref):
    half, channels, tokens = near_ref.shape
    unit = (lax.broadcasted_iota(jnp.int32, (LANES - channels, tokens), 0) == 0).astype(f32)
    for s in range(2 * half):
        block = near_ref[s] if s < half else far_ref[s - half]
        here = slice(s * tokens, (s + 1) * tokens)
        values_ref[0:channels, here] = block
        keys_ref[here, :] = jnp.concatenate([block.astype(f32), unit], axis=0).T.astype(bf16)
    values_ref[channels : channels + 16, :] = (
        lax.broadcasted_iota(jnp.int32, (16, 2 * half * tokens), 0) == 0
    ).astype(bf16)
    own_ref[...] = jnp.zeros_like(own_ref)
    for c in range(CORES):
        block = jnp.where(core_ref[0] == c, near_ref[0], near_ref[1])
        for p in range(2):
            left = (CORES * p + c) * tokens
            own_ref[p * channels : (p + 1) * channels, left : left + tokens] = block


def attend_kernel(
    pack_ref,
    keys_ref,
    values_ref,
    own_ref,
    ahead_ref,
    shared_ref,
    attended_ref,
    outward_ref,
    queries_ref,
    scores_ref,
    top_ref,
):
    pairs = pack_ref.shape[0]
    heads = 2 * pairs
    channels, tokens = ahead_ref.shape
    length = keys_ref.shape[0]
    wide = CORES * tokens

    own = own_ref[...]
    tails = pack_ref[:, 2 * channels : 2 * channels + 16, :]
    levels = dot(tails.reshape(pairs * 16, LANES), own)
    tails = tails.astype(f32)
    constants = jnp.concatenate(
        [tails[s, 0:1] for s in range(pairs)]
        + [jnp.sum(tails, axis=0), jnp.zeros((LANES - 16 - pairs, LANES), f32)],
        axis=0,
    ).T
    queries = dot(pack_ref[:, 0:channels, :].reshape(pairs * channels, LANES), own)
    first = lax.broadcasted_iota(jnp.int32, (16, wide), 0) == 0
    for s in range(pairs):
        outward_ref[:, s * LANES : (s + 1) * LANES] = pack_ref[s, channels : 2 * channels, :]
        for p in range(2):
            here = slice(p * wide, (p + 1) * wide)
            shift = constants[p * channels : (p + 1) * channels, s : s + 1]
            level = levels[16 * s + 1 : 16 * s + 2, here] + tails[s, 2:3, p * channels : p * channels + 1]
            queries_ref[2 * s + p, 0:channels, :] = (
                queries[s * channels : (s + 1) * channels, here] + shift
            ).astype(bf16)
            queries_ref[2 * s + p, channels : channels + 16, :] = jnp.where(first, level, 0.0).astype(bf16)
            queries_ref[2 * s + p, channels + 16 :, :] = jnp.zeros((LANES - channels - 16, wide), bf16)

    part = 256

    def start(slot, h):
        query = queries_ref[h]
        top = None
        for c in range(length // part):
            scores = dot(keys_ref[c * part : (c + 1) * part, :], query)
            scores_ref[slot, c * part : (c + 1) * part, :] = scores
            high = jnp.max(scores.reshape(part // 8, 8, wide), axis=0)
            top = high if top is None else jnp.maximum(top, high)
        top_ref[slot] = top

    def finish(slot, h):
        top = jnp.max(top_ref[slot], axis=0, keepdims=True)
        probs = jnp.exp2(scores_ref[slot] - top).astype(bf16)
        sums = dot(values_ref[...], probs)
        attended_ref[h] = (sums[0:channels] * (1.0 / sums[channels : channels + 1])).astype(bf16)

    start(0, 0)

    def body(i, carry):
        start(1, 2 * i + 1)
        finish(0, 2 * i)
        start(0, lax.rem(2 * i + 2, heads))
        finish(1, 2 * i + 1)
        return carry

    lax.fori_loop(0, pairs, body, 0, unroll=2)

    shared_ref[:, 0:wide] = (
        dot(outward_ref[...], attended_ref[...].reshape(heads * channels, wide))
        + constants[0:channels, pairs + 3 : pairs + 4]
    )
    shared_ref[:, wide:] = ahead_ref[...]


def finish_kernel(
    core_ref, mine_ref, other_ref, attended_ref, drawn_ref, fresh_ref, pieces_ref, *, steps_count
):
    channels, tokens = drawn_ref.shape
    wide = CORES * tokens
    is_first = core_ref[0] == 0
    change = (mine_ref[:, 0:wide] + other_ref[:, 0:wide]) * (1.0 / steps_count)
    mine, other = mine_ref[:, wide:], other_ref[:, wide:]
    residual = change + jnp.concatenate(
        [jnp.where(is_first, mine, other), jnp.where(is_first, other, mine)], axis=1
    )
    own = jnp.where(is_first, change[:, 0:tokens], change[:, tokens:])
    fresh_ref[...] = (drawn_ref[...] - own).astype(bf16)
    squared = jnp.sum(jnp.sum(residual * residual, axis=1, keepdims=True), axis=0, keepdims=True)
    residual = residual.astype(bf16)
    padded = jnp.concatenate([residual, jnp.zeros((LANES - channels, wide), bf16)], axis=0)
    column_sums = dot_nt(jnp.ones((16, wide), bf16), padded)
    slot = lax.broadcasted_iota(jnp.int32, (16, LANES), 0)
    high = squared.astype(bf16).astype(f32)
    tail = jnp.where(slot == 0, column_sums, jnp.where(slot == 1, high, jnp.where(slot == 2, squared - high, 0.0)))
    tail = tail.astype(bf16)
    attended = attended_ref[...]
    product = dot_nt(residual, attended.reshape(attended.shape[0] * channels, wide)).astype(bf16)
    for s in range(pieces_ref.shape[0]):
        pieces_ref[s, 0:channels, :] = product[:, s * LANES : (s + 1) * LANES]
        pieces_ref[s, channels : channels + 16, :] = tail


def gradient_kernel(pieces_ref, values_ref, offsets_ref, gain_ref, old_ref, out_ref, *, entries):
    total = pieces_ref[0].astype(f32)
    for s in range(1, pieces_ref.shape[0]):
        total += pieces_ref[s].astype(f32)
    channels = out_ref.shape[1]
    tail = total[channels : channels + 16]
    squared = tail[1:2, 0:1] + tail[2:3, 0:1]
    logp = -squared / (2.0 * noise_level * noise_level * entries)
    scale = gain_ref[0] * jnp.exp(logp - old_ref[0])
    column = jnp.concatenate([tail, jnp.zeros((LANES - 16, LANES), f32)], axis=0).T[0:channels, 0:1]
    product = total[0:channels]
    none = jnp.zeros((channels, LANES), f32)
    parts = []
    for h in range(2):
        values = values_ref[h * channels : (h + 1) * channels, :]
        padded = jnp.concatenate([values, none] if h == 0 else [none, values], axis=0)
        parts.append(dot(product, padded, HIGHEST) + column * offsets_ref[4 + h : 5 + h, :])
    gradient = (jnp.concatenate(parts, axis=1) * scale).astype(bf16)
    for i in range(out_ref.shape[0]):
        out_ref[i] = gradient


def total_kernel(parts_ref, gradient_ref, squares_ref):
    gradient = parts_ref[0].astype(f32)
    for i in range(1, parts_ref.shape[0]):
        gradient += parts_ref[i].astype(f32)
    gradient_ref[...] = gradient
    squares = jnp.sum(gradient * gradient, axis=0, keepdims=True)
    squares = squares[:, 0:LANES] + squares[:, LANES:]
    for s in range(squares_ref.shape[0]):
        squares_ref[s] = squares


def update_kernel(role_ref, gradient_ref, squares_ref, head_ref, fresh_ref, out_ref, *, entries):
    squares = squares_ref[0]
    for s in range(1, squares_ref.shape[0]):
        squares += squares_ref[s]
    mean_square = jnp.sum(squares, axis=1, keepdims=True) * (1.0 / entries)
    change = step_size * gradient_ref[...] * lax.rsqrt(mean_square + update_eps)
    fresh = fresh_ref[...]
    fresh = jnp.concatenate([fresh, jnp.zeros_like(fresh)], axis=1)
    out_ref[...] = jnp.where(role_ref[0] == 1, (head_ref[...].astype(f32) - change).astype(bf16), fresh)


def output_kernel(role_ref, mine_ref, other_ref, fresh_ref, head_ref):
    learner = role_ref[0] == 1
    mine, other = mine_ref[...], other_ref[...]
    head_ref[...] = jnp.where(learner, mine, other)
    fresh_ref[...] = jnp.where(learner, other, mine)[:, 0 : fresh_ref.shape[1]]


def call(kernel, outs, specs, scratch=(), flops=0, mib=32, place=VMEM):
    single = not isinstance(outs, (list, tuple))
    return pl.pallas_call(
        kernel,
        out_shape=outs,
        in_specs=specs,
        out_specs=place if single else [place] * len(outs),
        scratch_shapes=list(scratch),
        compiler_params=pltpu.CompilerParams(vmem_limit_bytes=mib * 1024 * 1024),
        cost_estimate=pl.CostEstimate(flops=flops, bytes_accessed=0, transcendentals=0),
    )


def shape(*dims, dtype=f32):
    return jax.ShapeDtypeStruct(dims, dtype)


def on_device(
    latents,
    next_latents,
    noise,
    advantage,
    old_logp,
    timesteps,
    embed_weight,
    modulation,
    qkv_weight,
    head_weight,
):
    core = (lax.axis_index("seq") % CORES).reshape(1)
    rollouts, blocks = lax.axis_size("dp"), lax.axis_size("seq")
    chips = blocks // CORES
    along = [[CORES * z + c for z in range(chips)] for c in range(CORES)]
    swap = [(i, i ^ 1) for i in range(blocks)]
    latent = latents[0, 0].T
    channels, tokens = latent.shape
    steps_count, _, width = modulation.shape
    rows, columns = qkv_weight.shape[2:]
    wide = CORES * tokens
    head = head_weight[0].T

    steps = call(step_kernel, shape(rollouts, 1, LANES, dtype=jnp.int32), [SMEM], mib=1)(timesteps)
    steps = lax.all_to_all(steps, "dp", 0, 0)[:, 0, 0]
    place = lax.axis_index("dp").reshape(1)
    near, centered, ahead, drawn = call(
        token_kernel,
        [
            shape(channels, tokens, dtype=bf16),
            shape(channels, rows),
            shape(channels, tokens),
            shape(channels, tokens),
        ],
        [SMEM] + [VMEM] * 4,
        flops=10**9,
        mib=16,
    )(place, latent, next_latents[0].T, noise[0].T, embed_weight)

    def across(value, bits):
        return lax.ppermute(value, "seq", [(i, i ^ bits) for i in range(blocks)])

    near = jnp.stack([near, across(near, 1)])
    near = jnp.concatenate([near] + [across(near, bits) for bits in (8, 4, 12)], axis=0)
    sums = call(
        partial_kernel,
        shape(steps_count, 6 * channels + 16, LANES, dtype=bf16),
        [SMEM] + [VMEM] * 3,
        [pltpu.VMEM((steps_count * (channels + 16), rows), bf16)],
        flops=3 * 10**9,
        mib=16,
    )(place, centered, modulation, qkv_weight[0])
    sums = call(
        choose_kernel, shape(rollouts, 6 * channels + 16, LANES, dtype=bf16), [SMEM, VMEM], mib=16
    )(steps, sums)

    far = across(near, 2)
    sums = lax.all_to_all(sums, "dp", 0, 0)
    pack, values, offsets = call(
        functools.partial(absorb_kernel, factor=width**-0.5, logit=math.log2(math.e) / HD**0.5),
        [shape(chips, 2 * channels + 16, LANES, dtype=bf16), shape(2 * channels, HD), shape(8, HD)],
        [VMEM] * 2,
    )(sums, head)
    pack, far = lax.optimization_barrier((pack, far))
    packs = lax.all_to_all(pack, "seq", 0, 0, axis_index_groups=along)
    keys, spread, own = call(
        tokens_kernel,
        [
            shape(blocks * tokens, LANES, dtype=bf16),
            shape(channels + 16, blocks * tokens, dtype=bf16),
            shape(2 * channels, 2 * wide, dtype=bf16),
        ],
        [SMEM, VMEM, VMEM],
        flops=10**9,
    )(core, near, far)
    shared, attended = call(
        attend_kernel,
        [shape(channels, wide + tokens), shape(2 * chips, channels, wide, dtype=bf16)],
        [VMEM] * 5,
        [
            pltpu.VMEM((channels, chips * LANES), bf16),
            pltpu.VMEM((2 * chips, LANES, wide), bf16),
            pltpu.VMEM((2, blocks * tokens, wide), f32),
            pltpu.VMEM((2, 8, wide), f32),
        ],
    )(packs, keys, spread, own, ahead)
    other = lax.ppermute(shared, "seq", swap)
    fresh, pieces = call(
        functools.partial(finish_kernel, steps_count=steps_count),
        [shape(channels, tokens, dtype=bf16), shape(chips, channels + 16, LANES, dtype=bf16)],
        [SMEM] + [VMEM] * 4,
    )(core, shared, other, attended, drawn)
    pieces = lax.all_to_all(pieces, "seq", 0, 0, axis_index_groups=along)
    parts = call(
        functools.partial(gradient_kernel, entries=tokens * blocks * channels),
        shape(rollouts, channels, columns, dtype=bf16),
        [VMEM, VMEM, VMEM, SMEM, SMEM],
    )(pieces, values, offsets, advantage, old_logp)
    parts = lax.all_to_all(parts, "dp", 0, 0)
    gradient, squares = call(
        total_kernel,
        [shape(channels, columns), shape(blocks, 1, LANES)],
        [VMEM],
    )(parts)
    squares = lax.all_to_all(squares, "seq", 0, 0)
    role = lax.axis_index("role").reshape(1)
    mine = call(
        functools.partial(update_kernel, entries=columns * blocks * channels),
        shape(channels, columns, dtype=bf16),
        [SMEM] + [VMEM] * 4,
    )(role, gradient, squares, head, fresh)
    other = lax.ppermute(mine, "role", [(0, 1), (1, 0)])
    fresh_out, head_out = call(
        output_kernel,
        [shape(channels, tokens, dtype=bf16), shape(channels, columns, dtype=bf16)],
        [SMEM, VMEM, VMEM],
    )(role, mine, other)
    return (fresh_out.T[None, None], head_out.T[None])


def solution(mesh):
    in_specs = (
        P("role", "dp", "seq", None),
        P("dp", "seq", None),
        P("dp", "seq", None),
        P("dp"),
        P("dp"),
        P("role", "dp"),
        P(),
        P(),
        P("role", None, "dp", "seq"),
        P("role", "seq", None),
    )
    out_specs = (P("role", "dp", "seq", None), P("role", "seq", None))
    return jax.shard_map(
        on_device, mesh=mesh, in_specs=in_specs, out_specs=out_specs, check_vma=False
    )
```

time: 133 us -> 109 us (0.82)
  blocking collectives: 39 us -> 9.97 us
  starting transfers between devices: 22.7 us -> 42.1 us
  Pallas kernels: 30.1 us -> 16.5 us
    all_gather x1 -> x0, blocking collectives: 25.5 us -> none  [on_device(): packs = lax.all_gather(pack, 'seq', axis=0, tiled=False)]
    pallas_call x2 -> x8, Pallas kernels: 27.4 us -> 13.9 us  [the longest x1 8.32 us: on_device(): call(attend_kernel, [shape(channels, wide + tokens), shape(2 * chips, cha...]
    ppermute x2 -> x7, starting transfers between devices: 5.64 us -> 15.8 us  [the longest x5 10.2 us: across(): return lax.ppermute(value, 'seq', [(i, i ^ bits) for i in range(blocks)])]
    all_to_all x3 -> x4, starting transfers between devices: 13.2 us -> 20.1 us  [the longest x1 5.95 us: on_device(): steps = lax.all_to_all(steps, 'dp', 0, 0)[:, 0, 0]]
    ppermute x2 -> x7, waiting for transfers between devices: 4.24 us -> 8.75 us  [the longest x5 6.02 us: across(): return lax.ppermute(value, 'seq', [(i, i ^ bits) for i in range(blocks)])]
    all_to_all x1, blocking collectives: 13.5 us -> 9.97 us  [on_device(): parts = lax.all_to_all(parts, 'dp', 0, 0)]
    all_to_all x3 -> x4, waiting for transfers between devices: 21.6 us -> 18.2 us  [the longest x1 10.5 us: on_device(): packs = lax.all_to_all(pack, 'seq', 0, 0, axis_index_groups=along)]
    all_to_all x1, starting transfers between devices: 3.78 us -> 6.24 us  [on_device(): squares = lax.all_to_all(squares, 'seq', 0, 0)]
  transfers between devices with their start and end apart: 6 -> 12, of which waited for: 5 -> 9; matrix products, arithmetic and copies ran while one was open for 0% -> 0% of each run, Pallas kernels for 1% -> 5%
where the time goes in v2:
time: 109 us; the launch traced here: 108 us
  starting transfers between devices  42.1 us (39%)
  waiting for transfers between devices  34 us (31%)
  Pallas kernels  16.5 us (15%)
  blocking collectives  9.97 us (9%)
  local copies, waits for them, and re-layouts  2.71 us (2%)
  between operations  2.7 us (2%)
    all_to_all x1, waiting for transfers between devices, on_device(): packs = lax.all_to_all(pack, 'seq', 0, 0, axis_index_groups=along)  10.5 us
    ppermute x5, starting transfers between devices, across(): return lax.ppermute(value, 'seq', [(i, i ^ bits) for i in range(blocks)])  10.2 us
    all_to_all x1, blocking collectives, on_device(): parts = lax.all_to_all(parts, 'dp', 0, 0)  9.97 us
    pallas_call x1, Pallas kernels, on_device(): call(attend_kernel, [shape(channels, wide + tokens), shape(2 * chips, cha...  8.32 us
    all_to_all x1, waiting for transfers between devices, on_device(): pieces = lax.all_to_all(pieces, 'seq', 0, 0, axis_index_groups=along)  7.78 us
    all_to_all x1, waiting for transfers between devices, on_device(): squares = lax.all_to_all(squares, 'seq', 0, 0)  6.98 us
    all_to_all x1, starting transfers between devices, on_device(): squares = lax.all_to_all(squares, 'seq', 0, 0)  6.24 us
    ppermute x5, waiting for transfers between devices, across(): return lax.ppermute(value, 'seq', [(i, i ^ bits) for i in range(blocks)])  6.02 us
  transfers between devices with their start and end apart: 12, of which 9 were waited for; matrix products, arithmetic and copies ran while one was open for 0% of the time, Pallas kernels for 5%

profile of v2, /device:TPU:1, one launch (start us, length us, event | category | flops | bytes accessed | tf_op | source)
XLA Modules:
  0.0 107.9 jit_solution(10506542300649059861)
XLA Ops:
  0.6 0.0 copy-start.4
  1.3 0.6 shard_map.113
  1.9 5.9 %all-to-all-start = ((s32[8,1,128]{2,1,0:T(1,128)}), s32[8,1,128]{2,1,0:T(1,128)S(1)}, u32[]{:S(2)}, u32[]{:S(2)}) async-start(s32[8,1,128]{2,1,0:T(1,128)} %shard_map.113), calls=%async_computation | async-start | bytes 8192 | tf_op jit(solution)/shard_map/all_to_all | solution.py:362
  7.8 0.0 copy-done.4
  7.8 0.0 copy-start.2
  7.9 1.0 copy-done.2
  8.8 0.0 copy-start.5
  8.8 0.7 copy-done.5
  9.6 0.0 copy-start.6
  9.6 0.7 copy-done.6
  10.3 0.0 copy-start.1
  10.3 0.0 copy-start.3
  10.3 0.8 shard_map.114
  11.1 1.0 collective-permute-start
  12.1 0.0 copy-done.1
  12.1 0.0 copy-done.3
  12.1 0.8 shard_map.115.sums_ref
  13.0 0.0 all-to-all-done
  13.0 0.2 slice_reduce_fusion.steps_ref
  13.2 1.5 %shard_map.116 = bf16[8,400,128]{2,1,0:T(8,128)(2,1)} custom-call(s32[8]{0:T(128)S(1)} %slice_reduce_fusion.steps_ref, bf16[10,400,128]{2,1,0:T(8,128)(2,1)S(1)} %shard_map.115.sums_ref), custom_call_target="tpu_custom_call" | custom-call | tf_op jit(solution)/shard_map/pallas_call | solution.py:390
  14.7 5.4 %all-to-all-start.1 = ((bf16[8,400,128]{2,1,0:T(8,128)(2,1)}), bf16[8,400,128]{2,1,0:T(8,128)(2,1)S(1)}, u32[]{:S(2)}, u32[]{:S(2)}) async-start(bf16[8,400,128]{2,1,0:T(8,128)(2,1)} %shard_map.116), calls=%async_computation.1 | async-start | bytes 1638400 | tf_op jit(solution)/shard_map/all_to_all | solution.py:395
  20.2 0.0 collective-permute-done
  20.2 7.0 %collective-permute-start.1 = (bf16[2,64,128]{2,1,0:T(8,128)(2,1)S(1)}, bf16[2,64,128]{2,1,0:T(8,128)(2,1)S(1)}, u32[]{:S(2)}, u32[]{:S(2)}) collective-permute-start(bf16[2,64,128]{2,1,0:T(8,128)(2,1)S(1)} %pad_maximum_fusion), channel_id=1, source_target_pairs={{0,8},{1,9},{2,10},{3,11},{4,12},{5,13},{6,14},{7,15},{8,0},{9,1},... | collective-permute-start | bytes 98312 | tf_op jit(solution)/shard_map/ppermute | solution.py:378
  27.2 1.2 %collective-permute-start.2 = (bf16[2,64,128]{2,1,0:T(8,128)(2,1)S(1)}, bf16[2,64,128]{2,1,0:T(8,128)(2,1)S(1)}, u32[]{:S(2)}, u32[]{:S(2)}) collective-permute-start(bf16[2,64,128]{2,1,0:T(8,128)(2,1)S(1)} %pad_maximum_fusion), channel_id=1, source_target_pairs={{0,4},{1,5},{2,6},{3,7},{4,0},{5,1},{6,2},{7,3},{8,12},{9,13},{10,... | collective-permute-start | bytes 98312 | tf_op jit(solution)/shard_map/ppermute | solution.py:378
  28.4 0.0 collective-permute-start.3
  28.4 0.1 collective-permute-done.1
  28.5 3.3 %collective-permute-done.2 = bf16[2,64,128]{2,1,0:T(8,128)(2,1)S(1)} collective-permute-done((bf16[2,64,128]{2,1,0:T(8,128)(2,1)S(1)}, bf16[2,64,128]{2,1,0:T(8,128)(2,1)S(1)}, u32[]{:S(2)}, u32[]{:S(2)}) %collective-permute-start.2) | collective-permute-done | bytes 32800 | tf_op jit(solution)/shard_map/ppermute | solution.py:378
  31.8 0.0 copy-start
  31.9 1.4 %collective-permute-done.3 = bf16[2,64,128]{2,1,0:T(8,128)(2,1)S(1)} collective-permute-done((bf16[2,64,128]{2,1,0:T(8,128)(2,1)S(1)}, bf16[2,64,128]{2,1,0:T(8,128)(2,1)S(1)}, u32[]{:S(2)}, u32[]{:S(2)}) %collective-permute-start.3) | collective-permute-done | bytes 32800 | tf_op jit(solution)/shard_map/ppermute | solution.py:378
  33.3 1.0 collective-permute-start.4
  34.3 0.0 all-to-all-done.1.sums_ref
  34.3 0.0 copy-done
  34.3 1.6 %shard_map.117 = (bf16[8,144,128]{2,1,0:T(8,128)(2,1)}, f32[128,128]{1,0:T(8,128)S(1)}, f32[8,128]{1,0:T(8,128)S(1)}) custom-call(bf16[8,400,128]{2,1,0:T(8,128)(2,1)S(1)} %all-to-all-done.1.sums_ref, bf16[64,256]{1,0:T(8,128)(2,1)S(1)} %bitcast.26), custom_call_target="tpu_custom_call" | custom-call | tf_op jit(solution)/shard_map/pallas_call | solution.py:396
  35.9 1.2 %collective-permute-done.4.far_ref = bf16[8,64,128]{2,1,0:T(8,128)(2,1)S(1)} collective-permute-done((bf16[8,64,128]{2,1,0:T(8,128)(2,1)S(1)}, bf16[8,64,128]{2,1,0:T(8,128)(2,1)S(1)}, u32[]{:S(2)}, u32[]{:S(2)}) %collective-permute-start.4) | collective-permute-done | bytes 131104 | tf_op jit(solution)/shard_map/ppermute | solution.py:378
  37.1 5.3 %all-to-all-start.2 = ((bf16[8,144,128]{2,1,0:T(8,128)(2,1)}), bf16[8,144,128]{2,1,0:T(8,128)(2,1)S(1)}, u32[]{:S(2)}, u32[]{:S(2)}) async-start(bf16[8,144,128]{2,1,0:T(8,128)(2,1)} %get-tuple-element.25), calls=%async_computation.2 | async-start | bytes 589824 | tf_op jit(solution)/shard_map/all_to_all | solution.py:402
  42.4 0.2 shard_map.118
  42.6 10.5 %all-to-all-done.2.pack_ref = bf16[8,144,128]{2,1,0:T(8,128)(2,1)S(1)} async-done(((bf16[8,144,128]{2,1,0:T(8,128)(2,1)}), bf16[8,144,128]{2,1,0:T(8,128)(2,1)S(1)}, u32[]{:S(2)}, u32[]{:S(2)}) %all-to-all-start.2) | async-done | bytes 294944 | tf_op jit(solution)/shard_map/all_to_all | solution.py:402
  53.1 8.3 %shard_map.119 = (f32[64,384]{1,0:T(8,128)S(1)}, bf16[16,64,256]{2,1,0:T(8,128)(2,1)S(1)}) custom-call(bf16[8,144,128]{2,1,0:T(8,128)(2,1)S(1)} %all-to-all-done.2.pack_ref, bf16[2048,128]{1,0:T(8,128)(2,1)S(1)} %get-tuple-element.27.keys_ref, bf16[80,2048]{1,0:T(8,128)(2,1)S(1)} %get-tuple-element.28.values_ref, ...), custom_call_target="tpu_custom_call" | custom-call | tf_op jit(solution)/shard_map/pallas_call | solution.py:413
  61.4 2.9 %collective-permute-start.5 = (f32[64,384]{1,0:T(8,128)S(1)}, f32[64,384]{1,0:T(8,128)S(1)}, u32[]{:S(2)}, u32[]{:S(2)}) collective-permute-start(f32[64,384]{1,0:T(8,128)S(1)} %get-tuple-element.31.mine_ref), channel_id=1, source_target_pairs={{0,1},{1,0},{2,3},{3,2},{4,5},{5,4},{6,7},{7,6},{8,9},{9,8},{10,11... | collective-permute-start | bytes 294920 | tf_op jit(solution)/shard_map/ppermute | solution.py:424
  64.3 0.9 collective-permute-done.5.other_ref
  65.3 1.0 shard_map.120
  66.2 3.4 %all-to-all-start.3 = ((bf16[8,80,128]{2,1,0:T(8,128)(2,1)}), bf16[8,80,128]{2,1,0:T(8,128)(2,1)S(1)}, u32[]{:S(2)}, u32[]{:S(2)}) async-start(bf16[8,80,128]{2,1,0:T(8,128)(2,1)} %get-tuple-element.34), calls=%async_computation.3 | async-start | bytes 327680 | tf_op jit(solution)/shard_map/all_to_all | solution.py:430
  70.9 7.8 %all-to-all-done.3.pieces_ref = bf16[8,80,128]{2,1,0:T(8,128)(2,1)S(1)} async-done(((bf16[8,80,128]{2,1,0:T(8,128)(2,1)}), bf16[8,80,128]{2,1,0:T(8,128)(2,1)S(1)}, u32[]{:S(2)}, u32[]{:S(2)}) %all-to-all-start.3) | async-done | bytes 163872 | tf_op jit(solution)/shard_map/all_to_all | solution.py:430
  78.7 0.2 shard_map.121
  79.0 10.0 %all_to_all.30.parts_ref = bf16[8,64,256]{2,1,0:T(8,128)(2,1)S(1)} all-to-all(bf16[8,64,256]{2,1,0:T(8,128)(2,1)S(1)} %shard_map.121), channel_id=1, replica_groups=mesh['role'=2,'dp'=8,'seq'=16] {'dp'}, dimensions={0} | all-to-all | bytes 524288 | tf_op jit(solution)/shard_map/all_to_all | solution.py:436
  88.9 0.7 shard_map.122
  89.6 6.2 %all-to-all-start.5 = ((f32[16,1,128]{2,1,0:T(1,128)}), f32[16,1,128]{2,1,0:T(1,128)S(1)}, u32[]{:S(2)}, u32[]{:S(2)}) async-start(f32[16,1,128]{2,1,0:T(1,128)} %get-tuple-element.38), calls=%async_computation.5 | async-start | bytes 16384 | tf_op jit(solution)/shard_map/all_to_all | solution.py:442
  95.8 7.0 %all-to-all-done.5.squares_ref = f32[16,1,128]{2,1,0:T(1,128)S(1)} async-done(((f32[16,1,128]{2,1,0:T(1,128)}), f32[16,1,128]{2,1,0:T(1,128)S(1)}, u32[]{:S(2)}, u32[]{:S(2)}) %all-to-all-start.5) | async-done | bytes 8224 | tf_op jit(solution)/shard_map/all_to_all | solution.py:442
  102.8 0.1 shard_map.123.mine_ref
  102.9 2.6 %collective-permute-start.6 = (bf16[64,256]{1,0:T(8,128)(2,1)S(1)}, bf16[64,256]{1,0:T(8,128)(2,1)S(1)}, u32[]{:S(2)}, u32[]{:S(2)}) collective-permute-start(bf16[64,256]{1,0:T(8,128)(2,1)S(1)} %shard_map.123.mine_ref), channel_id=1, source_target_pairs={{0,128},{128,0},{1,129},{129,1},{2,130},{130,2},{3,131},{131,3},{4... | collective-permute-start | bytes 98312 | tf_op jit(solution)/shard_map/ppermute | solution.py:449
  105.5 1.8 %collective-permute-done.6.other_ref = bf16[64,256]{1,0:T(8,128)(2,1)S(1)} collective-permute-done((bf16[64,256]{1,0:T(8,128)(2,1)S(1)}, bf16[64,256]{1,0:T(8,128)(2,1)S(1)}, u32[]{:S(2)}, u32[]{:S(2)}) %collective-permute-start.6) | collective-permute-done | bytes 32800 | tf_op jit(solution)/shard_map/ppermute | solution.py:449
  107.3 0.6 shard_map.124
  (6 shorter events, 0.0 us)
Async XLA Ops:
  0.6 7.2 %copy-start.4 = (bf16[1,1,128,64]{2,3,1,0:T(8,128)(2,1)S(1)}, bf16[1,1,128,64]{2,3,1,0:T(8,128)(2,1)}, u32[]{:S(2)}) copy-start(bf16[1,1,128,64]{2,3,1,0:T(8,128)(2,1)} %param.10) | copy-start | bytes 49156
  1.9 11.1 %all-to-all-start = ((s32[8,1,128]{2,1,0:T(1,128)}), s32[8,1,128]{2,1,0:T(1,128)S(1)}, u32[]{:S(2)}, u32[]{:S(2)}) async-start(s32[8,1,128]{2,1,0:T(1,128)} %shard_map.113), calls=%async_computation | async-start | bytes 8192 | tf_op jit(solution)/shard_map/all_to_all | solution.py:362
  7.8 1.0 copy-start.2
  8.8 0.7 copy-start.5
  9.6 0.7 copy-start.6
  10.3 1.9 %copy-start.1 = (bf16[1,3,384,256]{3,2,1,0:T(8,128)(2,1)S(1)}, bf16[1,3,384,256]{3,2,1,0:T(8,128)(2,1)}, u32[]{:S(2)}) copy-start(bf16[1,3,384,256]{3,2,1,0:T(8,128)(2,1)} %param.18) | copy-start | bytes 1769476
  10.3 1.9 %copy-start.3 = (f32[10,2,3072]{2,1,0:T(2,128)S(1)}, f32[10,2,3072]{2,1,0:T(2,128)}, u32[]{:S(2)}) copy-start(f32[10,2,3072]{2,1,0:T(2,128)} %modulation_ref.1) | copy-start | bytes 737284
  11.1 9.1 %collective-permute-start = (bf16[64,128]{1,0:T(8,128)(2,1)S(1)}, bf16[64,128]{1,0:T(8,128)(2,1)S(1)}, u32[]{:S(2)}, u32[]{:S(2)}) collective-permute-start(bf16[64,128]{1,0:T(8,128)(2,1)S(1)} %get-tuple-element.24), channel_id=1, source_target_pairs={{0,1},{1,0},{2,3},{3,2},{4,5},{5,4},{6,7},{7,6},{8,9},{9,8},{10,11... | collective-permute-start | bytes 49160 | tf_op jit(solution)/shard_map/ppermute | solution.py:378
  14.7 19.6 %all-to-all-start.1 = ((bf16[8,400,128]{2,1,0:T(8,128)(2,1)}), bf16[8,400,128]{2,1,0:T(8,128)(2,1)S(1)}, u32[]{:S(2)}, u32[]{:S(2)}) async-start(bf16[8,400,128]{2,1,0:T(8,128)(2,1)} %shard_map.116), calls=%async_computation.1 | async-start | bytes 1638400 | tf_op jit(solution)/shard_map/all_to_all | solution.py:395
  20.2 8.3 %collective-permute-start.1 = (bf16[2,64,128]{2,1,0:T(8,128)(2,1)S(1)}, bf16[2,64,128]{2,1,0:T(8,128)(2,1)S(1)}, u32[]{:S(2)}, u32[]{:S(2)}) collective-permute-start(bf16[2,64,128]{2,1,0:T(8,128)(2,1)S(1)} %pad_maximum_fusion), channel_id=1, source_target_pairs={{0,8},{1,9},{2,10},{3,11},{4,12},{5,13},{6,14},{7,15},{8,0},{9,1},... | collective-permute-start | bytes 98312 | tf_op jit(solution)/shard_map/ppermute | solution.py:378
  27.2 4.7 %collective-permute-start.2 = (bf16[2,64,128]{2,1,0:T(8,128)(2,1)S(1)}, bf16[2,64,128]{2,1,0:T(8,128)(2,1)S(1)}, u32[]{:S(2)}, u32[]{:S(2)}) collective-permute-start(bf16[2,64,128]{2,1,0:T(8,128)(2,1)S(1)} %pad_maximum_fusion), channel_id=1, source_target_pairs={{0,4},{1,5},{2,6},{3,7},{4,0},{5,1},{6,2},{7,3},{8,12},{9,13},{10,... | collective-permute-start | bytes 98312 | tf_op jit(solution)/shard_map/ppermute | solution.py:378
  28.4 4.9 %collective-permute-start.3 = (bf16[2,64,128]{2,1,0:T(8,128)(2,1)S(1)}, bf16[2,64,128]{2,1,0:T(8,128)(2,1)S(1)}, u32[]{:S(2)}, u32[]{:S(2)}) collective-permute-start(bf16[2,64,128]{2,1,0:T(8,128)(2,1)S(1)} %pad_maximum_fusion), channel_id=1, source_target_pairs={{0,12},{1,13},{2,14},{3,15},{4,8},{5,9},{6,10},{7,11},{8,4},{9,5},... | collective-permute-start | bytes 98312 | tf_op jit(solution)/shard_map/ppermute | solution.py:378
  31.8 2.4 %copy-start = (bf16[1,256,64]{1,2,0:T(8,128)(2,1)S(1)}, bf16[1,256,64]{1,2,0:T(8,128)(2,1)}, u32[]{:S(2)}) copy-start(bf16[1,256,64]{1,2,0:T(8,128)(2,1)} %param.19) | copy-start | bytes 98308
  33.3 3.8 %collective-permute-start.4 = (bf16[8,64,128]{2,1,0:T(8,128)(2,1)S(1)}, bf16[8,64,128]{2,1,0:T(8,128)(2,1)S(1)}, u32[]{:S(2)}, u32[]{:S(2)}) collective-permute-start(bf16[8,64,128]{2,1,0:T(8,128)(2,1)S(1)} %constant_dynamic-update-slice_fusion.near_ref), channel_id=1, source_target_pairs={{0,2},{1,3},{2,0},{3,1},{4,6},{5,7},{6,4},{7,5},{8,10},{9,11},{10,... | collective-permute-start | bytes 393224 | tf_op jit(solution)/shard_map/ppermute | solution.py:378
  37.1 16.0 %all-to-all-start.2 = ((bf16[8,144,128]{2,1,0:T(8,128)(2,1)}), bf16[8,144,128]{2,1,0:T(8,128)(2,1)S(1)}, u32[]{:S(2)}, u32[]{:S(2)}) async-start(bf16[8,144,128]{2,1,0:T(8,128)(2,1)} %get-tuple-element.25), calls=%async_computation.2 | async-start | bytes 589824 | tf_op jit(solution)/shard_map/all_to_all | solution.py:402
  61.4 3.9 %collective-permute-start.5 = (f32[64,384]{1,0:T(8,128)S(1)}, f32[64,384]{1,0:T(8,128)S(1)}, u32[]{:S(2)}, u32[]{:S(2)}) collective-permute-start(f32[64,384]{1,0:T(8,128)S(1)} %get-tuple-element.31.mine_ref), channel_id=1, source_target_pairs={{0,1},{1,0},{2,3},{3,2},{4,5},{5,4},{6,7},{7,6},{8,9},{9,8},{10,11... | collective-permute-start | bytes 294920 | tf_op jit(solution)/shard_map/ppermute | solution.py:424
  66.2 12.5 %all-to-all-start.3 = ((bf16[8,80,128]{2,1,0:T(8,128)(2,1)}), bf16[8,80,128]{2,1,0:T(8,128)(2,1)S(1)}, u32[]{:S(2)}, u32[]{:S(2)}) async-start(bf16[8,80,128]{2,1,0:T(8,128)(2,1)} %get-tuple-element.34), calls=%async_computation.3 | async-start | bytes 327680 | tf_op jit(solution)/shard_map/all_to_all | solution.py:430
  89.6 13.2 %all-to-all-start.5 = ((f32[16,1,128]{2,1,0:T(1,128)}), f32[16,1,128]{2,1,0:T(1,128)S(1)}, u32[]{:S(2)}, u32[]{:S(2)}) async-start(f32[16,1,128]{2,1,0:T(1,128)} %get-tuple-element.38), calls=%async_computation.5 | async-start | bytes 16384 | tf_op jit(solution)/shard_map/all_to_all | solution.py:442
  102.9 4.4 %collective-permute-start.6 = (bf16[64,256]{1,0:T(8,128)(2,1)S(1)}, bf16[64,256]{1,0:T(8,128)(2,1)S(1)}, u32[]{:S(2)}, u32[]{:S(2)}) collective-permute-start(bf16[64,256]{1,0:T(8,128)(2,1)S(1)} %shard_map.123.mine_ref), channel_id=1, source_target_pairs={{0,128},{128,0},{1,129},{129,1},{2,130},{130,2},{3,131},{131,3},{4... | collective-permute-start | bytes 98312 | tf_op jit(solution)/shard_map/ppermute | solution.py:449

commit v3 on v2

--- a/solution.py
+++ b/solution.py
@@ -133,9 +133,7 @@
     tail = jnp.where(slot == 1, key_constant, tail)
     tail = jnp.where(slot == 2, jnp.where(lane < channels, both[0], both[1]), tail)
     tail = jnp.where(slot == 3, outward_constant, tail)
-    pack = jnp.concatenate([bilinear, outward, tail, jnp.zeros_like(tail)], axis=0).astype(bf16)
-    for z in range(pack_ref.shape[0]):
-        pack_ref[z] = pack
+    pack_ref[0] = jnp.concatenate([bilinear, outward, tail, jnp.zeros_like(tail)], axis=0).astype(bf16)
     values_ref[0:channels, :] = values[0]
     values_ref[channels : 2 * channels, :] = values[1]
     offsets_ref[...] = offsets
@@ -154,7 +152,7 @@
     ).astype(bf16)
     own_ref[...] = jnp.zeros_like(own_ref)
     for c in range(CORES):
-        block = jnp.where(core_ref[0] == c, near_ref[0], near_ref[1])
+        block = jnp.where(core_ref[0] == c, near_ref[0], far_ref[0])
         for p in range(2):
             left = (CORES * p + c) * tokens
             own_ref[p * channels : (p + 1) * channels, left : left + tokens] = block
@@ -165,7 +163,7 @@
     keys_ref,
     values_ref,
     own_ref,
-    ahead_ref,
+    before_ref,
     shared_ref,
     attended_ref,
     outward_ref,
@@ -175,9 +173,8 @@
 ):
     pairs = pack_ref.shape[0]
     heads = 2 * pairs
-    channels, tokens = ahead_ref.shape
+    channels, wide = before_ref.shape
     length = keys_ref.shape[0]
-    wide = CORES * tokens
 
     own = own_ref[...]
     tails = pack_ref[:, 2 * channels : 2 * channels + 16, :]
@@ -231,15 +228,25 @@
 
     lax.fori_loop(0, pairs, body, 0, unroll=2)
 
-    shared_ref[:, 0:wide] = (
-        dot(outward_ref[...], attended_ref[...].reshape(heads * channels, wide))
+    shared_ref[...] = (
+        before_ref[...]
+        + dot(outward_ref[...], attended_ref[...].reshape(heads * channels, wide))
         + constants[0:channels, pairs + 3 : pairs + 4]
     )
-    shared_ref[:, wide:] = ahead_ref[...]
 
 
 def finish_kernel(
-    core_ref, mine_ref, other_ref, attended_ref, drawn_ref, fresh_ref, pieces_ref, *, steps_count
+    core_ref,
+    chip_ref,
+    mine_ref,
+    other_ref,
+    attended_ref,
+    attended_far_ref,
+    drawn_ref,
+    fresh_ref,
+    pieces_ref,
+    *,
+    steps_count,
 ):
     channels, tokens = drawn_ref.shape
     wide = CORES * tokens
@@ -259,11 +266,13 @@
     high = squared.astype(bf16).astype(f32)
     tail = jnp.where(slot == 0, column_sums, jnp.where(slot == 1, high, jnp.where(slot == 2, squared - high, 0.0)))
     tail = tail.astype(bf16)
-    attended = attended_ref[...]
-    product = dot_nt(residual, attended.reshape(attended.shape[0] * channels, wide)).astype(bf16)
-    for s in range(pieces_ref.shape[0]):
-        pieces_ref[s, 0:channels, :] = product[:, s * LANES : (s + 1) * LANES]
-        pieces_ref[s, channels : channels + 16, :] = tail
+    half = pieces_ref.shape[0] // 2
+    for part, bits in ((attended_ref, 0), (attended_far_ref, 2 * half - 1)):
+        product = dot_nt(residual, part[...].reshape(2 * half * channels, wide)).astype(bf16)
+        for s in range(half):
+            place = chip_ref[0] ^ (s ^ bits)
+            pieces_ref[place, 0:channels, :] = product[:, s * LANES : (s + 1) * LANES]
+            pieces_ref[place, channels : channels + 16, :] = tail
 
 
 def gradient_kernel(pieces_ref, values_ref, offsets_ref, gain_ref, old_ref, out_ref, *, entries):
@@ -347,16 +356,19 @@
     head_weight,
 ):
     core = (lax.axis_index("seq") % CORES).reshape(1)
+    chip = (lax.axis_index("seq") // CORES).reshape(1)
     rollouts, blocks = lax.axis_size("dp"), lax.axis_size("seq")
     chips = blocks // CORES
     along = [[CORES * z + c for z in range(chips)] for c in range(CORES)]
-    swap = [(i, i ^ 1) for i in range(blocks)]
     latent = latents[0, 0].T
     channels, tokens = latent.shape
     steps_count, _, width = modulation.shape
     rows, columns = qkv_weight.shape[2:]
     wide = CORES * tokens
     head = head_weight[0].T
+
+    def across(value, axis, bits):
+        return lax.ppermute(value, axis, [(i, i ^ bits) for i in range(lax.axis_size(axis))])
 
     steps = call(step_kernel, shape(rollouts, 1, LANES, dtype=jnp.int32), [SMEM], mib=1)(timesteps)
     steps = lax.all_to_all(steps, "dp", 0, 0)[:, 0, 0]
@@ -374,11 +386,9 @@
         mib=16,
     )(place, latent, next_latents[0].T, noise[0].T, embed_weight)
 
-    def across(value, bits):
-        return lax.ppermute(value, "seq", [(i, i ^ bits) for i in range(blocks)])
-
-    near = jnp.stack([near, across(near, 1)])
-    near = jnp.concatenate([near] + [across(near, bits) for bits in (8, 4, 12)], axis=0)
+    near = jnp.stack([near, across(near, "seq", 14)])
+    near = jnp.concatenate([near] + [across(near, "seq", bits) for bits in (2, 4, 6)], axis=0)
+    far = across(near, "seq", 1)
     sums = call(
         partial_kernel,
         shape(steps_count, 6 * channels + 16, LANES, dtype=bf16),
@@ -391,15 +401,14 @@
         choose_kernel, shape(rollouts, 6 * channels + 16, LANES, dtype=bf16), [SMEM, VMEM], mib=16
     )(steps, sums)
 
-    far = across(near, 2)
     sums = lax.all_to_all(sums, "dp", 0, 0)
     pack, values, offsets = call(
         functools.partial(absorb_kernel, factor=width**-0.5, logit=math.log2(math.e) / HD**0.5),
-        [shape(chips, 2 * channels + 16, LANES, dtype=bf16), shape(2 * channels, HD), shape(8, HD)],
+        [shape(1, 2 * channels + 16, LANES, dtype=bf16), shape(2 * channels, HD), shape(8, HD)],
         [VMEM] * 2,
     )(sums, head)
-    pack, far = lax.optimization_barrier((pack, far))
-    packs = lax.all_to_all(pack, "seq", 0, 0, axis_index_groups=along)
+    pack = jnp.concatenate([pack] + [across(pack, "seq", bits) for bits in (2, 4, 6)], axis=0)
+    pack_far = across(pack, "seq", 14)
     keys, spread, own = call(
         tokens_kernel,
         [
@@ -410,23 +419,30 @@
         [SMEM, VMEM, VMEM],
         flops=10**9,
     )(core, near, far)
-    shared, attended = call(
-        attend_kernel,
-        [shape(channels, wide + tokens), shape(2 * chips, channels, wide, dtype=bf16)],
-        [VMEM] * 5,
-        [
-            pltpu.VMEM((channels, chips * LANES), bf16),
-            pltpu.VMEM((2 * chips, LANES, wide), bf16),
-            pltpu.VMEM((2, blocks * tokens, wide), f32),
-            pltpu.VMEM((2, 8, wide), f32),
-        ],
-    )(packs, keys, spread, own, ahead)
-    other = lax.ppermute(shared, "seq", swap)
+    def attend(pack, before):
+        count = pack.shape[0]
+        return call(
+            attend_kernel,
+            [shape(channels, wide), shape(2 * count, channels, wide, dtype=bf16)],
+            [VMEM] * 5,
+            [
+                pltpu.VMEM((channels, count * LANES), bf16),
+                pltpu.VMEM((2 * count, LANES, wide), bf16),
+                pltpu.VMEM((2, blocks * tokens, wide), f32),
+                pltpu.VMEM((2, 8, wide), f32),
+            ],
+            flops=4 * 10**9,
+        )(pack, keys, spread, own, before)
+
+    shared, attended = attend(pack, jnp.zeros((channels, wide), f32))
+    shared, attended_far = attend(pack_far, shared)
+    shared = jnp.concatenate([shared, ahead], axis=1)
+    other = across(shared, "seq", 1)
     fresh, pieces = call(
         functools.partial(finish_kernel, steps_count=steps_count),
         [shape(channels, tokens, dtype=bf16), shape(chips, channels + 16, LANES, dtype=bf16)],
-        [SMEM] + [VMEM] * 4,
-    )(core, shared, other, attended, drawn)
+        [SMEM, SMEM] + [VMEM] * 5,
+    )(core, chip, shared, other, attended, attended_far, drawn)
     pieces = lax.all_to_all(pieces, "seq", 0, 0, axis_index_groups=along)
     parts = call(
         functools.partial(gradient_kernel, entries=tokens * blocks * channels),

time: 109 us -> 105 us (0.963)
  waiting for transfers between devices: 34 us -> 26 us
  starting transfers between devices: 42.1 us -> 44.8 us
    all_to_all x1 -> x0, waiting for transfers between devices: 10.5 us -> none  [on_device(): packs = lax.all_to_all(pack, 'seq', 0, 0, axis_index_groups=along)]
    ppermute x6 -> x10, starting transfers between devices: 13.2 us -> 21.6 us  [across(): lax.ppermute(value, axis, [(i, i ^ bits) for i in range(lax.axis_size(axi...]
    all_to_all x1 -> x0, starting transfers between devices: 5.32 us -> none  [on_device(): packs = lax.all_to_all(pack, 'seq', 0, 0, axis_index_groups=along)]
    ppermute x6 -> x10, waiting for transfers between devices: 6.96 us -> 9.4 us  [across(): lax.ppermute(value, axis, [(i, i ^ bits) for i in range(lax.axis_size(axi...]
    pallas_call x1 -> x2, Pallas kernels: 8.32 us -> 9.54 us  [attend(): call(attend_kernel, [shape(channels, wide), shape(2 * count, channels, wi...]
    unnamed x18 -> x22, local copies, waits for them, and re-layouts: 2.47 us -> 3.03 us
  transfers between devices with their start and end apart: 12 -> 15, of which waited for: 9 -> 10; matrix products, arithmetic and copies ran while one was open for 0% -> 0% of each run, Pallas kernels for 5% -> 8%
where the time goes in v3:
time: 105 us; the launch traced here: 104 us
  starting transfers between devices  44.8 us (43%)
  waiting for transfers between devices  26 us (25%)
  Pallas kernels  17 us (16%)
  blocking collectives  10.4 us (10%)
  local copies, waits for them, and re-layouts  3.29 us (3%)
  between operations  2.76 us (3%)
    ppermute x10, starting transfers between devices, across(): lax.ppermute(value, axis, [(i, i ^ bits) for i in range(lax.axis_size(axi...  21.6 us
    all_to_all x1, blocking collectives, on_device(): parts = lax.all_to_all(parts, 'dp', 0, 0)  10.4 us
    pallas_call x2, Pallas kernels, attend(): call(attend_kernel, [shape(channels, wide), shape(2 * count, channels, wi...  9.54 us
    ppermute x10, waiting for transfers between devices, across(): lax.ppermute(value, axis, [(i, i ^ bits) for i in range(lax.axis_size(axi...  9.4 us
    all_to_all x1, waiting for transfers between devices, on_device(): pieces = lax.all_to_all(pieces, 'seq', 0, 0, axis_index_groups=along)  7.78 us
    all_to_all x1, waiting for transfers between devices, on_device(): squares = lax.all_to_all(squares, 'seq', 0, 0)  6.98 us
    all_to_all x1, starting transfers between devices, on_device(): squares = lax.all_to_all(squares, 'seq', 0, 0)  6.26 us
    all_to_all x1, starting transfers between devices, on_device(): steps = lax.all_to_all(steps, 'dp', 0, 0)[:, 0, 0]  5.95 us
  transfers between devices with their start and end apart: 15, of which 10 were waited for; matrix products, arithmetic and copies ran while one was open for 0% of the time, Pallas kernels for 8%

profile of v3, /device:TPU:1, one launch (start us, length us, event | category | flops | bytes accessed | tf_op | source)
XLA Modules:
  0.0 104.2 jit_solution(7955215718409677751)
XLA Ops:
  0.6 0.0 copy-start.4
  1.3 0.6 shard_map.113
  1.9 5.9 %all-to-all-start = ((s32[8,1,128]{2,1,0:T(1,128)}), s32[8,1,128]{2,1,0:T(1,128)S(1)}, u32[]{:S(2)}, u32[]{:S(2)}) async-start(s32[8,1,128]{2,1,0:T(1,128)} %shard_map.113), calls=%async_computation | async-start | bytes 8192 | tf_op jit(solution)/shard_map/all_to_all | solution.py:374
  7.8 0.0 copy-done.4
  7.8 0.0 copy-start.2
  7.9 1.0 copy-done.2
  8.8 0.0 copy-start.5
  8.8 0.7 copy-done.5
  9.6 0.0 copy-start.6
  9.6 0.7 copy-done.6
  10.3 0.0 copy-start.1
  10.3 0.0 copy-start.3
  10.3 0.8 shard_map.114
  11.1 5.6 %collective-permute-start.4 = (bf16[64,128]{1,0:T(8,128)(2,1)S(1)}, bf16[64,128]{1,0:T(8,128)(2,1)S(1)}, u32[]{:S(2)}, u32[]{:S(2)}) collective-permute-start(bf16[64,128]{1,0:T(8,128)(2,1)S(1)} %get-tuple-element.24), channel_id=1, source_target_pairs={{0,14},{1,15},{2,12},{3,13},{4,10},{5,11},{6,8},{7,9},{8,6},{9,7},... | collective-permute-start | bytes 49160 | tf_op jit(solution)/shard_map/ppermute | solution.py:371
  16.8 0.0 copy-done.1
  16.8 0.0 copy-done.3
  16.8 0.8 shard_map.115.sums_ref
  17.6 0.0 all-to-all-done
  17.6 0.2 slice_reduce_fusion.steps_ref
  17.8 1.5 %shard_map.116 = bf16[8,400,128]{2,1,0:T(8,128)(2,1)} custom-call(s32[8]{0:T(128)S(1)} %slice_reduce_fusion.steps_ref, bf16[10,400,128]{2,1,0:T(8,128)(2,1)S(1)} %shard_map.115.sums_ref), custom_call_target="tpu_custom_call" | custom-call | tf_op jit(solution)/shard_map/pallas_call | solution.py:400
  19.4 5.1 %all-to-all-start.1 = ((bf16[8,400,128]{2,1,0:T(8,128)(2,1)}), bf16[8,400,128]{2,1,0:T(8,128)(2,1)S(1)}, u32[]{:S(2)}, u32[]{:S(2)}) async-start(bf16[8,400,128]{2,1,0:T(8,128)(2,1)} %shard_map.116), calls=%async_computation.1 | async-start | bytes 1638400 | tf_op jit(solution)/shard_map/all_to_all | solution.py:404
  24.5 0.0 collective-permute-done.4
  24.5 1.7 %collective-permute-start.5 = (bf16[2,64,128]{2,1,0:T(8,128)(2,1)S(1)}, bf16[2,64,128]{2,1,0:T(8,128)(2,1)S(1)}, u32[]{:S(2)}, u32[]{:S(2)}) collective-permute-start(bf16[2,64,128]{2,1,0:T(8,128)(2,1)S(1)} %pad_maximum_fusion), channel_id=1, source_target_pairs={{0,2},{1,3},{2,0},{3,1},{4,6},{5,7},{6,4},{7,5},{8,10},{9,11},{10,... | collective-permute-start | bytes 98312 | tf_op jit(solution)/shard_map/ppermute | solution.py:371
  26.2 0.5 collective-permute-start.6
  26.8 1.6 %collective-permute-start.7 = (bf16[2,64,128]{2,1,0:T(8,128)(2,1)S(1)}, bf16[2,64,128]{2,1,0:T(8,128)(2,1)S(1)}, u32[]{:S(2)}, u32[]{:S(2)}) collective-permute-start(bf16[2,64,128]{2,1,0:T(8,128)(2,1)S(1)} %pad_maximum_fusion), channel_id=1, source_target_pairs={{0,6},{1,7},{2,4},{3,5},{4,2},{5,3},{6,0},{7,1},{8,14},{9,15},{10,... | collective-permute-start | bytes 98312 | tf_op jit(solution)/shard_map/ppermute | solution.py:371
  28.4 0.0 collective-permute-done.5
  28.4 1.6 %collective-permute-done.6 = bf16[2,64,128]{2,1,0:T(8,128)(2,1)S(1)} collective-permute-done((bf16[2,64,128]{2,1,0:T(8,128)(2,1)S(1)}, bf16[2,64,128]{2,1,0:T(8,128)(2,1)S(1)}, u32[]{:S(2)}, u32[]{:S(2)}) %collective-permute-start.6) | collective-permute-done | bytes 32800 | tf_op jit(solution)/shard_map/ppermute | solution.py:371
  30.1 1.5 %collective-permute-done.7 = bf16[2,64,128]{2,1,0:T(8,128)(2,1)S(1)} collective-permute-done((bf16[2,64,128]{2,1,0:T(8,128)(2,1)S(1)}, bf16[2,64,128]{2,1,0:T(8,128)(2,1)S(1)}, u32[]{:S(2)}, u32[]{:S(2)}) %collective-permute-start.7) | collective-permute-done | bytes 32800 | tf_op jit(solution)/shard_map/ppermute | solution.py:371
  31.6 3.0 %collective-permute-start.8 = (bf16[8,64,128]{2,1,0:T(8,128)(2,1)S(1)}, bf16[8,64,128]{2,1,0:T(8,128)(2,1)S(1)}, u32[]{:S(2)}, u32[]{:S(2)}) collective-permute-start(bf16[8,64,128]{2,1,0:T(8,128)(2,1)S(1)} %constant_dynamic-update-slice_fusion.4.near_ref), channel_id=1, source_target_pairs={{0,1},{1,0},{2,3},{3,2},{4,5},{5,4},{6,7},{7,6},{8,9},{9,8},{10,11... | collective-permute-start | bytes 393224 | tf_op jit(solution)/shard_map/ppermute | solution.py:371
  34.6 1.0 collective-permute-done.8.far_ref
  35.6 0.0 copy-start
  35.6 0.2 shard_map.118
  35.8 0.0 all-to-all-done.1.sums_ref
  35.8 0.5 copy-done
  36.3 0.9 shard_map.117
  37.2 0.1 collective-permute-start
  37.3 1.9 %collective-permute-start.1 = (bf16[1,144,128]{2,1,0:T(8,128)(2,1)S(1)}, bf16[1,144,128]{2,1,0:T(8,128)(2,1)S(1)}, u32[]{:S(2)}, u32[]{:S(2)}) collective-permute-start(bf16[1,144,128]{2,1,0:T(8,128)(2,1)S(1)} %get-tuple-element.23), channel_id=1, source_target_pairs={{0,4},{1,5},{2,6},{3,7},{4,0},{5,1},{6,2},{7,3},{8,12},{9,13},{10,... | collective-permute-start | bytes 110600 | tf_op jit(solution)/shard_map/ppermute | solution.py:371
  39.2 1.6 %collective-permute-start.2 = (bf16[1,144,128]{2,1,0:T(8,128)(2,1)S(1)}, bf16[1,144,128]{2,1,0:T(8,128)(2,1)S(1)}, u32[]{:S(2)}, u32[]{:S(2)}) collective-permute-start(bf16[1,144,128]{2,1,0:T(8,128)(2,1)S(1)} %get-tuple-element.23), channel_id=1, source_target_pairs={{0,6},{1,7},{2,4},{3,5},{4,2},{5,3},{6,0},{7,1},{8,14},{9,15},{10,... | collective-permute-start | bytes 110600 | tf_op jit(solution)/shard_map/ppermute | solution.py:371
  40.8 0.0 collective-permute-done
  40.9 0.3 collective-permute-done.1
  41.1 3.1 %collective-permute-done.2 = bf16[1,144,128]{2,1,0:T(8,128)(2,1)S(1)} collective-permute-done((bf16[1,144,128]{2,1,0:T(8,128)(2,1)S(1)}, bf16[1,144,128]{2,1,0:T(8,128)(2,1)S(1)}, u32[]{:S(2)}, u32[]{:S(2)}) %collective-permute-start.2) | collective-permute-done | bytes 36896 | tf_op jit(solution)/shard_map/ppermute | solution.py:371
  44.2 0.3 collective-permute-start.3
  44.5 4.8 %shard_map.119 = (f32[64,256]{1,0:T(8,128)S(1)}, bf16[8,64,256]{2,1,0:T(8,128)(2,1)S(1)}) custom-call(bf16[4,144,128]{2,1,0:T(8,128)(2,1)S(1)} %constant_dynamic-update-slice_fusion.pack_ref, bf16[2048,128]{1,0:T(8,128)(2,1)S(1)} %get-tuple-element.25.keys_ref, bf16[80,2048]{1,0:T(8,128)(2,1)S(1)} %get-tuple-element.26.values_ref, ...), custom_call_target="tpu_custom_call" | custom-call | flops 4000000000 | tf_op jit(solution)/shard_map/pallas_call | solution.py:424
  49.3 1.0 collective-permute-done.3.pack_ref
  50.2 4.8 %shard_map.120 = (f32[64,256]{1,0:T(8,128)S(1)}, bf16[8,64,256]{2,1,0:T(8,128)(2,1)S(1)}) custom-call(bf16[4,144,128]{2,1,0:T(8,128)(2,1)S(1)} %collective-permute-done.3.pack_ref, bf16[2048,128]{1,0:T(8,128)(2,1)S(1)} %get-tuple-element.25.keys_ref, bf16[80,2048]{1,0:T(8,128)(2,1)S(1)} %get-tuple-element.26.values_ref, ...), custom_call_target="tpu_custom_call" | custom-call | flops 4000000000 | tf_op jit(solution)/shard_map/pallas_call | solution.py:424
  55.0 5.2 %collective-permute-start.9 = (f32[64,384]{1,0:T(8,128)S(1)}, f32[64,384]{1,0:T(8,128)S(1)}, u32[]{:S(2)}, u32[]{:S(2)}) collective-permute-start(f32[64,384]{1,0:T(8,128)S(1)} %constant_dynamic-update-slice_fusion.9.mine_ref), channel_id=1, source_target_pairs={{0,1},{1,0},{2,3},{3,2},{4,5},{5,4},{6,7},{7,6},{8,9},{9,8},{10,11... | collective-permute-start | bytes 294920 | tf_op jit(solution)/shard_map/ppermute | solution.py:371
  60.2 0.9 collective-permute-done.9.other_ref
  61.2 1.0 shard_map.121
  62.2 3.4 %all-to-all-start.2 = ((bf16[8,80,128]{2,1,0:T(8,128)(2,1)}), bf16[8,80,128]{2,1,0:T(8,128)(2,1)S(1)}, u32[]{:S(2)}, u32[]{:S(2)}) async-start(bf16[8,80,128]{2,1,0:T(8,128)(2,1)} %get-tuple-element.34), calls=%async_computation.2 | async-start | bytes 327680 | tf_op jit(solution)/shard_map/all_to_all | solution.py:446
  66.8 7.8 %all-to-all-done.2.pieces_ref = bf16[8,80,128]{2,1,0:T(8,128)(2,1)S(1)} async-done(((bf16[8,80,128]{2,1,0:T(8,128)(2,1)}), bf16[8,80,128]{2,1,0:T(8,128)(2,1)S(1)}, u32[]{:S(2)}, u32[]{:S(2)}) %all-to-all-start.2) | async-done | bytes 163872 | tf_op jit(solution)/shard_map/all_to_all | solution.py:446
  74.6 0.2 shard_map.122
  74.9 10.4 %all_to_all.25.parts_ref = bf16[8,64,256]{2,1,0:T(8,128)(2,1)S(1)} all-to-all(bf16[8,64,256]{2,1,0:T(8,128)(2,1)S(1)} %shard_map.122), channel_id=1, replica_groups=mesh['role'=2,'dp'=8,'seq'=16] {'dp'}, dimensions={0} | all-to-all | bytes 524288 | tf_op jit(solution)/shard_map/all_to_all | solution.py:452
  85.2 0.7 shard_map.123
  85.9 6.3 %all-to-all-start.4 = ((f32[16,1,128]{2,1,0:T(1,128)}), f32[16,1,128]{2,1,0:T(1,128)S(1)}, u32[]{:S(2)}, u32[]{:S(2)}) async-start(f32[16,1,128]{2,1,0:T(1,128)} %get-tuple-element.38), calls=%async_computation.4 | async-start | bytes 16384 | tf_op jit(solution)/shard_map/all_to_all | solution.py:458
  92.1 7.0 %all-to-all-done.4.squares_ref = f32[16,1,128]{2,1,0:T(1,128)S(1)} async-done(((f32[16,1,128]{2,1,0:T(1,128)}), f32[16,1,128]{2,1,0:T(1,128)S(1)}, u32[]{:S(2)}, u32[]{:S(2)}) %all-to-all-start.4) | async-done | bytes 8224 | tf_op jit(solution)/shard_map/all_to_all | solution.py:458
  99.1 0.1 shard_map.124.mine_ref
  99.2 2.5 %collective-permute-start.10 = (bf16[64,256]{1,0:T(8,128)(2,1)S(1)}, bf16[64,256]{1,0:T(8,128)(2,1)S(1)}, u32[]{:S(2)}, u32[]{:S(2)}) collective-permute-start(bf16[64,256]{1,0:T(8,128)(2,1)S(1)} %shard_map.124.mine_ref), channel_id=1, source_target_pairs={{0,128},{128,0},{1,129},{129,1},{2,130},{130,2},{3,131},{131,3},{4... | collective-permute-start | bytes 98312 | tf_op jit(solution)/shard_map/ppermute | solution.py:465
  101.8 1.8 %collective-permute-done.10.other_ref = bf16[64,256]{1,0:T(8,128)(2,1)S(1)} collective-permute-done((bf16[64,256]{1,0:T(8,128)(2,1)S(1)}, bf16[64,256]{1,0:T(8,128)(2,1)S(1)}, u32[]{:S(2)}, u32[]{:S(2)}) %collective-permute-start.10) | collective-permute-done | bytes 32800 | tf_op jit(solution)/shard_map/ppermute | solution.py:465
  103.6 0.6 shard_map.125
  (13 shorter events, 0.1 us)
Async XLA Ops:
  0.6 7.2 %copy-start.4 = (bf16[1,1,128,64]{2,3,1,0:T(8,128)(2,1)S(1)}, bf16[1,1,128,64]{2,3,1,0:T(8,128)(2,1)}, u32[]{:S(2)}) copy-start(bf16[1,1,128,64]{2,3,1,0:T(8,128)(2,1)} %param.10) | copy-start | bytes 49156
  1.9 15.7 %all-to-all-start = ((s32[8,1,128]{2,1,0:T(1,128)}), s32[8,1,128]{2,1,0:T(1,128)S(1)}, u32[]{:S(2)}, u32[]{:S(2)}) async-start(s32[8,1,128]{2,1,0:T(1,128)} %shard_map.113), calls=%async_computation | async-start | bytes 8192 | tf_op jit(solution)/shard_map/all_to_all | solution.py:374
  7.8 1.0 copy-start.2
  8.8 0.7 copy-start.5
  9.6 0.7 copy-start.6
  10.3 6.5 %copy-start.1 = (bf16[1,3,384,256]{3,2,1,0:T(8,128)(2,1)S(1)}, bf16[1,3,384,256]{3,2,1,0:T(8,128)(2,1)}, u32[]{:S(2)}) copy-start(bf16[1,3,384,256]{3,2,1,0:T(8,128)(2,1)} %param.18) | copy-start | bytes 1769476
  10.3 6.5 %copy-start.3 = (f32[10,2,3072]{2,1,0:T(2,128)S(1)}, f32[10,2,3072]{2,1,0:T(2,128)}, u32[]{:S(2)}) copy-start(f32[10,2,3072]{2,1,0:T(2,128)} %modulation_ref.1) | copy-start | bytes 737284
  11.1 13.4 %collective-permute-start.4 = (bf16[64,128]{1,0:T(8,128)(2,1)S(1)}, bf16[64,128]{1,0:T(8,128)(2,1)S(1)}, u32[]{:S(2)}, u32[]{:S(2)}) collective-permute-start(bf16[64,128]{1,0:T(8,128)(2,1)S(1)} %get-tuple-element.24), channel_id=1, source_target_pairs={{0,14},{1,15},{2,12},{3,13},{4,10},{5,11},{6,8},{7,9},{8,6},{9,7},... | collective-permute-start | bytes 49160 | tf_op jit(solution)/shard_map/ppermute | solution.py:371
  19.4 16.4 %all-to-all-start.1 = ((bf16[8,400,128]{2,1,0:T(8,128)(2,1)}), bf16[8,400,128]{2,1,0:T(8,128)(2,1)S(1)}, u32[]{:S(2)}, u32[]{:S(2)}) async-start(bf16[8,400,128]{2,1,0:T(8,128)(2,1)} %shard_map.116), calls=%async_computation.1 | async-start | bytes 1638400 | tf_op jit(solution)/shard_map/all_to_all | solution.py:404
  24.5 3.9 %collective-permute-start.5 = (bf16[2,64,128]{2,1,0:T(8,128)(2,1)S(1)}, bf16[2,64,128]{2,1,0:T(8,128)(2,1)S(1)}, u32[]{:S(2)}, u32[]{:S(2)}) collective-permute-start(bf16[2,64,128]{2,1,0:T(8,128)(2,1)S(1)} %pad_maximum_fusion), channel_id=1, source_target_pairs={{0,2},{1,3},{2,0},{3,1},{4,6},{5,7},{6,4},{7,5},{8,10},{9,11},{10,... | collective-permute-start | bytes 98312 | tf_op jit(solution)/shard_map/ppermute | solution.py:371
  26.2 3.8 %collective-permute-start.6 = (bf16[2,64,128]{2,1,0:T(8,128)(2,1)S(1)}, bf16[2,64,128]{2,1,0:T(8,128)(2,1)S(1)}, u32[]{:S(2)}, u32[]{:S(2)}) collective-permute-start(bf16[2,64,128]{2,1,0:T(8,128)(2,1)S(1)} %pad_maximum_fusion), channel_id=1, source_target_pairs={{0,4},{1,5},{2,6},{3,7},{4,0},{5,1},{6,2},{7,3},{8,12},{9,13},{10,... | collective-permute-start | bytes 98312 | tf_op jit(solution)/shard_map/ppermute | solution.py:371
  26.8 4.8 %collective-permute-start.7 = (bf16[2,64,128]{2,1,0:T(8,128)(2,1)S(1)}, bf16[2,64,128]{2,1,0:T(8,128)(2,1)S(1)}, u32[]{:S(2)}, u32[]{:S(2)}) collective-permute-start(bf16[2,64,128]{2,1,0:T(8,128)(2,1)S(1)} %pad_maximum_fusion), channel_id=1, source_target_pairs={{0,6},{1,7},{2,4},{3,5},{4,2},{5,3},{6,0},{7,1},{8,14},{9,15},{10,... | collective-permute-start | bytes 98312 | tf_op jit(solution)/shard_map/ppermute | solution.py:371
  31.6 3.9 %collective-permute-start.8 = (bf16[8,64,128]{2,1,0:T(8,128)(2,1)S(1)}, bf16[8,64,128]{2,1,0:T(8,128)(2,1)S(1)}, u32[]{:S(2)}, u32[]{:S(2)}) collective-permute-start(bf16[8,64,128]{2,1,0:T(8,128)(2,1)S(1)} %constant_dynamic-update-slice_fusion.4.near_ref), channel_id=1, source_target_pairs={{0,1},{1,0},{2,3},{3,2},{4,5},{5,4},{6,7},{7,6},{8,9},{9,8},{10,11... | collective-permute-start | bytes 393224 | tf_op jit(solution)/shard_map/ppermute | solution.py:371
  35.6 0.8 copy-start
  37.2 3.6 %collective-permute-start = (bf16[1,144,128]{2,1,0:T(8,128)(2,1)S(1)}, bf16[1,144,128]{2,1,0:T(8,128)(2,1)S(1)}, u32[]{:S(2)}, u32[]{:S(2)}) collective-permute-start(bf16[1,144,128]{2,1,0:T(8,128)(2,1)S(1)} %get-tuple-element.23), channel_id=1, source_target_pairs={{0,2},{1,3},{2,0},{3,1},{4,6},{5,7},{6,4},{7,5},{8,10},{9,11},{10,... | collective-permute-start | bytes 110600 | tf_op jit(solution)/shard_map/ppermute | solution.py:371
  37.3 3.8 %collective-permute-start.1 = (bf16[1,144,128]{2,1,0:T(8,128)(2,1)S(1)}, bf16[1,144,128]{2,1,0:T(8,128)(2,1)S(1)}, u32[]{:S(2)}, u32[]{:S(2)}) collective-permute-start(bf16[1,144,128]{2,1,0:T(8,128)(2,1)S(1)} %get-tuple-element.23), channel_id=1, source_target_pairs={{0,4},{1,5},{2,6},{3,7},{4,0},{5,1},{6,2},{7,3},{8,12},{9,13},{10,... | collective-permute-start | bytes 110600 | tf_op jit(solution)/shard_map/ppermute | solution.py:371
  39.2 5.0 %collective-permute-start.2 = (bf16[1,144,128]{2,1,0:T(8,128)(2,1)S(1)}, bf16[1,144,128]{2,1,0:T(8,128)(2,1)S(1)}, u32[]{:S(2)}, u32[]{:S(2)}) collective-permute-start(bf16[1,144,128]{2,1,0:T(8,128)(2,1)S(1)} %get-tuple-element.23), channel_id=1, source_target_pairs={{0,6},{1,7},{2,4},{3,5},{4,2},{5,3},{6,0},{7,1},{8,14},{9,15},{10,... | collective-permute-start | bytes 110600 | tf_op jit(solution)/shard_map/ppermute | solution.py:371
  44.2 6.0 %collective-permute-start.3 = (bf16[4,144,128]{2,1,0:T(8,128)(2,1)S(1)}, bf16[4,144,128]{2,1,0:T(8,128)(2,1)S(1)}, u32[]{:S(2)}, u32[]{:S(2)}) collective-permute-start(bf16[4,144,128]{2,1,0:T(8,128)(2,1)S(1)} %constant_dynamic-update-slice_fusion.pack_ref), channel_id=1, source_target_pairs={{0,14},{1,15},{2,12},{3,13},{4,10},{5,11},{6,8},{7,9},{8,6},{9,7},... | collective-permute-start | bytes 442376 | tf_op jit(solution)/shard_map/ppermute | solution.py:371
  55.0 6.2 %collective-permute-start.9 = (f32[64,384]{1,0:T(8,128)S(1)}, f32[64,384]{1,0:T(8,128)S(1)}, u32[]{:S(2)}, u32[]{:S(2)}) collective-permute-start(f32[64,384]{1,0:T(8,128)S(1)} %constant_dynamic-update-slice_fusion.9.mine_ref), channel_id=1, source_target_pairs={{0,1},{1,0},{2,3},{3,2},{4,5},{5,4},{6,7},{7,6},{8,9},{9,8},{10,11... | collective-permute-start | bytes 294920 | tf_op jit(solution)/shard_map/ppermute | solution.py:371
  62.2 12.5 %all-to-all-start.2 = ((bf16[8,80,128]{2,1,0:T(8,128)(2,1)}), bf16[8,80,128]{2,1,0:T(8,128)(2,1)S(1)}, u32[]{:S(2)}, u32[]{:S(2)}) async-start(bf16[8,80,128]{2,1,0:T(8,128)(2,1)} %get-tuple-element.34), calls=%async_computation.2 | async-start | bytes 327680 | tf_op jit(solution)/shard_map/all_to_all | solution.py:446
  85.9 13.2 %all-to-all-start.4 = ((f32[16,1,128]{2,1,0:T(1,128)}), f32[16,1,128]{2,1,0:T(1,128)S(1)}, u32[]{:S(2)}, u32[]{:S(2)}) async-start(f32[16,1,128]{2,1,0:T(1,128)} %get-tuple-element.38), calls=%async_computation.4 | async-start | bytes 16384 | tf_op jit(solution)/shard_map/all_to_all | solution.py:458
  99.2 4.4 %collective-permute-start.10 = (bf16[64,256]{1,0:T(8,128)(2,1)S(1)}, bf16[64,256]{1,0:T(8,128)(2,1)S(1)}, u32[]{:S(2)}, u32[]{:S(2)}) collective-permute-start(bf16[64,256]{1,0:T(8,128)(2,1)S(1)} %shard_map.124.mine_ref), channel_id=1, source_target_pairs={{0,128},{128,0},{1,129},{129,1},{2,130},{130,2},{3,131},{131,3},{4... | collective-permute-start | bytes 98312 | tf_op jit(solution)/shard_map/ppermute | solution.py:465

commit v4 on v3

--- a/solution.py
+++ b/solution.py
@@ -388,7 +388,6 @@
 
     near = jnp.stack([near, across(near, "seq", 14)])
     near = jnp.concatenate([near] + [across(near, "seq", bits) for bits in (2, 4, 6)], axis=0)
-    far = across(near, "seq", 1)
     sums = call(
         partial_kernel,
         shape(steps_count, 6 * channels + 16, LANES, dtype=bf16),
@@ -402,6 +401,8 @@
     )(steps, sums)
 
     sums = lax.all_to_all(sums, "dp", 0, 0)
+    sums, near = lax.optimization_barrier((sums, near))
+    far = across(near, "seq", 1)
     pack, values, offsets = call(
         functools.partial(absorb_kernel, factor=width**-0.5, logit=math.log2(math.e) / HD**0.5),
         [shape(1, 2 * channels + 16, LANES, dtype=bf16), shape(2 * channels, HD), shape(8, HD)],
@@ -449,13 +450,13 @@
         shape(rollouts, channels, columns, dtype=bf16),
         [VMEM, VMEM, VMEM, SMEM, SMEM],
     )(pieces, values, offsets, advantage, old_logp)
-    parts = lax.all_to_all(parts, "dp", 0, 0)
+    parts = lax.all_to_all(parts, "dp", 0, 0, axis_index_groups=[list(reversed(range(rollouts)))])
     gradient, squares = call(
         total_kernel,
         [shape(channels, columns), shape(blocks, 1, LANES)],
         [VMEM],
     )(parts)
-    squares = lax.all_to_all(squares, "seq", 0, 0)
+    squares = lax.all_to_all(squares, "seq", 0, 0, axis_index_groups=[[(i + blocks // 2) % blocks for i in range(blocks)]])
     role = lax.axis_index("role").reshape(1)
     mine = call(
         functools.partial(update_kernel, entries=columns * blocks * channels),

time: 105 us -> 102 us (0.971)
  waiting for transfers between devices: 26 us -> 19.7 us
  starting transfers between devices: 44.8 us -> 50.2 us
    all_to_all x1, waiting for transfers between devices: 6.98 us -> 1.96 us  [on_device(): lax.all_to_all(squares, 'seq', 0, 0, axis_index_groups=[[(i + blocks // 2...]
    ppermute x10, waiting for transfers between devices: 9.4 us -> 5.84 us  [across(): lax.ppermute(value, axis, [(i, i ^ bits) for i in range(lax.axis_size(axi...]
    all_to_all x1, starting transfers between devices: 6.26 us -> 9.7 us  [on_device(): lax.all_to_all(squares, 'seq', 0, 0, axis_index_groups=[[(i + blocks // 2...]
    all_to_all x1, waiting for transfers between devices: 0.01 us -> 2.31 us  [on_device(): sums = lax.all_to_all(sums, 'dp', 0, 0)]
    ppermute x10, starting transfers between devices: 21.6 us -> 23.4 us  [across(): lax.ppermute(value, axis, [(i, i ^ bits) for i in range(lax.axis_size(axi...]
  transfers between devices with their start and end apart: 15 -> 15, of which waited for: 10 -> 9; matrix products, arithmetic and copies ran while one was open for 0% -> 0% of each run, Pallas kernels for 8% -> 8%
where the time goes in v4:
time: 102 us
  starting transfers between devices  50.2 us (49%)
  waiting for transfers between devices  19.7 us (19%)
  Pallas kernels  16.8 us (16%)
  blocking collectives  9.37 us (9%)
  local copies, waits for them, and re-layouts  2.77 us (3%)
  between operations  2.77 us (3%)
    ppermute x10, starting transfers between devices, across(): lax.ppermute(value, axis, [(i, i ^ bits) for i in range(lax.axis_size(axi...  23.4 us
    all_to_all x1, starting transfers between devices, on_device(): lax.all_to_all(squares, 'seq', 0, 0, axis_index_groups=[[(i + blocks // 2...  9.7 us
    all_to_all x1, blocking collectives, on_device(): lax.all_to_all(parts, 'dp', 0, 0, axis_index_groups=[list(reversed(range(...  9.37 us
    pallas_call x2, Pallas kernels, attend(): call(attend_kernel, [shape(channels, wide), shape(2 * count, channels, wi...  9.36 us
    all_to_all x1, waiting for transfers between devices, on_device(): pieces = lax.all_to_all(pieces, 'seq', 0, 0, axis_index_groups=along)  7.79 us
    all_to_all x1, starting transfers between devices, on_device(): steps = lax.all_to_all(steps, 'dp', 0, 0)[:, 0, 0]  5.95 us
    ppermute x10, waiting for transfers between devices, across(): lax.ppermute(value, axis, [(i, i ^ bits) for i in range(lax.axis_size(axi...  5.84 us
    all_to_all x1, starting transfers between devices, on_device(): sums = lax.all_to_all(sums, 'dp', 0, 0)  5.14 us
  transfers between devices with their start and end apart: 15, of which 9 were waited for; matrix products, arithmetic and copies ran while one was open for 0% of the time, Pallas kernels for 8%

profile of v4, /device:TPU:1, one launch (start us, length us, event | category | flops | bytes accessed | tf_op | source)
XLA Modules:
  0.0 101.6 jit_solution(9349401658381911048)
XLA Ops:
  0.6 0.0 copy-start.4
  1.3 0.6 shard_map.113
  1.9 5.9 %all-to-all-start = ((s32[8,1,128]{2,1,0:T(1,128)}), s32[8,1,128]{2,1,0:T(1,128)S(1)}, u32[]{:S(2)}, u32[]{:S(2)}) async-start(s32[8,1,128]{2,1,0:T(1,128)} %shard_map.113), calls=%async_computation | async-start | bytes 8192 | tf_op jit(solution)/shard_map/all_to_all | solution.py:374
  7.8 0.0 copy-done.4
  7.8 0.0 copy-start.2
  7.9 1.0 copy-done.2
  8.8 0.0 copy-start.5
  8.8 0.7 copy-done.5
  9.6 0.0 copy-start.6
  9.6 0.7 copy-done.6
  10.3 0.0 copy-start.1
  10.3 0.0 copy-start.3
  10.3 0.8 shard_map.114
  11.1 5.6 %collective-permute-start = (bf16[64,128]{1,0:T(8,128)(2,1)S(1)}, bf16[64,128]{1,0:T(8,128)(2,1)S(1)}, u32[]{:S(2)}, u32[]{:S(2)}) collective-permute-start(bf16[64,128]{1,0:T(8,128)(2,1)S(1)} %get-tuple-element.25), channel_id=1, source_target_pairs={{0,14},{1,15},{2,12},{3,13},{4,10},{5,11},{6,8},{7,9},{8,6},{9,7},... | collective-permute-start | bytes 49160 | tf_op jit(solution)/shard_map/ppermute | solution.py:371
  16.8 0.0 copy-done.1
  16.8 0.0 copy-done.3
  16.8 0.8 shard_map.115.sums_ref
  17.6 0.0 all-to-all-done
  17.6 0.2 slice_reduce_fusion.steps_ref
  17.8 1.5 %shard_map.116 = bf16[8,400,128]{2,1,0:T(8,128)(2,1)} custom-call(s32[8]{0:T(128)S(1)} %slice_reduce_fusion.steps_ref, bf16[10,400,128]{2,1,0:T(8,128)(2,1)S(1)} %shard_map.115.sums_ref), custom_call_target="tpu_custom_call" | custom-call | tf_op jit(solution)/shard_map/pallas_call | solution.py:399
  19.3 5.1 %all-to-all-start.1 = ((bf16[8,400,128]{2,1,0:T(8,128)(2,1)}), bf16[8,400,128]{2,1,0:T(8,128)(2,1)S(1)}, u32[]{:S(2)}, u32[]{:S(2)}) async-start(bf16[8,400,128]{2,1,0:T(8,128)(2,1)} %shard_map.116), calls=%async_computation.1 | async-start | bytes 1638400 | tf_op jit(solution)/shard_map/all_to_all | solution.py:403
  24.5 0.0 collective-permute-done
  24.5 1.7 %collective-permute-start.1 = (bf16[2,64,128]{2,1,0:T(8,128)(2,1)S(1)}, bf16[2,64,128]{2,1,0:T(8,128)(2,1)S(1)}, u32[]{:S(2)}, u32[]{:S(2)}) collective-permute-start(bf16[2,64,128]{2,1,0:T(8,128)(2,1)S(1)} %pad_maximum_fusion), channel_id=1, source_target_pairs={{0,2},{1,3},{2,0},{3,1},{4,6},{5,7},{6,4},{7,5},{8,10},{9,11},{10,... | collective-permute-start | bytes 98312 | tf_op jit(solution)/shard_map/ppermute | solution.py:371
  26.2 0.5 collective-permute-start.2
  26.8 1.6 %collective-permute-start.3 = (bf16[2,64,128]{2,1,0:T(8,128)(2,1)S(1)}, bf16[2,64,128]{2,1,0:T(8,128)(2,1)S(1)}, u32[]{:S(2)}, u32[]{:S(2)}) collective-permute-start(bf16[2,64,128]{2,1,0:T(8,128)(2,1)S(1)} %pad_maximum_fusion), channel_id=1, source_target_pairs={{0,6},{1,7},{2,4},{3,5},{4,2},{5,3},{6,0},{7,1},{8,14},{9,15},{10,... | collective-permute-start | bytes 98312 | tf_op jit(solution)/shard_map/ppermute | solution.py:371
  28.4 0.0 collective-permute-done.1
  28.4 1.6 %collective-permute-done.2 = bf16[2,64,128]{2,1,0:T(8,128)(2,1)S(1)} collective-permute-done((bf16[2,64,128]{2,1,0:T(8,128)(2,1)S(1)}, bf16[2,64,128]{2,1,0:T(8,128)(2,1)S(1)}, u32[]{:S(2)}, u32[]{:S(2)}) %collective-permute-start.2) | collective-permute-done | bytes 32800 | tf_op jit(solution)/shard_map/ppermute | solution.py:371
  30.1 0.0 copy-start
  30.1 1.5 %collective-permute-done.3 = bf16[2,64,128]{2,1,0:T(8,128)(2,1)S(1)} collective-permute-done((bf16[2,64,128]{2,1,0:T(8,128)(2,1)S(1)}, bf16[2,64,128]{2,1,0:T(8,128)(2,1)S(1)}, u32[]{:S(2)}, u32[]{:S(2)}) %collective-permute-start.3) | collective-permute-done | bytes 32800 | tf_op jit(solution)/shard_map/ppermute | solution.py:371
  31.6 2.3 %all-to-all-done.1.sums_ref = bf16[8,400,128]{2,1,0:T(8,128)(2,1)S(1)} async-done(((bf16[8,400,128]{2,1,0:T(8,128)(2,1)}), bf16[8,400,128]{2,1,0:T(8,128)(2,1)S(1)}, u32[]{:S(2)}, u32[]{:S(2)}) %all-to-all-start.1) | async-done | bytes 819232 | tf_op jit(solution)/shard_map/all_to_all | solution.py:403
  33.9 0.0 copy-done
  33.9 0.9 shard_map.117
  34.8 1.7 %collective-permute-start.4 = (bf16[1,144,128]{2,1,0:T(8,128)(2,1)S(1)}, bf16[1,144,128]{2,1,0:T(8,128)(2,1)S(1)}, u32[]{:S(2)}, u32[]{:S(2)}) collective-permute-start(bf16[1,144,128]{2,1,0:T(8,128)(2,1)S(1)} %get-tuple-element.27), channel_id=1, source_target_pairs={{0,2},{1,3},{2,0},{3,1},{4,6},{5,7},{6,4},{7,5},{8,10},{9,11},{10,... | collective-permute-start | bytes 110600 | tf_op jit(solution)/shard_map/ppermute | solution.py:371
  36.5 0.5 collective-permute-start.5
  37.1 1.6 %collective-permute-start.6 = (bf16[1,144,128]{2,1,0:T(8,128)(2,1)S(1)}, bf16[1,144,128]{2,1,0:T(8,128)(2,1)S(1)}, u32[]{:S(2)}, u32[]{:S(2)}) collective-permute-start(bf16[1,144,128]{2,1,0:T(8,128)(2,1)S(1)} %get-tuple-element.27), channel_id=1, source_target_pairs={{0,6},{1,7},{2,4},{3,5},{4,2},{5,3},{6,0},{7,1},{8,14},{9,15},{10,... | collective-permute-start | bytes 110600 | tf_op jit(solution)/shard_map/ppermute | solution.py:371
  38.7 4.5 %collective-permute-start.8 = (bf16[8,64,128]{2,1,0:T(8,128)(2,1)S(1)}, bf16[8,64,128]{2,1,0:T(8,128)(2,1)S(1)}, u32[]{:S(2)}, u32[]{:S(2)}) collective-permute-start(bf16[8,64,128]{2,1,0:T(8,128)(2,1)S(1)} %constant_dynamic-update-slice_fusion.near_ref), channel_id=1, source_target_pairs={{0,1},{1,0},{2,3},{3,2},{4,5},{5,4},{6,7},{7,6},{8,9},{9,8},{10,11... | collective-permute-start | bytes 393224 | tf_op jit(solution)/shard_map/ppermute | solution.py:371
  43.2 0.0 collective-permute-done.4
  43.2 0.0 collective-permute-done.5
  43.2 0.0 collective-permute-done.6
  43.3 0.4 collective-permute-start.7
  43.7 0.5 collective-permute-done.8.far_ref
  44.2 0.2 shard_map.118
  44.4 4.7 %shard_map.119 = (f32[64,256]{1,0:T(8,128)S(1)}, bf16[8,64,256]{2,1,0:T(8,128)(2,1)S(1)}) custom-call(bf16[4,144,128]{2,1,0:T(8,128)(2,1)S(1)} %constant_dynamic-update-slice_fusion.5.pack_ref, bf16[2048,128]{1,0:T(8,128)(2,1)S(1)} %get-tuple-element.29.keys_ref, bf16[80,2048]{1,0:T(8,128)(2,1)S(1)} %get-tuple-element.30.values_ref, ...), custom_call_target="tpu_custom_call" | custom-call | flops 4000000000 | tf_op jit(solution)/shard_map/pallas_call | solution.py:425
  49.1 1.2 %collective-permute-done.7.pack_ref = bf16[4,144,128]{2,1,0:T(8,128)(2,1)S(1)} collective-permute-done((bf16[4,144,128]{2,1,0:T(8,128)(2,1)S(1)}, bf16[4,144,128]{2,1,0:T(8,128)(2,1)S(1)}, u32[]{:S(2)}, u32[]{:S(2)}) %collective-permute-start.7) | collective-permute-done | bytes 147488 | tf_op jit(solution)/shard_map/ppermute | solution.py:371
  50.3 4.7 %shard_map.120 = (f32[64,256]{1,0:T(8,128)S(1)}, bf16[8,64,256]{2,1,0:T(8,128)(2,1)S(1)}) custom-call(bf16[4,144,128]{2,1,0:T(8,128)(2,1)S(1)} %collective-permute-done.7.pack_ref, bf16[2048,128]{1,0:T(8,128)(2,1)S(1)} %get-tuple-element.29.keys_ref, bf16[80,2048]{1,0:T(8,128)(2,1)S(1)} %get-tuple-element.30.values_ref, ...), custom_call_target="tpu_custom_call" | custom-call | flops 4000000000 | tf_op jit(solution)/shard_map/pallas_call | solution.py:425
  55.0 5.1 %collective-permute-start.9 = (f32[64,384]{1,0:T(8,128)S(1)}, f32[64,384]{1,0:T(8,128)S(1)}, u32[]{:S(2)}, u32[]{:S(2)}) collective-permute-start(f32[64,384]{1,0:T(8,128)S(1)} %constant_dynamic-update-slice_fusion.9.mine_ref), channel_id=1, source_target_pairs={{0,1},{1,0},{2,3},{3,2},{4,5},{5,4},{6,7},{7,6},{8,9},{9,8},{10,11... | collective-permute-start | bytes 294920 | tf_op jit(solution)/shard_map/ppermute | solution.py:371
  60.1 0.9 collective-permute-done.9.other_ref
  61.1 1.0 shard_map.121
  62.1 3.4 %all-to-all-start.2 = ((bf16[8,80,128]{2,1,0:T(8,128)(2,1)}), bf16[8,80,128]{2,1,0:T(8,128)(2,1)S(1)}, u32[]{:S(2)}, u32[]{:S(2)}) async-start(bf16[8,80,128]{2,1,0:T(8,128)(2,1)} %get-tuple-element.38), calls=%async_computation.2 | async-start | bytes 327680 | tf_op jit(solution)/shard_map/all_to_all | solution.py:447
  66.7 7.8 %all-to-all-done.2.pieces_ref = bf16[8,80,128]{2,1,0:T(8,128)(2,1)S(1)} async-done(((bf16[8,80,128]{2,1,0:T(8,128)(2,1)}), bf16[8,80,128]{2,1,0:T(8,128)(2,1)S(1)}, u32[]{:S(2)}, u32[]{:S(2)}) %all-to-all-start.2) | async-done | bytes 163872 | tf_op jit(solution)/shard_map/all_to_all | solution.py:447
  74.5 0.2 shard_map.122
  74.8 9.4 %all_to_all.25.parts_ref = bf16[8,64,256]{2,1,0:T(8,128)(2,1)S(1)} all-to-all(bf16[8,64,256]{2,1,0:T(8,128)(2,1)S(1)} %shard_map.122), channel_id=1, replica_groups={{112,96,80,64,48,32,16,0},{113,97,81,65,49,33,17,1},{114,98,82,66,50,34..., dimensions={0} | all-to-all | bytes 524288 | tf_op jit(solution)/shard_map/all_to_all | solution.py:453
  84.1 0.7 shard_map.123
  84.8 9.7 %all-to-all-start.4 = ((f32[16,1,128]{2,1,0:T(1,128)}), f32[16,1,128]{2,1,0:T(1,128)S(1)}, u32[]{:S(2)}, u32[]{:S(2)}) async-start(f32[16,1,128]{2,1,0:T(1,128)} %get-tuple-element.42), calls=%async_computation.4 | async-start | bytes 16384 | tf_op jit(solution)/shard_map/all_to_all | solution.py:459
  94.5 2.0 %all-to-all-done.4.squares_ref = f32[16,1,128]{2,1,0:T(1,128)S(1)} async-done(((f32[16,1,128]{2,1,0:T(1,128)}), f32[16,1,128]{2,1,0:T(1,128)S(1)}, u32[]{:S(2)}, u32[]{:S(2)}) %all-to-all-start.4) | async-done | bytes 8224 | tf_op jit(solution)/shard_map/all_to_all | solution.py:459
  96.5 0.1 shard_map.124.mine_ref
  96.6 2.5 %collective-permute-start.10 = (bf16[64,256]{1,0:T(8,128)(2,1)S(1)}, bf16[64,256]{1,0:T(8,128)(2,1)S(1)}, u32[]{:S(2)}, u32[]{:S(2)}) collective-permute-start(bf16[64,256]{1,0:T(8,128)(2,1)S(1)} %shard_map.124.mine_ref), channel_id=1, source_target_pairs={{0,128},{128,0},{1,129},{129,1},{2,130},{130,2},{3,131},{131,3},{4... | collective-permute-start | bytes 98312 | tf_op jit(solution)/shard_map/ppermute | solution.py:466
  99.1 1.8 %collective-permute-done.10.other_ref = bf16[64,256]{1,0:T(8,128)(2,1)S(1)} collective-permute-done((bf16[64,256]{1,0:T(8,128)(2,1)S(1)}, bf16[64,256]{1,0:T(8,128)(2,1)S(1)}, u32[]{:S(2)}, u32[]{:S(2)}) %collective-permute-start.10) | collective-permute-done | bytes 32800 | tf_op jit(solution)/shard_map/ppermute | solution.py:466
  100.9 0.6 shard_map.125
  (13 shorter events, 0.1 us)
Async XLA Ops:
  0.6 7.2 %copy-start.4 = (bf16[1,1,128,64]{2,3,1,0:T(8,128)(2,1)S(1)}, bf16[1,1,128,64]{2,3,1,0:T(8,128)(2,1)}, u32[]{:S(2)}) copy-start(bf16[1,1,128,64]{2,3,1,0:T(8,128)(2,1)} %param.10) | copy-start | bytes 49156
  1.9 15.7 %all-to-all-start = ((s32[8,1,128]{2,1,0:T(1,128)}), s32[8,1,128]{2,1,0:T(1,128)S(1)}, u32[]{:S(2)}, u32[]{:S(2)}) async-start(s32[8,1,128]{2,1,0:T(1,128)} %shard_map.113), calls=%async_computation | async-start | bytes 8192 | tf_op jit(solution)/shard_map/all_to_all | solution.py:374
  7.8 1.0 copy-start.2
  8.8 0.7 copy-start.5
  9.6 0.7 copy-start.6
  10.3 6.5 %copy-start.1 = (bf16[1,3,384,256]{3,2,1,0:T(8,128)(2,1)S(1)}, bf16[1,3,384,256]{3,2,1,0:T(8,128)(2,1)}, u32[]{:S(2)}) copy-start(bf16[1,3,384,256]{3,2,1,0:T(8,128)(2,1)} %param.18) | copy-start | bytes 1769476
  10.3 6.5 %copy-start.3 = (f32[10,2,3072]{2,1,0:T(2,128)S(1)}, f32[10,2,3072]{2,1,0:T(2,128)}, u32[]{:S(2)}) copy-start(f32[10,2,3072]{2,1,0:T(2,128)} %modulation_ref.1) | copy-start | bytes 737284
  11.1 13.4 %collective-permute-start = (bf16[64,128]{1,0:T(8,128)(2,1)S(1)}, bf16[64,128]{1,0:T(8,128)(2,1)S(1)}, u32[]{:S(2)}, u32[]{:S(2)}) collective-permute-start(bf16[64,128]{1,0:T(8,128)(2,1)S(1)} %get-tuple-element.25), channel_id=1, source_target_pairs={{0,14},{1,15},{2,12},{3,13},{4,10},{5,11},{6,8},{7,9},{8,6},{9,7},... | collective-permute-start | bytes 49160 | tf_op jit(solution)/shard_map/ppermute | solution.py:371
  19.3 14.6 %all-to-all-start.1 = ((bf16[8,400,128]{2,1,0:T(8,128)(2,1)}), bf16[8,400,128]{2,1,0:T(8,128)(2,1)S(1)}, u32[]{:S(2)}, u32[]{:S(2)}) async-start(bf16[8,400,128]{2,1,0:T(8,128)(2,1)} %shard_map.116), calls=%async_computation.1 | async-start | bytes 1638400 | tf_op jit(solution)/shard_map/all_to_all | solution.py:403
  24.5 3.9 %collective-permute-start.1 = (bf16[2,64,128]{2,1,0:T(8,128)(2,1)S(1)}, bf16[2,64,128]{2,1,0:T(8,128)(2,1)S(1)}, u32[]{:S(2)}, u32[]{:S(2)}) collective-permute-start(bf16[2,64,128]{2,1,0:T(8,128)(2,1)S(1)} %pad_maximum_fusion), channel_id=1, source_target_pairs={{0,2},{1,3},{2,0},{3,1},{4,6},{5,7},{6,4},{7,5},{8,10},{9,11},{10,... | collective-permute-start | bytes 98312 | tf_op jit(solution)/shard_map/ppermute | solution.py:371
  26.2 3.8 %collective-permute-start.2 = (bf16[2,64,128]{2,1,0:T(8,128)(2,1)S(1)}, bf16[2,64,128]{2,1,0:T(8,128)(2,1)S(1)}, u32[]{:S(2)}, u32[]{:S(2)}) collective-permute-start(bf16[2,64,128]{2,1,0:T(8,128)(2,1)S(1)} %pad_maximum_fusion), channel_id=1, source_target_pairs={{0,4},{1,5},{2,6},{3,7},{4,0},{5,1},{6,2},{7,3},{8,12},{9,13},{10,... | collective-permute-start | bytes 98312 | tf_op jit(solution)/shard_map/ppermute | solution.py:371
  26.8 4.8 %collective-permute-start.3 = (bf16[2,64,128]{2,1,0:T(8,128)(2,1)S(1)}, bf16[2,64,128]{2,1,0:T(8,128)(2,1)S(1)}, u32[]{:S(2)}, u32[]{:S(2)}) collective-permute-start(bf16[2,64,128]{2,1,0:T(8,128)(2,1)S(1)} %pad_maximum_fusion), channel_id=1, source_target_pairs={{0,6},{1,7},{2,4},{3,5},{4,2},{5,3},{6,0},{7,1},{8,14},{9,15},{10,... | collective-permute-start | bytes 98312 | tf_op jit(solution)/shard_map/ppermute | solution.py:371
  30.1 3.9 %copy-start = (bf16[1,256,64]{1,2,0:T(8,128)(2,1)S(1)}, bf16[1,256,64]{1,2,0:T(8,128)(2,1)}, u32[]{:S(2)}) copy-start(bf16[1,256,64]{1,2,0:T(8,128)(2,1)} %param.19) | copy-start | bytes 98308
  34.8 8.4 %collective-permute-start.4 = (bf16[1,144,128]{2,1,0:T(8,128)(2,1)S(1)}, bf16[1,144,128]{2,1,0:T(8,128)(2,1)S(1)}, u32[]{:S(2)}, u32[]{:S(2)}) collective-permute-start(bf16[1,144,128]{2,1,0:T(8,128)(2,1)S(1)} %get-tuple-element.27), channel_id=1, source_target_pairs={{0,2},{1,3},{2,0},{3,1},{4,6},{5,7},{6,4},{7,5},{8,10},{9,11},{10,... | collective-permute-start | bytes 110600 | tf_op jit(solution)/shard_map/ppermute | solution.py:371
  36.5 6.7 %collective-permute-start.5 = (bf16[1,144,128]{2,1,0:T(8,128)(2,1)S(1)}, bf16[1,144,128]{2,1,0:T(8,128)(2,1)S(1)}, u32[]{:S(2)}, u32[]{:S(2)}) collective-permute-start(bf16[1,144,128]{2,1,0:T(8,128)(2,1)S(1)} %get-tuple-element.27), channel_id=1, source_target_pairs={{0,4},{1,5},{2,6},{3,7},{4,0},{5,1},{6,2},{7,3},{8,12},{9,13},{10,... | collective-permute-start | bytes 110600 | tf_op jit(solution)/shard_map/ppermute | solution.py:371
  37.1 6.2 %collective-permute-start.6 = (bf16[1,144,128]{2,1,0:T(8,128)(2,1)S(1)}, bf16[1,144,128]{2,1,0:T(8,128)(2,1)S(1)}, u32[]{:S(2)}, u32[]{:S(2)}) collective-permute-start(bf16[1,144,128]{2,1,0:T(8,128)(2,1)S(1)} %get-tuple-element.27), channel_id=1, source_target_pairs={{0,6},{1,7},{2,4},{3,5},{4,2},{5,3},{6,0},{7,1},{8,14},{9,15},{10,... | collective-permute-start | bytes 110600 | tf_op jit(solution)/shard_map/ppermute | solution.py:371
  38.7 5.5 %collective-permute-start.8 = (bf16[8,64,128]{2,1,0:T(8,128)(2,1)S(1)}, bf16[8,64,128]{2,1,0:T(8,128)(2,1)S(1)}, u32[]{:S(2)}, u32[]{:S(2)}) collective-permute-start(bf16[8,64,128]{2,1,0:T(8,128)(2,1)S(1)} %constant_dynamic-update-slice_fusion.near_ref), channel_id=1, source_target_pairs={{0,1},{1,0},{2,3},{3,2},{4,5},{5,4},{6,7},{7,6},{8,9},{9,8},{10,11... | collective-permute-start | bytes 393224 | tf_op jit(solution)/shard_map/ppermute | solution.py:371
  43.3 7.1 %collective-permute-start.7 = (bf16[4,144,128]{2,1,0:T(8,128)(2,1)S(1)}, bf16[4,144,128]{2,1,0:T(8,128)(2,1)S(1)}, u32[]{:S(2)}, u32[]{:S(2)}) collective-permute-start(bf16[4,144,128]{2,1,0:T(8,128)(2,1)S(1)} %constant_dynamic-update-slice_fusion.5.pack_ref), channel_id=1, source_target_pairs={{0,14},{1,15},{2,12},{3,13},{4,10},{5,11},{6,8},{7,9},{8,6},{9,7},... | collective-permute-start | bytes 442376 | tf_op jit(solution)/shard_map/ppermute | solution.py:371
  55.0 6.1 %collective-permute-start.9 = (f32[64,384]{1,0:T(8,128)S(1)}, f32[64,384]{1,0:T(8,128)S(1)}, u32[]{:S(2)}, u32[]{:S(2)}) collective-permute-start(f32[64,384]{1,0:T(8,128)S(1)} %constant_dynamic-update-slice_fusion.9.mine_ref), channel_id=1, source_target_pairs={{0,1},{1,0},{2,3},{3,2},{4,5},{5,4},{6,7},{7,6},{8,9},{9,8},{10,11... | collective-permute-start | bytes 294920 | tf_op jit(solution)/shard_map/ppermute | solution.py:371
  62.1 12.5 %all-to-all-start.2 = ((bf16[8,80,128]{2,1,0:T(8,128)(2,1)}), bf16[8,80,128]{2,1,0:T(8,128)(2,1)S(1)}, u32[]{:S(2)}, u32[]{:S(2)}) async-start(bf16[8,80,128]{2,1,0:T(8,128)(2,1)} %get-tuple-element.38), calls=%async_computation.2 | async-start | bytes 327680 | tf_op jit(solution)/shard_map/all_to_all | solution.py:447
  84.8 11.7 %all-to-all-start.4 = ((f32[16,1,128]{2,1,0:T(1,128)}), f32[16,1,128]{2,1,0:T(1,128)S(1)}, u32[]{:S(2)}, u32[]{:S(2)}) async-start(f32[16,1,128]{2,1,0:T(1,128)} %get-tuple-element.42), calls=%async_computation.4 | async-start | bytes 16384 | tf_op jit(solution)/shard_map/all_to_all | solution.py:459
  96.6 4.4 %collective-permute-start.10 = (bf16[64,256]{1,0:T(8,128)(2,1)S(1)}, bf16[64,256]{1,0:T(8,128)(2,1)S(1)}, u32[]{:S(2)}, u32[]{:S(2)}) collective-permute-start(bf16[64,256]{1,0:T(8,128)(2,1)S(1)} %shard_map.124.mine_ref), channel_id=1, source_target_pairs={{0,128},{128,0},{1,129},{129,1},{2,130},{130,2},{3,131},{131,3},{4... | collective-permute-start | bytes 98312 | tf_op jit(solution)/shard_map/ppermute | solution.py:466

commit v5 on v4

--- a/solution.py
+++ b/solution.py
@@ -270,7 +270,7 @@
     for part, bits in ((attended_ref, 0), (attended_far_ref, 2 * half - 1)):
         product = dot_nt(residual, part[...].reshape(2 * half * channels, wide)).astype(bf16)
         for s in range(half):
-            place = chip_ref[0] ^ (s ^ bits)
+            place = chip_ref[0] ^ (s ^ bits ^ (2 * half - 1))
             pieces_ref[place, 0:channels, :] = product[:, s * LANES : (s + 1) * LANES]
             pieces_ref[place, channels : channels + 16, :] = tail
 
@@ -359,7 +359,7 @@
     chip = (lax.axis_index("seq") // CORES).reshape(1)
     rollouts, blocks = lax.axis_size("dp"), lax.axis_size("seq")
     chips = blocks // CORES
-    along = [[CORES * z + c for z in range(chips)] for c in range(CORES)]
+    along = [[CORES * (z ^ (chips - 1)) + c for z in range(chips)] for c in range(CORES)]
     latent = latents[0, 0].T
     channels, tokens = latent.shape
     steps_count, _, width = modulation.shape

time: 102 us -> 102 us (level)
  waiting for transfers between devices: 19.7 us -> 15.8 us
  starting transfers between devices: 50.2 us -> 53.5 us
    all_to_all x1, waiting for transfers between devices: 7.79 us -> 3.89 us  [on_device(): pieces = lax.all_to_all(pieces, 'seq', 0, 0, axis_index_groups=along)]
    all_to_all x1, starting transfers between devices: 3.38 us -> 5.32 us  [on_device(): pieces = lax.all_to_all(pieces, 'seq', 0, 0, axis_index_groups=along)]
    all_to_all x1, starting transfers between devices: 9.7 us -> 11.1 us  [on_device(): lax.all_to_all(squares, 'seq', 0, 0, axis_index_groups=[[(i + blocks // 2...]
where the time goes in v5:
time: 102 us; the launch traced here: 101 us
  starting transfers between devices  53.5 us (52%)
  Pallas kernels  16.8 us (16%)
  waiting for transfers between devices  15.8 us (15%)
  blocking collectives  9.54 us (9%)
  local copies, waits for them, and re-layouts  2.77 us (3%)
  between operations  2.77 us (3%)
    ppermute x10, starting transfers between devices, across(): lax.ppermute(value, axis, [(i, i ^ bits) for i in range(lax.axis_size(axi...  23.4 us
    all_to_all x1, starting transfers between devices, on_device(): lax.all_to_all(squares, 'seq', 0, 0, axis_index_groups=[[(i + blocks // 2...  11.1 us
    all_to_all x1, blocking collectives, on_device(): lax.all_to_all(parts, 'dp', 0, 0, axis_index_groups=[list(reversed(range(...  9.54 us
    pallas_call x2, Pallas kernels, attend(): call(attend_kernel, [shape(channels, wide), shape(2 * count, channels, wi...  9.36 us
    all_to_all x1, starting transfers between devices, on_device(): steps = lax.all_to_all(steps, 'dp', 0, 0)[:, 0, 0]  5.95 us
    ppermute x10, waiting for transfers between devices, across(): lax.ppermute(value, axis, [(i, i ^ bits) for i in range(lax.axis_size(axi...  5.83 us
    all_to_all x1, starting transfers between devices, on_device(): pieces = lax.all_to_all(pieces, 'seq', 0, 0, axis_index_groups=along)  5.32 us
    all_to_all x1, starting transfers between devices, on_device(): sums = lax.all_to_all(sums, 'dp', 0, 0)  5.14 us
  transfers between devices with their start and end apart: 15, of which 9 were waited for; matrix products, arithmetic and copies ran while one was open for 0% of the time, Pallas kernels for 8%

profile of v5, /device:TPU:1, one launch (start us, length us, event | category | flops | bytes accessed | tf_op | source)
XLA Modules:
  0.0 101.2 jit_solution(7036869449096188284)
XLA Ops:
  0.6 0.0 copy-start.4
  1.3 0.6 shard_map.113
  1.9 5.9 %all-to-all-start = ((s32[8,1,128]{2,1,0:T(1,128)}), s32[8,1,128]{2,1,0:T(1,128)S(1)}, u32[]{:S(2)}, u32[]{:S(2)}) async-start(s32[8,1,128]{2,1,0:T(1,128)} %shard_map.113), calls=%async_computation | async-start | bytes 8192 | tf_op jit(solution)/shard_map/all_to_all | solution.py:374
  7.8 0.0 copy-done.4
  7.8 0.0 copy-start.2
  7.9 1.0 copy-done.2
  8.8 0.0 copy-start.5
  8.8 0.7 copy-done.5
  9.6 0.0 copy-start.6
  9.6 0.7 copy-done.6
  10.3 0.0 copy-start.1
  10.3 0.0 copy-start.3
  10.3 0.8 shard_map.114
  11.1 5.6 %collective-permute-start = (bf16[64,128]{1,0:T(8,128)(2,1)S(1)}, bf16[64,128]{1,0:T(8,128)(2,1)S(1)}, u32[]{:S(2)}, u32[]{:S(2)}) collective-permute-start(bf16[64,128]{1,0:T(8,128)(2,1)S(1)} %get-tuple-element.25), channel_id=1, source_target_pairs={{0,14},{1,15},{2,12},{3,13},{4,10},{5,11},{6,8},{7,9},{8,6},{9,7},... | collective-permute-start | bytes 49160 | tf_op jit(solution)/shard_map/ppermute | solution.py:371
  16.8 0.0 copy-done.1
  16.8 0.0 copy-done.3
  16.8 0.8 shard_map.115.sums_ref
  17.6 0.0 all-to-all-done
  17.6 0.2 slice_reduce_fusion.steps_ref
  17.8 1.5 %shard_map.116 = bf16[8,400,128]{2,1,0:T(8,128)(2,1)} custom-call(s32[8]{0:T(128)S(1)} %slice_reduce_fusion.steps_ref, bf16[10,400,128]{2,1,0:T(8,128)(2,1)S(1)} %shard_map.115.sums_ref), custom_call_target="tpu_custom_call" | custom-call | tf_op jit(solution)/shard_map/pallas_call | solution.py:399
  19.3 5.1 %all-to-all-start.1 = ((bf16[8,400,128]{2,1,0:T(8,128)(2,1)}), bf16[8,400,128]{2,1,0:T(8,128)(2,1)S(1)}, u32[]{:S(2)}, u32[]{:S(2)}) async-start(bf16[8,400,128]{2,1,0:T(8,128)(2,1)} %shard_map.116), calls=%async_computation.1 | async-start | bytes 1638400 | tf_op jit(solution)/shard_map/all_to_all | solution.py:403
  24.5 0.0 collective-permute-done
  24.5 1.7 %collective-permute-start.1 = (bf16[2,64,128]{2,1,0:T(8,128)(2,1)S(1)}, bf16[2,64,128]{2,1,0:T(8,128)(2,1)S(1)}, u32[]{:S(2)}, u32[]{:S(2)}) collective-permute-start(bf16[2,64,128]{2,1,0:T(8,128)(2,1)S(1)} %pad_maximum_fusion), channel_id=1, source_target_pairs={{0,2},{1,3},{2,0},{3,1},{4,6},{5,7},{6,4},{7,5},{8,10},{9,11},{10,... | collective-permute-start | bytes 98312 | tf_op jit(solution)/shard_map/ppermute | solution.py:371
  26.2 0.5 collective-permute-start.2
  26.8 1.6 %collective-permute-start.3 = (bf16[2,64,128]{2,1,0:T(8,128)(2,1)S(1)}, bf16[2,64,128]{2,1,0:T(8,128)(2,1)S(1)}, u32[]{:S(2)}, u32[]{:S(2)}) collective-permute-start(bf16[2,64,128]{2,1,0:T(8,128)(2,1)S(1)} %pad_maximum_fusion), channel_id=1, source_target_pairs={{0,6},{1,7},{2,4},{3,5},{4,2},{5,3},{6,0},{7,1},{8,14},{9,15},{10,... | collective-permute-start | bytes 98312 | tf_op jit(solution)/shard_map/ppermute | solution.py:371
  28.4 0.0 collective-permute-done.1
  28.4 1.6 %collective-permute-done.2 = bf16[2,64,128]{2,1,0:T(8,128)(2,1)S(1)} collective-permute-done((bf16[2,64,128]{2,1,0:T(8,128)(2,1)S(1)}, bf16[2,64,128]{2,1,0:T(8,128)(2,1)S(1)}, u32[]{:S(2)}, u32[]{:S(2)}) %collective-permute-start.2) | collective-permute-done | bytes 32800 | tf_op jit(solution)/shard_map/ppermute | solution.py:371
  30.1 0.0 copy-start
  30.1 1.5 %collective-permute-done.3 = bf16[2,64,128]{2,1,0:T(8,128)(2,1)S(1)} collective-permute-done((bf16[2,64,128]{2,1,0:T(8,128)(2,1)S(1)}, bf16[2,64,128]{2,1,0:T(8,128)(2,1)S(1)}, u32[]{:S(2)}, u32[]{:S(2)}) %collective-permute-start.3) | collective-permute-done | bytes 32800 | tf_op jit(solution)/shard_map/ppermute | solution.py:371
  31.6 2.3 %all-to-all-done.1.sums_ref = bf16[8,400,128]{2,1,0:T(8,128)(2,1)S(1)} async-done(((bf16[8,400,128]{2,1,0:T(8,128)(2,1)}), bf16[8,400,128]{2,1,0:T(8,128)(2,1)S(1)}, u32[]{:S(2)}, u32[]{:S(2)}) %all-to-all-start.1) | async-done | bytes 819232 | tf_op jit(solution)/shard_map/all_to_all | solution.py:403
  33.9 0.0 copy-done
  34.0 0.9 shard_map.117
  34.8 1.7 %collective-permute-start.4 = (bf16[1,144,128]{2,1,0:T(8,128)(2,1)S(1)}, bf16[1,144,128]{2,1,0:T(8,128)(2,1)S(1)}, u32[]{:S(2)}, u32[]{:S(2)}) collective-permute-start(bf16[1,144,128]{2,1,0:T(8,128)(2,1)S(1)} %get-tuple-element.27), channel_id=1, source_target_pairs={{0,2},{1,3},{2,0},{3,1},{4,6},{5,7},{6,4},{7,5},{8,10},{9,11},{10,... | collective-permute-start | bytes 110600 | tf_op jit(solution)/shard_map/ppermute | solution.py:371
  36.5 0.6 collective-permute-start.5
  37.1 1.6 %collective-permute-start.6 = (bf16[1,144,128]{2,1,0:T(8,128)(2,1)S(1)}, bf16[1,144,128]{2,1,0:T(8,128)(2,1)S(1)}, u32[]{:S(2)}, u32[]{:S(2)}) collective-permute-start(bf16[1,144,128]{2,1,0:T(8,128)(2,1)S(1)} %get-tuple-element.27), channel_id=1, source_target_pairs={{0,6},{1,7},{2,4},{3,5},{4,2},{5,3},{6,0},{7,1},{8,14},{9,15},{10,... | collective-permute-start | bytes 110600 | tf_op jit(solution)/shard_map/ppermute | solution.py:371
  38.7 4.5 %collective-permute-start.8 = (bf16[8,64,128]{2,1,0:T(8,128)(2,1)S(1)}, bf16[8,64,128]{2,1,0:T(8,128)(2,1)S(1)}, u32[]{:S(2)}, u32[]{:S(2)}) collective-permute-start(bf16[8,64,128]{2,1,0:T(8,128)(2,1)S(1)} %constant_dynamic-update-slice_fusion.near_ref), channel_id=1, source_target_pairs={{0,1},{1,0},{2,3},{3,2},{4,5},{5,4},{6,7},{7,6},{8,9},{9,8},{10,11... | collective-permute-start | bytes 393224 | tf_op jit(solution)/shard_map/ppermute | solution.py:371
  43.2 0.0 collective-permute-done.4
  43.2 0.0 collective-permute-done.5
  43.2 0.0 collective-permute-done.6
  43.3 0.4 collective-permute-start.7
  43.7 0.5 collective-permute-done.8.far_ref
  44.2 0.2 shard_map.118
  44.4 4.7 %shard_map.119 = (f32[64,256]{1,0:T(8,128)S(1)}, bf16[8,64,256]{2,1,0:T(8,128)(2,1)S(1)}) custom-call(bf16[4,144,128]{2,1,0:T(8,128)(2,1)S(1)} %constant_dynamic-update-slice_fusion.5.pack_ref, bf16[2048,128]{1,0:T(8,128)(2,1)S(1)} %get-tuple-element.29.keys_ref, bf16[80,2048]{1,0:T(8,128)(2,1)S(1)} %get-tuple-element.30.values_ref, ...), custom_call_target="tpu_custom_call" | custom-call | flops 4000000000 | tf_op jit(solution)/shard_map/pallas_call | solution.py:425
  49.1 1.2 %collective-permute-done.7.pack_ref = bf16[4,144,128]{2,1,0:T(8,128)(2,1)S(1)} collective-permute-done((bf16[4,144,128]{2,1,0:T(8,128)(2,1)S(1)}, bf16[4,144,128]{2,1,0:T(8,128)(2,1)S(1)}, u32[]{:S(2)}, u32[]{:S(2)}) %collective-permute-start.7) | collective-permute-done | bytes 147488 | tf_op jit(solution)/shard_map/ppermute | solution.py:371
  50.3 4.7 %shard_map.120 = (f32[64,256]{1,0:T(8,128)S(1)}, bf16[8,64,256]{2,1,0:T(8,128)(2,1)S(1)}) custom-call(bf16[4,144,128]{2,1,0:T(8,128)(2,1)S(1)} %collective-permute-done.7.pack_ref, bf16[2048,128]{1,0:T(8,128)(2,1)S(1)} %get-tuple-element.29.keys_ref, bf16[80,2048]{1,0:T(8,128)(2,1)S(1)} %get-tuple-element.30.values_ref, ...), custom_call_target="tpu_custom_call" | custom-call | flops 4000000000 | tf_op jit(solution)/shard_map/pallas_call | solution.py:425
  55.0 5.1 %collective-permute-start.9 = (f32[64,384]{1,0:T(8,128)S(1)}, f32[64,384]{1,0:T(8,128)S(1)}, u32[]{:S(2)}, u32[]{:S(2)}) collective-permute-start(f32[64,384]{1,0:T(8,128)S(1)} %constant_dynamic-update-slice_fusion.9.mine_ref), channel_id=1, source_target_pairs={{0,1},{1,0},{2,3},{3,2},{4,5},{5,4},{6,7},{7,6},{8,9},{9,8},{10,11... | collective-permute-start | bytes 294920 | tf_op jit(solution)/shard_map/ppermute | solution.py:371
  60.1 0.9 collective-permute-done.9.other_ref
  61.1 1.0 shard_map.121
  62.1 5.3 %all-to-all-start.2 = ((bf16[8,80,128]{2,1,0:T(8,128)(2,1)}), bf16[8,80,128]{2,1,0:T(8,128)(2,1)S(1)}, u32[]{:S(2)}, u32[]{:S(2)}) async-start(bf16[8,80,128]{2,1,0:T(8,128)(2,1)} %get-tuple-element.38), calls=%async_computation.2 | async-start | bytes 327680 | tf_op jit(solution)/shard_map/all_to_all | solution.py:447
  68.7 3.9 %all-to-all-done.2.pieces_ref = bf16[8,80,128]{2,1,0:T(8,128)(2,1)S(1)} async-done(((bf16[8,80,128]{2,1,0:T(8,128)(2,1)}), bf16[8,80,128]{2,1,0:T(8,128)(2,1)S(1)}, u32[]{:S(2)}, u32[]{:S(2)}) %all-to-all-start.2) | async-done | bytes 163872 | tf_op jit(solution)/shard_map/all_to_all | solution.py:447
  72.6 0.2 shard_map.122
  72.8 9.5 %all_to_all.25.parts_ref = bf16[8,64,256]{2,1,0:T(8,128)(2,1)S(1)} all-to-all(bf16[8,64,256]{2,1,0:T(8,128)(2,1)S(1)} %shard_map.122), channel_id=1, replica_groups={{112,96,80,64,48,32,16,0},{113,97,81,65,49,33,17,1},{114,98,82,66,50,34..., dimensions={0} | all-to-all | bytes 524288 | tf_op jit(solution)/shard_map/all_to_all | solution.py:453
  82.3 0.7 shard_map.123
  83.0 11.1 %all-to-all-start.4 = ((f32[16,1,128]{2,1,0:T(1,128)}), f32[16,1,128]{2,1,0:T(1,128)S(1)}, u32[]{:S(2)}, u32[]{:S(2)}) async-start(f32[16,1,128]{2,1,0:T(1,128)} %get-tuple-element.42), calls=%async_computation.4 | async-start | bytes 16384 | tf_op jit(solution)/shard_map/all_to_all | solution.py:459
  94.1 2.0 %all-to-all-done.4.squares_ref = f32[16,1,128]{2,1,0:T(1,128)S(1)} async-done(((f32[16,1,128]{2,1,0:T(1,128)}), f32[16,1,128]{2,1,0:T(1,128)S(1)}, u32[]{:S(2)}, u32[]{:S(2)}) %all-to-all-start.4) | async-done | bytes 8224 | tf_op jit(solution)/shard_map/all_to_all | solution.py:459
  96.1 0.1 shard_map.124.mine_ref
  96.2 2.5 %collective-permute-start.10 = (bf16[64,256]{1,0:T(8,128)(2,1)S(1)}, bf16[64,256]{1,0:T(8,128)(2,1)S(1)}, u32[]{:S(2)}, u32[]{:S(2)}) collective-permute-start(bf16[64,256]{1,0:T(8,128)(2,1)S(1)} %shard_map.124.mine_ref), channel_id=1, source_target_pairs={{0,128},{128,0},{1,129},{129,1},{2,130},{130,2},{3,131},{131,3},{4... | collective-permute-start | bytes 98312 | tf_op jit(solution)/shard_map/ppermute | solution.py:466
  98.7 1.8 %collective-permute-done.10.other_ref = bf16[64,256]{1,0:T(8,128)(2,1)S(1)} collective-permute-done((bf16[64,256]{1,0:T(8,128)(2,1)S(1)}, bf16[64,256]{1,0:T(8,128)(2,1)S(1)}, u32[]{:S(2)}, u32[]{:S(2)}) %collective-permute-start.10) | collective-permute-done | bytes 32800 | tf_op jit(solution)/shard_map/ppermute | solution.py:466
  100.5 0.6 shard_map.125
  (13 shorter events, 0.1 us)
Async XLA Ops:
  0.6 7.2 %copy-start.4 = (bf16[1,1,128,64]{2,3,1,0:T(8,128)(2,1)S(1)}, bf16[1,1,128,64]{2,3,1,0:T(8,128)(2,1)}, u32[]{:S(2)}) copy-start(bf16[1,1,128,64]{2,3,1,0:T(8,128)(2,1)} %param.10) | copy-start | bytes 49156
  1.9 15.7 %all-to-all-start = ((s32[8,1,128]{2,1,0:T(1,128)}), s32[8,1,128]{2,1,0:T(1,128)S(1)}, u32[]{:S(2)}, u32[]{:S(2)}) async-start(s32[8,1,128]{2,1,0:T(1,128)} %shard_map.113), calls=%async_computation | async-start | bytes 8192 | tf_op jit(solution)/shard_map/all_to_all | solution.py:374
  7.8 1.0 copy-start.2
  8.8 0.7 copy-start.5
  9.6 0.7 copy-start.6
  10.3 6.5 %copy-start.1 = (bf16[1,3,384,256]{3,2,1,0:T(8,128)(2,1)S(1)}, bf16[1,3,384,256]{3,2,1,0:T(8,128)(2,1)}, u32[]{:S(2)}) copy-start(bf16[1,3,384,256]{3,2,1,0:T(8,128)(2,1)} %param.18) | copy-start | bytes 1769476
  10.3 6.5 %copy-start.3 = (f32[10,2,3072]{2,1,0:T(2,128)S(1)}, f32[10,2,3072]{2,1,0:T(2,128)}, u32[]{:S(2)}) copy-start(f32[10,2,3072]{2,1,0:T(2,128)} %modulation_ref.1) | copy-start | bytes 737284
  11.1 13.4 %collective-permute-start = (bf16[64,128]{1,0:T(8,128)(2,1)S(1)}, bf16[64,128]{1,0:T(8,128)(2,1)S(1)}, u32[]{:S(2)}, u32[]{:S(2)}) collective-permute-start(bf16[64,128]{1,0:T(8,128)(2,1)S(1)} %get-tuple-element.25), channel_id=1, source_target_pairs={{0,14},{1,15},{2,12},{3,13},{4,10},{5,11},{6,8},{7,9},{8,6},{9,7},... | collective-permute-start | bytes 49160 | tf_op jit(solution)/shard_map/ppermute | solution.py:371
  19.3 14.6 %all-to-all-start.1 = ((bf16[8,400,128]{2,1,0:T(8,128)(2,1)}), bf16[8,400,128]{2,1,0:T(8,128)(2,1)S(1)}, u32[]{:S(2)}, u32[]{:S(2)}) async-start(bf16[8,400,128]{2,1,0:T(8,128)(2,1)} %shard_map.116), calls=%async_computation.1 | async-start | bytes 1638400 | tf_op jit(solution)/shard_map/all_to_all | solution.py:403
  24.5 3.9 %collective-permute-start.1 = (bf16[2,64,128]{2,1,0:T(8,128)(2,1)S(1)}, bf16[2,64,128]{2,1,0:T(8,128)(2,1)S(1)}, u32[]{:S(2)}, u32[]{:S(2)}) collective-permute-start(bf16[2,64,128]{2,1,0:T(8,128)(2,1)S(1)} %pad_maximum_fusion), channel_id=1, source_target_pairs={{0,2},{1,3},{2,0},{3,1},{4,6},{5,7},{6,4},{7,5},{8,10},{9,11},{10,... | collective-permute-start | bytes 98312 | tf_op jit(solution)/shard_map/ppermute | solution.py:371
  26.2 3.8 %collective-permute-start.2 = (bf16[2,64,128]{2,1,0:T(8,128)(2,1)S(1)}, bf16[2,64,128]{2,1,0:T(8,128)(2,1)S(1)}, u32[]{:S(2)}, u32[]{:S(2)}) collective-permute-start(bf16[2,64,128]{2,1,0:T(8,128)(2,1)S(1)} %pad_maximum_fusion), channel_id=1, source_target_pairs={{0,4},{1,5},{2,6},{3,7},{4,0},{5,1},{6,2},{7,3},{8,12},{9,13},{10,... | collective-permute-start | bytes 98312 | tf_op jit(solution)/shard_map/ppermute | solution.py:371
  26.8 4.8 %collective-permute-start.3 = (bf16[2,64,128]{2,1,0:T(8,128)(2,1)S(1)}, bf16[2,64,128]{2,1,0:T(8,128)(2,1)S(1)}, u32[]{:S(2)}, u32[]{:S(2)}) collective-permute-start(bf16[2,64,128]{2,1,0:T(8,128)(2,1)S(1)} %pad_maximum_fusion), channel_id=1, source_target_pairs={{0,6},{1,7},{2,4},{3,5},{4,2},{5,3},{6,0},{7,1},{8,14},{9,15},{10,... | collective-permute-start | bytes 98312 | tf_op jit(solution)/shard_map/ppermute | solution.py:371
  30.1 3.9 %copy-start = (bf16[1,256,64]{1,2,0:T(8,128)(2,1)S(1)}, bf16[1,256,64]{1,2,0:T(8,128)(2,1)}, u32[]{:S(2)}) copy-start(bf16[1,256,64]{1,2,0:T(8,128)(2,1)} %param.19) | copy-start | bytes 98308
  34.8 8.4 %collective-permute-start.4 = (bf16[1,144,128]{2,1,0:T(8,128)(2,1)S(1)}, bf16[1,144,128]{2,1,0:T(8,128)(2,1)S(1)}, u32[]{:S(2)}, u32[]{:S(2)}) collective-permute-start(bf16[1,144,128]{2,1,0:T(8,128)(2,1)S(1)} %get-tuple-element.27), channel_id=1, source_target_pairs={{0,2},{1,3},{2,0},{3,1},{4,6},{5,7},{6,4},{7,5},{8,10},{9,11},{10,... | collective-permute-start | bytes 110600 | tf_op jit(solution)/shard_map/ppermute | solution.py:371
  36.5 6.7 %collective-permute-start.5 = (bf16[1,144,128]{2,1,0:T(8,128)(2,1)S(1)}, bf16[1,144,128]{2,1,0:T(8,128)(2,1)S(1)}, u32[]{:S(2)}, u32[]{:S(2)}) collective-permute-start(bf16[1,144,128]{2,1,0:T(8,128)(2,1)S(1)} %get-tuple-element.27), channel_id=1, source_target_pairs={{0,4},{1,5},{2,6},{3,7},{4,0},{5,1},{6,2},{7,3},{8,12},{9,13},{10,... | collective-permute-start | bytes 110600 | tf_op jit(solution)/shard_map/ppermute | solution.py:371
  37.1 6.2 %collective-permute-start.6 = (bf16[1,144,128]{2,1,0:T(8,128)(2,1)S(1)}, bf16[1,144,128]{2,1,0:T(8,128)(2,1)S(1)}, u32[]{:S(2)}, u32[]{:S(2)}) collective-permute-start(bf16[1,144,128]{2,1,0:T(8,128)(2,1)S(1)} %get-tuple-element.27), channel_id=1, source_target_pairs={{0,6},{1,7},{2,4},{3,5},{4,2},{5,3},{6,0},{7,1},{8,14},{9,15},{10,... | collective-permute-start | bytes 110600 | tf_op jit(solution)/shard_map/ppermute | solution.py:371
  38.7 5.5 %collective-permute-start.8 = (bf16[8,64,128]{2,1,0:T(8,128)(2,1)S(1)}, bf16[8,64,128]{2,1,0:T(8,128)(2,1)S(1)}, u32[]{:S(2)}, u32[]{:S(2)}) collective-permute-start(bf16[8,64,128]{2,1,0:T(8,128)(2,1)S(1)} %constant_dynamic-update-slice_fusion.near_ref), channel_id=1, source_target_pairs={{0,1},{1,0},{2,3},{3,2},{4,5},{5,4},{6,7},{7,6},{8,9},{9,8},{10,11... | collective-permute-start | bytes 393224 | tf_op jit(solution)/shard_map/ppermute | solution.py:371
  43.3 7.1 %collective-permute-start.7 = (bf16[4,144,128]{2,1,0:T(8,128)(2,1)S(1)}, bf16[4,144,128]{2,1,0:T(8,128)(2,1)S(1)}, u32[]{:S(2)}, u32[]{:S(2)}) collective-permute-start(bf16[4,144,128]{2,1,0:T(8,128)(2,1)S(1)} %constant_dynamic-update-slice_fusion.5.pack_ref), channel_id=1, source_target_pairs={{0,14},{1,15},{2,12},{3,13},{4,10},{5,11},{6,8},{7,9},{8,6},{9,7},... | collective-permute-start | bytes 442376 | tf_op jit(solution)/shard_map/ppermute | solution.py:371
  55.0 6.1 %collective-permute-start.9 = (f32[64,384]{1,0:T(8,128)S(1)}, f32[64,384]{1,0:T(8,128)S(1)}, u32[]{:S(2)}, u32[]{:S(2)}) collective-permute-start(f32[64,384]{1,0:T(8,128)S(1)} %constant_dynamic-update-slice_fusion.9.mine_ref), channel_id=1, source_target_pairs={{0,1},{1,0},{2,3},{3,2},{4,5},{5,4},{6,7},{7,6},{8,9},{9,8},{10,11... | collective-permute-start | bytes 294920 | tf_op jit(solution)/shard_map/ppermute | solution.py:371
  62.1 10.5 %all-to-all-start.2 = ((bf16[8,80,128]{2,1,0:T(8,128)(2,1)}), bf16[8,80,128]{2,1,0:T(8,128)(2,1)S(1)}, u32[]{:S(2)}, u32[]{:S(2)}) async-start(bf16[8,80,128]{2,1,0:T(8,128)(2,1)} %get-tuple-element.38), calls=%async_computation.2 | async-start | bytes 327680 | tf_op jit(solution)/shard_map/all_to_all | solution.py:447
  83.0 13.1 %all-to-all-start.4 = ((f32[16,1,128]{2,1,0:T(1,128)}), f32[16,1,128]{2,1,0:T(1,128)S(1)}, u32[]{:S(2)}, u32[]{:S(2)}) async-start(f32[16,1,128]{2,1,0:T(1,128)} %get-tuple-element.42), calls=%async_computation.4 | async-start | bytes 16384 | tf_op jit(solution)/shard_map/all_to_all | solution.py:459
  96.2 4.4 %collective-permute-start.10 = (bf16[64,256]{1,0:T(8,128)(2,1)S(1)}, bf16[64,256]{1,0:T(8,128)(2,1)S(1)}, u32[]{:S(2)}, u32[]{:S(2)}) collective-permute-start(bf16[64,256]{1,0:T(8,128)(2,1)S(1)} %shard_map.124.mine_ref), channel_id=1, source_target_pairs={{0,128},{128,0},{1,129},{129,1},{2,130},{130,2},{3,131},{131,3},{4... | collective-permute-start | bytes 98312 | tf_op jit(solution)/shard_map/ppermute | solution.py:466
